TPU v7x, 512 devices: a whole 4x8x8 slice. The times are simulated.
512 devices in a mesh: ctx: 8 (over x, core), hs: 64 (over z, y).
Axes of the slice: x: 4, y: 8, z: 8, core: 2. Of those that a mesh axis runs over, the one named last changes fastest.
Arguments:
- key_rows: bfloat16 [64, 4096, 512], P('hs', 'ctx'), may hold values from -6 to 6
- value_rows: bfloat16 [64, 4096, 512], P('hs', 'ctx'), may hold values from -6 to 6
- query_rows: bfloat16 [64, 4096, 512], P('hs', 'ctx'), may hold values from -6 to 6
- step_rates: float32 [64, 4096], P('hs', 'ctx'), may hold values from 0.0003 to 0.003
- fast_gate: bfloat16 [64, 512, 512], P('hs', 'ctx'), may hold values from -0.25 to 0.25
- fast_up: bfloat16 [64, 512, 512], P('hs', 'ctx'), may hold values from -0.25 to 0.25
- fast_down: bfloat16 [64, 512, 512], P('hs', 'ctx'), may hold values from -0.25 to 0.25
- out_gain: float32 [2048], replicated, may hold values from 0.1 to 1.9
- gate_input: bfloat16 [4096, 16, 2048], P(('ctx', 'hs')), may hold values from -6 to 6
- out_weight: bfloat16 [2048, 1024], P('hs'), may hold values from -0.125 to 0.125
Outputs:
- layer_out: bfloat16 [4096, 16, 1024], P(('ctx', 'hs'))
All inputs are finite; a program needn't handle non-finite values.
Results may differ from a plain program's by a relative error of at most 0.01.
Values may be sent and summed in bfloat16 or wider, within the bound.
No kernel may reach another device: no remote copies, remote signals or barrier semaphores. Data moves between devices by JAX's collectives and lax.ppermute only.
A program may use at most 64 MiB of HBM per device.

v0:
```python
import jax
import jax.numpy as jnp
from jax import lax
from jax.sharding import PartitionSpec as P

epsilon = 1e-06


def rescale_rows(weight, update):
    base = weight.astype(jnp.float32)
    moved = base + update
    factor = jnp.sqrt(jnp.mean(base * base, -1, keepdims=True) + epsilon) / jnp.sqrt(
        jnp.mean(moved * moved, -1, keepdims=True) + epsilon
    )
    return (moved * factor).astype(jnp.bfloat16)


def inner_rows(left, right):
    return lax.dot_general(
        left, right, (((0,), (0,)), ((), ())), preferred_element_type=jnp.float32
    )


def body(
    key_rows,
    value_rows,
    query_rows,
    step_rates,
    fast_gate,
    fast_up,
    fast_down,
    out_gain,
    gate_input,
    out_weight,
):
    key_row = key_rows[0]
    value_row = value_rows[0]
    query_row = query_rows[0]
    rate_row = step_rates[0]
    whole_gate, whole_up, whole_down = (
        lax.all_gather(fast_gate, "ctx", axis=1, tiled=True),
        lax.all_gather(fast_up, "ctx", axis=1, tiled=True),
        lax.all_gather(fast_down, "ctx", axis=1, tiled=True),
    )
    gate_fast = whole_gate[0]
    up_fast = whole_up[0]
    down_fast = whole_down[0]
    pre_gate = jnp.dot(key_row, gate_fast.T, preferred_element_type=jnp.float32)
    pre_up = jnp.dot(key_row, up_fast.T, preferred_element_type=jnp.float32)
    sig_gate = jax.nn.sigmoid(pre_gate)
    act_gate = pre_gate * sig_gate
    hidden = (act_gate * pre_up).astype(jnp.bfloat16)
    scaled = (rate_row[:, None] * value_row.astype(jnp.float32)).astype(jnp.bfloat16)
    grad_down = inner_rows(scaled, hidden)
    back_hidden = jnp.dot(scaled, down_fast, preferred_element_type=jnp.float32)
    back_gate = (back_hidden * pre_up * sig_gate * (1.0 + pre_gate * (1.0 - sig_gate))).astype(
        jnp.bfloat16
    )
    back_up = (back_hidden * act_gate).astype(jnp.bfloat16)
    grad_gate = inner_rows(back_gate, key_row)
    grad_up = inner_rows(back_up, key_row)
    grad_gate, grad_up, grad_down = lax.psum((grad_gate, grad_up, grad_down), "ctx")
    new_gate = rescale_rows(gate_fast, grad_gate)
    new_up = rescale_rows(up_fast, grad_up)
    new_down = rescale_rows(down_fast, grad_down)
    query_gate = jnp.dot(query_row, new_gate.T, preferred_element_type=jnp.float32)
    query_up = jnp.dot(query_row, new_up.T, preferred_element_type=jnp.float32)
    query_hidden = (jax.nn.silu(query_gate) * query_up).astype(jnp.bfloat16)
    head_out = jnp.dot(query_hidden, new_down.T, preferred_element_type=jnp.float32).astype(
        jnp.bfloat16
    )
    width_hs = lax.axis_size("hs")
    head_size = head_out.shape[1]
    token_count = head_out.shape[0] // width_hs
    blocks = head_out.reshape(width_hs, token_count, head_size)
    moved = lax.all_to_all(blocks, "hs", split_axis=0, concat_axis=2, tiled=True)
    seq_count = gate_input.shape[1]
    model_width = gate_input.shape[2]
    head_count = model_width // head_size
    mixed = moved.reshape(token_count, seq_count, head_count, head_size).astype(jnp.float32)
    square = jnp.mean(mixed * mixed, -1, keepdims=True)
    scaled_heads = mixed * lax.rsqrt(square + epsilon) * out_gain.reshape(head_count, head_size)
    normed = (
        scaled_heads.reshape(token_count, seq_count, model_width)
        * jax.nn.silu(gate_input.astype(jnp.float32))
    ).astype(jnp.bfloat16)
    flat_rows = normed.reshape(token_count * seq_count, model_width)
    out_cols = out_weight.shape[1]
    full_weight = lax.all_gather(out_weight, "hs", axis=0, tiled=True)
    result = jnp.dot(flat_rows, full_weight, preferred_element_type=jnp.float32)
    return result.astype(jnp.bfloat16).reshape(token_count, seq_count, out_cols)


def solution(mesh):
    return jax.shard_map(
        body,
        mesh=mesh,
        in_specs=(
            P("hs", "ctx", None),
            P("hs", "ctx", None),
            P("hs", "ctx", None),
            P("hs", "ctx"),
            P("hs", "ctx", None),
            P("hs", "ctx", None),
            P("hs", "ctx", None),
            P(),
            P(("ctx", "hs"), None, None),
            P("hs", None),
        ),
        out_specs=P(("ctx", "hs"), None, None),
        check_vma=False,
    )
```

profile of v0, /device:TPU:15, one launch (start us, length us, event | category | flops | bytes accessed | tf_op | source)
XLA Modules:
  0.0 197.6 jit_solution(18019016704699141221)
XLA Ops:
  7.4 0.0 all-reduce.3.cloned.1.call-start
  7.4 14.0 %all_gather.13 = bf16[1,512,512]{2,1,0:T(8,128)(2,1)S(1)} all-gather(bf16[1,64,512]{2,1,0:T(8,128)(2,1)} %param.16), channel_id=1, replica_groups=mesh['ctx'=8,'hs'=64] {'ctx'}, dimensions={1}, use_global_device_ids=true | all-gather | bytes 589824 | tf_op jit(solution)/shard_map/all_gather | solution.py:43
  21.3 13.3 %all_gather.12 = bf16[1,512,512]{2,1,0:T(8,128)(2,1)S(1)} all-gather(bf16[1,64,512]{2,1,0:T(8,128)(2,1)} %param.14), channel_id=1, replica_groups=mesh['ctx'=8,'hs'=64] {'ctx'}, dimensions={1}, use_global_device_ids=true | all-gather | bytes 589824 | tf_op jit(solution)/shard_map/all_gather | solution.py:41
  34.7 13.3 %all_gather.14 = bf16[1,512,512]{2,1,0:T(8,128)(2,1)S(1)} all-gather(bf16[1,64,512]{2,1,0:T(8,128)(2,1)} %param.15), channel_id=1, replica_groups=mesh['ctx'=8,'hs'=64] {'ctx'}, dimensions={1}, use_global_device_ids=true | all-gather | bytes 589824 | tf_op jit(solution)/shard_map/all_gather | solution.py:42
  48.0 0.5 fusion.37
  48.4 0.5 fusion.32
  48.9 0.5 fusion.25
  49.4 1.6 fusion.21
  51.0 1.7 fusion.35
  52.7 1.7 fusion.22
  54.4 0.0 all-reduce.3.cloned.1.call-update
  54.4 0.0 all-gather.2.cloned.1.call-start
  54.5 0.5 all-gather.2.cloned.1.call-update
  55.0 84.7 %all-reduce.3.cloned.1.call-done = (f32[512,512]{1,0:T(8,128)}, f32[512,512]{1,0:T(8,128)}, f32[512,512]{1,0:T(8,128)}) async-done(((f32[512,512]{1,0:T(8,128)}, f32[512,512]{1,0:T(8,128)}, f32[512,512]{1,0:T(8,128)}), (f32[512,512]{1,0:T(8,128)}, f32[512,512]{1,0:T(8,128)}, f32[512,512]{1,0:T(8,128)})) %all-reduce.3.cloned.1.call-update) | async-done | bytes 3145744 | tf_op jit(solution)/shard_map/psum | solution.py:62
  139.7 1.7 fusion.8
  141.4 2.0 %fusion.3 = (f32[512]{0:T(512)S(1)}, f32[512]{0:T(512)S(1)}, f32[512]{0:T(512)S(1)}, f32[512]{0:T(512)S(1)}) fusion(bf16[1,512,512]{2,1,0:T(8,128)(2,1)S(1)} %all_gather.12, f32[512,512]{1,0:T(8,128)} %get-tuple-element.11, f32[512,512]{1,0:T(8,128)} %get-tuple-element.12, bf16[1,512,512]{2,1,0:T(8,128)(2,1)S(1)} %all_gather.14), kind=kLoop, calls=%fused_computation.19 | loop fusion | flops 3143680 | bytes 3153920 | tf_op jit(solution)/shard_map/reduce_sum | solution.py:12
  143.5 2.6 %convolution_bitcast_fusion.1 = f32[512,512]{1,0:T(8,128)} fusion(f32[512,512]{1,0:T(8,128)S(1)} %copy-done.1, bf16[1,512,512]{2,1,0:T(8,128)(2,1)} %param.12, bf16[1,512,512]{2,1,0:T(8,128)(2,1)S(1)} %all_gather.12, f32[512]{0:T(512)S(1)} %rsqrt_multiply_fusion.2), kind=kOutput, calls=%fused_computation.2 | convolution fusion | flops 269484032 | bytes 3147776 | tf_op jit(solution)/shard_map/dot_general | solution.py:66
  146.1 2.6 %fusion.2 = bf16[64,8,512]{2,1,0:T(8,128)(2,1)S(1)} fusion(f32[512,512]{1,0:T(8,128)} %convolution_bitcast_fusion.1, f32[512,512]{1,0:T(8,128)S(1)} %copy-done.2, f32[512,512]{1,0:T(8,128)} %get-tuple-element.13, bf16[1,512,512]{2,1,0:T(8,128)(2,1)} %param.12, bf16[1,512,512]{2,1,0:T(8,128)(2,1)S(1)} %all_gather.14, ...), kind=kOutput, calls=%fused_computation.17 | convolution fusion | flops 540803072 | bytes 5246976 | tf_op jit(solution)/shard_map/dot_general | solution.py:69
  148.7 31.5 %all_to_all.4 = bf16[64,8,512]{2,1,0:T(8,128)(2,1)S(1)} all-to-all(bf16[64,8,512]{2,1,0:T(8,128)(2,1)S(1)} %fusion.2), channel_id=1, replica_groups=mesh['ctx'=8,'hs'=64] {'hs'}, dimensions={0} | all-to-all | bytes 1048576 | tf_op jit(solution)/shard_map/all_to_all | solution.py:76
  180.2 0.1 convert_bitcast_fusion
  180.3 0.0 copy-start.4
  180.4 0.6 copy.23
  181.0 0.5 reshape.108
  181.5 0.2 fusion.13
  181.6 0.1 copy.24
  181.7 0.1 copy.25
  181.8 0.2 copy.26
  182.0 1.2 mul.142
  183.2 1.9 mul.143
  185.1 1.4 fusion.20
  186.5 0.0 all-gather.2.cloned.1.call-done
  186.5 3.6 %convolution_convert_fusion.1 = bf16[128,1024]{1,0:T(8,128)(2,1)} fusion(bf16[128,2048]{1,0:T(8,128)(2,1)S(1)} %bitcast.81, bf16[2048,1024]{1,0:T(8,128)(2,1)} %all-gather.2.cloned.1.call-done), kind=kOutput, calls=%fused_computation.18 | convolution fusion | flops 537001984 | bytes 4980736 | tf_op jit(solution)/shard_map/dot_general | solution.py:90
  (15 shorter events, 0.1 us)
Async XLA Ops:
  7.4 40.6 %copy-start = (bf16[1,512,512]{2,1,0:T(8,128)(2,1)S(1)}, bf16[1,512,512]{2,1,0:T(8,128)(2,1)}, u32[]{:S(2)}) copy-start(bf16[1,512,512]{2,1,0:T(8,128)(2,1)} %param.10) | copy-start | bytes 1572868
  7.4 41.5 %copy-start.5 = (f32[1,512]{1,0:T(1,128)S(1)}, f32[1,512]{1,0:T(1,128)}, u32[]{:S(2)}) copy-start(f32[1,512]{1,0:T(1,128)} %param.13) | copy-start | bytes 6148
  7.4 41.5 %copy-start.3 = (bf16[1,512,512]{2,1,0:T(8,128)(2,1)S(1)}, bf16[1,512,512]{2,1,0:T(8,128)(2,1)}, u32[]{:S(2)}) copy-start(bf16[1,512,512]{2,1,0:T(8,128)(2,1)} %param.11) | copy-start | bytes 1572868
  7.4 132.3 %all-reduce.3.cloned.1.call-start = ((), (), s32[]{:S(2)}) async-start(), calls=%async_computation.2 | async-start | bytes 6291456 | tf_op jit(solution)/shard_map/psum | solution.py:62
  54.4 132.1 %all-gather.2.cloned.1.call-start = ((), (), s32[]{:S(2)}) async-start(), calls=%async_computation.1 | async-start | bytes 4259840 | tf_op jit(solution)/shard_map/all_gather | solution.py:89
  139.7 3.8 %copy-start.1 = (f32[512,512]{1,0:T(8,128)S(1)}, f32[512,512]{1,0:T(8,128)}, u32[]{:S(2)}) copy-start(f32[512,512]{1,0:T(8,128)} %get-tuple-element.11) | copy-start | bytes 3145732
  139.7 6.4 %copy-start.2 = (f32[512,512]{1,0:T(8,128)S(1)}, f32[512,512]{1,0:T(8,128)}, u32[]{:S(2)}) copy-start(f32[512,512]{1,0:T(8,128)} %get-tuple-element.12) | copy-start | bytes 3145732
  180.3 4.8 %copy-start.4 = (f32[2048]{0:T(1024)S(1)}, f32[2048]{0:T(1024)}, u32[]{:S(2)}) copy-start(f32[2048]{0:T(1024)} %param.17) | copy-start | bytes 24580
Sparse Core Ops, SparseCore 0:
  54.5 85.0 all-reduce.2
Sparse Core Ops, SparseCore 1:
  58.0 86.7 all-gather.1
where the time goes:
time: 198 us
  waiting for transfers between devices  85.2 us (43%)
  blocking collectives  72.1 us (36%)
  matrix products  15.2 us (8%)
  between operations  15 us (8%)
  other arithmetic  5.47 us (3%)
  local copies, waits for them, and re-layouts  4.57 us (2%)
    psum x1, waiting for transfers between devices, body(): lax.psum((grad_gate, grad_up, grad_down), 'ctx')  84.7 us
    all_to_all x1, blocking collectives, body(): lax.all_to_all(blocks, 'hs', split_axis=0, concat_axis=2, tiled=True)  31.5 us
    all_gather x1, blocking collectives, body(): lax.all_gather(fast_down, 'ctx', axis=1, tiled=True)  14 us
    all_gather x1, blocking collectives, body(): lax.all_gather(fast_up, 'ctx', axis=1, tiled=True)  13.3 us
    all_gather x1, blocking collectives, body(): lax.all_gather(fast_gate, 'ctx', axis=1, tiled=True)  13.3 us
    dot_general x3, matrix products, inner_rows(): lax.dot_general(left, right, (((0,), (0,)), ((), ())), preferred_element_...  4.99 us
  transfers between devices with their start and end apart: 2, of which 1 were waited for; matrix products, arithmetic and copies ran while one was open for 8% of the time, Pallas kernels for 0%

commit v1 on v0

v1 whole, which is shorter than its diff:
```python
import functools

import jax
import jax.numpy as jnp
from jax import lax
from jax.experimental import pallas as pl
from jax.experimental.pallas import tpu as pltpu
from jax.sharding import Mesh
from jax.sharding import PartitionSpec as P

epsilon = 1e-06
BF = jnp.bfloat16
F32 = jnp.float32
VMEM = pl.BlockSpec(memory_space=pltpu.VMEM)
SMEM = pl.BlockSpec(memory_space=pltpu.SMEM)
PARAMS = pltpu.CompilerParams(vmem_limit_bytes=40 * 1024 * 1024)


def dot(left, right, a, b):
    return lax.dot_general(left, right, (((a,), (b,)), ((), ())), preferred_element_type=F32)


def assemble(core, own, other, fulls):
    chips, rows, _ = own.shape
    part = rows // 3
    for i, full in enumerate(fulls):
        for x in range(chips):
            mine = pl.multiple_of(x * 2 * part + core * part, part)
            theirs = pl.multiple_of(x * 2 * part + (1 - core) * part, part)
            full[pl.ds(mine, part), :] = own[x, i * part : (i + 1) * part, :]
            full[pl.ds(theirs, part), :] = other[x, i * part : (i + 1) * part, :]


def grad_kernel(core_ref, key, value, rate, own, other, keep, send, gate, up, down, g0, g1, g2):
    core = core_ref[0]
    assemble(core, own, other, (gate, up, down))
    tokens, width = key.shape
    column = jnp.transpose(jnp.broadcast_to(rate[...], (128, tokens)))
    scaled = (jnp.concatenate([column] * (width // 128), axis=1) * value[...].astype(F32)).astype(BF)
    k = key[...]
    units = gate.shape[0]
    step = 256
    for n in range(0, units, step):
        pre_gate = dot(k, gate[n : n + step, :], 1, 1)
        pre_up = dot(k, up[n : n + step, :], 1, 1)
        back = dot(scaled, down[:, n : n + step], 1, 0)
        sig = jax.nn.sigmoid(pre_gate)
        act = pre_gate * sig
        hidden = (act * pre_up).astype(BF)
        back_gate = (back * pre_up * sig * (1.0 + pre_gate * (1.0 - sig))).astype(BF)
        back_up = (back * act).astype(BF)
        g0[n : n + step, :] = dot(back_gate, k, 0, 0).astype(BF)
        g1[n : n + step, :] = dot(back_up, k, 0, 0).astype(BF)
        g2[:, n : n + step] = dot(scaled, hidden, 0, 0).astype(BF)
    chips, rows, _ = keep.shape
    part = rows // 3
    for i, grad in enumerate((g0, g1, g2)):
        for x in range(chips):
            mine = pl.multiple_of(x * 2 * part + core * part, part)
            theirs = pl.multiple_of(x * 2 * part + (1 - core) * part, part)
            keep[x, i * part : (i + 1) * part, :] = grad[pl.ds(mine, part), :]
            send[x, i * part : (i + 1) * part, :] = grad[pl.ds(theirs, part), :]


def rescale_kernel(parts, weight, new):
    base = weight[...].astype(F32)
    moved = base
    total = parts[0].astype(F32)
    for x in range(1, parts.shape[0]):
        total = total + parts[x].astype(F32)
    moved = base + total
    factor = jnp.sqrt(jnp.mean(base * base, -1, keepdims=True) + epsilon) / jnp.sqrt(
        jnp.mean(moved * moved, -1, keepdims=True) + epsilon
    )
    new[...] = (moved * factor).astype(BF)


def query_kernel(core_ref, query, own, other, out, gate, up, down):
    assemble(core_ref[0], own, other, (gate, up, down))
    q = query[...]
    units = gate.shape[0]
    step = 256
    pieces = []
    for n in range(0, units, step):
        pre_gate = dot(q, gate[n : n + step, :], 1, 1)
        pre_up = dot(q, up[n : n + step, :], 1, 1)
        pieces.append((pre_gate * jax.nn.sigmoid(pre_gate) * pre_up).astype(BF))
    hidden = jnp.concatenate(pieces, axis=1)
    out[...] = dot(hidden, down[...], 1, 1).astype(BF)


def output_kernel(moved, gain, gate, weight, out, *, seqs, heads):
    total, size = moved.shape
    rows = total // heads
    tokens = rows // seqs
    everything = moved[...]
    row = lax.broadcasted_iota(jnp.int32, (rows, total), 0)
    column = lax.broadcasted_iota(jnp.int32, (rows, total), 1)
    acc = None
    for h in range(heads):
        source = (row % seqs * heads + h) * tokens + row // seqs
        pick = jnp.where(column == source, 1.0, 0.0).astype(BF)
        mixed = dot(pick, everything, 1, 0)
        square = jnp.mean(mixed * mixed, -1, keepdims=True)
        g = gate[:, h * size : (h + 1) * size].astype(F32)
        normed = mixed * lax.rsqrt(square + epsilon) * gain[:, h * size : (h + 1) * size] * (
            g * jax.nn.sigmoid(g)
        )
        part = dot(normed.astype(BF), weight[h * size : (h + 1) * size, :], 1, 0)
        acc = part if acc is None else acc + part
    out[...] = acc.astype(BF)


def swap(a):
    return lax.ppermute(a, "core", [(0, 1), (1, 0)])


def body(
    key_rows,
    value_rows,
    query_rows,
    step_rates,
    fast_gate,
    fast_up,
    fast_down,
    out_gain,
    gate_input,
    out_weight,
):
    chips = lax.axis_size("x")
    core = lax.axis_index("core").astype(jnp.int32).reshape(1)
    tokens, width = key_rows.shape[1:]
    part = fast_gate.shape[1]
    units = part * chips * 2
    full_weight = lax.all_gather(out_weight, "hs", axis=0, tiled=True)
    weights = jnp.concatenate([fast_gate[0], fast_up[0], fast_down[0]], axis=0)
    rows = weights.shape[0]
    own = lax.all_gather(weights, "x", axis=0, tiled=False)
    other = swap(own)
    piece = jax.ShapeDtypeStruct((chips, rows, width), BF)
    square = pltpu.VMEM((units, width), BF)
    keep, send = pl.pallas_call(
        grad_kernel,
        out_shape=(piece, piece),
        in_specs=[SMEM] + [VMEM] * 5,
        out_specs=(VMEM, VMEM),
        scratch_shapes=[square] * 6,
        compiler_params=PARAMS,
        name="grads",
    )(core, key_rows[0], value_rows[0], step_rates, own, other)
    summed = (keep.astype(F32) + swap(send).astype(F32)).astype(BF)
    parts = lax.all_to_all(summed, "x", split_axis=0, concat_axis=0, tiled=True)
    new = pl.pallas_call(
        rescale_kernel,
        out_shape=jax.ShapeDtypeStruct((rows, width), BF),
        in_specs=[VMEM] * 2,
        out_specs=VMEM,
        compiler_params=PARAMS,
        name="rescale",
    )(parts, weights)
    own = lax.all_gather(new, "x", axis=0, tiled=False)
    other = swap(own)
    head_out = pl.pallas_call(
        query_kernel,
        out_shape=jax.ShapeDtypeStruct((tokens, width), BF),
        in_specs=[SMEM] + [VMEM] * 3,
        out_specs=VMEM,
        scratch_shapes=[square] * 3,
        compiler_params=PARAMS,
        name="query",
    )(core, query_rows[0], own, other)
    pairs = lax.axis_size("hs")
    blocks = head_out.reshape(pairs, tokens // pairs, width)
    moved = lax.all_to_all(blocks, "hs", split_axis=0, concat_axis=0, tiled=True)
    few, seqs, model = gate_input.shape
    heads = model // width
    columns = out_weight.shape[1]
    result = pl.pallas_call(
        functools.partial(output_kernel, seqs=seqs, heads=heads),
        out_shape=jax.ShapeDtypeStruct((few * seqs, columns), BF),
        in_specs=[VMEM] * 4,
        out_specs=VMEM,
        compiler_params=PARAMS,
        name="project",
    )(
        moved.reshape(tokens, width),
        out_gain.reshape(1, model),
        gate_input.reshape(few * seqs, model),
        full_weight,
    )
    return result.reshape(few, seqs, columns)


def solution(mesh):
    ctx, pairs = mesh.devices.shape
    split = Mesh(mesh.devices.reshape(ctx // 2, 2, pairs), ("x", "core", "hs"))
    c = ("x", "core")
    return jax.shard_map(
        body,
        mesh=split,
        in_specs=(
            P("hs", c, None),
            P("hs", c, None),
            P("hs", c, None),
            P("hs", c),
            P("hs", c, None),
            P("hs", c, None),
            P("hs", c, None),
            P(),
            P(c + ("hs",), None, None),
            P("hs", None),
        ),
        out_specs=P(c + ("hs",), None, None),
        check_vma=False,
    )
```

time: 198 us -> 123 us (0.62)
  the two profiles are of different devices: /device:TPU:15 before, /device:TPU:4 now
where the time goes in v1:
time: 123 us; the launch traced here: 122 us
  blocking collectives  83.8 us (68%)
  between operations  13.5 us (11%)
  waiting for transfers between devices  9.14 us (7%)
  Pallas kernels  6.26 us (5%)
  starting transfers between devices  5.85 us (5%)
  local copies, waits for them, and re-layouts  2.89 us (2%)
    all_to_all x1, blocking collectives, body(): lax.all_to_all(blocks, 'hs', split_axis=0, concat_axis=0, tiled=True)  36.9 us
    all_gather x1, blocking collectives, body(): own = lax.all_gather(weights, 'x', axis=0, tiled=False)  17.1 us
    all_gather x1, blocking collectives, body(): own = lax.all_gather(new, 'x', axis=0, tiled=False)  15 us
    all_to_all x1, blocking collectives, body(): parts = lax.all_to_all(summed, 'x', split_axis=0, concat_axis=0, tiled=True)  14.8 us
    ppermute x3, waiting for transfers between devices, swap(): return lax.ppermute(a, 'core', [(0, 1), (1, 0)])  6.63 us
    ppermute x3, starting transfers between devices, swap(): return lax.ppermute(a, 'core', [(0, 1), (1, 0)])  5.85 us
    unnamed x14, local copies, waits for them, and re-layouts  2.89 us
    pallas_call x1, Pallas kernels, body(): pl.pallas_call(grad_kernel, out_shape=(piece, piece), in_specs=[SMEM] + [...  2.53 us
  transfers between devices with their start and end apart: 4, of which 4 were waited for; matrix products, arithmetic and copies ran while one was open for 1% of the time, Pallas kernels for 3%

profile of v1, /device:TPU:4, one launch (start us, length us, event | category | flops | bytes accessed | tf_op | source)
XLA Modules:
  0.0 122.5 jit_solution(17682101196086399102)
XLA Ops:
  6.5 0.0 copy-start.1
  6.5 0.0 copy-start.2
  6.5 0.0 all-gather.4.cloned.1.call-start
  6.5 0.7 all-gather.4.cloned.1.call-update
  7.3 0.9 pad_maximum_fusion.weight
  8.2 17.1 %all-gather = bf16[768,512]{1,0:T(8,128)(2,1)S(1)} all-gather(bf16[192,512]{1,0:T(8,128)(2,1)S(1)} %pad_maximum_fusion.weight), channel_id=2, replica_groups=mesh['x'=4,'core'=2,'hs'=64] {'x'}, dimensions={0}, use_global_device_ids=true | all-gather | bytes 983040 | tf_op jit(solution)/shard_map/all_gather | solution.py:138
  25.3 1.9 %collective-permute-start = (bf16[4,192,512]{2,1,0:T(8,128)(2,1)S(1)}, bf16[4,192,512]{2,1,0:T(8,128)(2,1)S(1)}, u32[]{:S(2)}, u32[]{:S(2)}) collective-permute-start(bf16[4,192,512]{2,1,0:T(8,128)(2,1)S(1)} %bitcast.14), channel_id=1, source_target_pairs={{0,64},{64,0},{1,65},{65,1},{2,66},{66,2},{3,67},{67,3},{4,68},{68... | collective-permute-start | bytes 2359304 | tf_op jit(solution)/shard_map/ppermute | solution.py:115
  27.2 2.2 %collective-permute-done.other = bf16[4,192,512]{2,1,0:T(8,128)(2,1)S(1)} collective-permute-done((bf16[4,192,512]{2,1,0:T(8,128)(2,1)S(1)}, bf16[4,192,512]{2,1,0:T(8,128)(2,1)S(1)}, u32[]{:S(2)}, u32[]{:S(2)}) %collective-permute-start) | collective-permute-done | bytes 786464 | tf_op jit(solution)/shard_map/ppermute | solution.py:115
  29.5 0.0 copy-done.1
  29.5 0.0 copy-done.2
  29.5 0.0 copy-start.6
  29.5 0.7 copy-done.6
  30.2 2.5 %grads.1 = (bf16[4,192,512]{2,1,0:T(8,128)(2,1)S(1)}, bf16[4,192,512]{2,1,0:T(8,128)(2,1)S(1)}) custom-call(s32[1]{0:T(128)} %bitcast.core_ref, bf16[512,512]{1,0:T(8,128)(2,1)S(1)} %bitcast.20, bf16[512,512]{1,0:T(8,128)(2,1)S(1)} %bitcast.21, f32[1,512]{1,0:T(1,128)S(1)} %copy-done.6, bf16[4,192,512]{2,1,0:T(8,128)(2,1)S(1)} %bitcast.15, ...), custom_call_target="tpu_custom_call" | custom-call | tf_op jit(solution)/shard_map/grads/pallas_call | solution.py:142
  32.7 2.0 %collective-permute-start.1 = (bf16[4,192,512]{2,1,0:T(8,128)(2,1)S(1)}, bf16[4,192,512]{2,1,0:T(8,128)(2,1)S(1)}, u32[]{:S(2)}, u32[]{:S(2)}) collective-permute-start(bf16[4,192,512]{2,1,0:T(8,128)(2,1)S(1)} %get-tuple-element.8), channel_id=1, source_target_pairs={{0,64},{64,0},{1,65},{65,1},{2,66},{66,2},{3,67},{67,3},{4,68},{68... | collective-permute-start | bytes 2359304 | tf_op jit(solution)/shard_map/ppermute | solution.py:115
  34.7 2.1 %collective-permute-done.1 = bf16[4,192,512]{2,1,0:T(8,128)(2,1)S(1)} collective-permute-done((bf16[4,192,512]{2,1,0:T(8,128)(2,1)S(1)}, bf16[4,192,512]{2,1,0:T(8,128)(2,1)S(1)}, u32[]{:S(2)}, u32[]{:S(2)}) %collective-permute-start.1) | collective-permute-done | bytes 786464 | tf_op jit(solution)/shard_map/ppermute | solution.py:115
  36.9 0.2 add_convert_fusion
  37.1 0.0 copy-start.3
  37.1 14.8 %all_to_all.10.parts = bf16[4,192,512]{2,1,0:T(8,128)(2,1)S(1)} all-to-all(bf16[4,192,512]{2,1,0:T(8,128)(2,1)S(1)} %add_convert_fusion), channel_id=1, replica_groups=mesh['x'=4,'core'=2,'hs'=64] {'x'}, dimensions={0} | all-to-all | bytes 1572864 | tf_op jit(solution)/shard_map/all_to_all | solution.py:152
  51.9 0.3 rescale.1
  52.2 15.0 %all-gather.1 = bf16[768,512]{1,0:T(8,128)(2,1)S(1)} all-gather(bf16[192,512]{1,0:T(8,128)(2,1)S(1)} %rescale.1), channel_id=3, replica_groups=mesh['x'=4,'core'=2,'hs'=64] {'x'}, dimensions={0}, use_global_device_ids=true | all-gather | bytes 983040 | tf_op jit(solution)/shard_map/all_gather | solution.py:161
  67.1 1.9 %collective-permute-start.2 = (bf16[4,192,512]{2,1,0:T(8,128)(2,1)S(1)}, bf16[4,192,512]{2,1,0:T(8,128)(2,1)S(1)}, u32[]{:S(2)}, u32[]{:S(2)}) collective-permute-start(bf16[4,192,512]{2,1,0:T(8,128)(2,1)S(1)} %bitcast.16), channel_id=1, source_target_pairs={{0,64},{64,0},{1,65},{65,1},{2,66},{66,2},{3,67},{67,3},{4,68},{68... | collective-permute-start | bytes 2359304 | tf_op jit(solution)/shard_map/ppermute | solution.py:115
  69.1 2.3 %collective-permute-done.2.other = bf16[4,192,512]{2,1,0:T(8,128)(2,1)S(1)} collective-permute-done((bf16[4,192,512]{2,1,0:T(8,128)(2,1)S(1)}, bf16[4,192,512]{2,1,0:T(8,128)(2,1)S(1)}, u32[]{:S(2)}, u32[]{:S(2)}) %collective-permute-start.2) | collective-permute-done | bytes 786464 | tf_op jit(solution)/shard_map/ppermute | solution.py:115
  71.3 0.0 copy-done.3
  71.3 0.0 copy-start.4
  71.3 0.0 copy-start.5
  71.3 1.1 query.1
  72.4 36.9 %all_to_all.11 = bf16[64,8,512]{2,1,0:T(8,128)(2,1)S(1)} all-to-all(bf16[64,8,512]{2,1,0:T(8,128)(2,1)S(1)} %bitcast.18), channel_id=1, replica_groups=mesh['x'=4,'core'=2,'hs'=64] {'hs'}, dimensions={0} | all-to-all | bytes 1048576 | tf_op jit(solution)/shard_map/all_to_all | solution.py:174
  109.3 1.8 %all-gather.4.cloned.1.call-done.weight = bf16[2048,1024]{1,0:T(8,128)(2,1)} async-done(((bf16[32,1024]{1,0:T(8,128)(2,1)}), bf16[2048,1024]{1,0:T(8,128)(2,1)}) %all-gather.4.cloned.1.call-update) | async-done | bytes 4194320 | tf_op jit(solution)/shard_map/all_gather | solution.py:135
  111.1 0.0 copy-done.4
  111.1 0.0 copy-done.5
  111.1 2.2 %copy-done = bf16[2048,1024]{1,0:T(8,128)(2,1)S(1)} copy-done((bf16[2048,1024]{1,0:T(8,128)(2,1)S(1)}, bf16[2048,1024]{1,0:T(8,128)(2,1)}, u32[]{:S(2)}) %copy-start) | copy-done | bytes 4194328
  113.3 2.4 %project.1 = bf16[128,1024]{1,0:T(8,128)(2,1)} custom-call(bf16[512,512]{1,0:T(8,128)(2,1)S(1)} %bitcast.19, f32[1,2048]{1,0:T(1,128)S(1)} %bitcast.24, bf16[128,2048]{1,0:T(8,128)(2,1)S(1)} %bitcast.23, bf16[2048,1024]{1,0:T(8,128)(2,1)S(1)} %copy-done), custom_call_target="tpu_custom_call" | custom-call | tf_op jit(solution)/shard_map/project/pallas_call | solution.py:178
  (1 shorter events, 0.0 us)
Async XLA Ops:
  6.5 22.9 %copy-start.1 = (bf16[1,512,512]{2,1,0:T(8,128)(2,1)S(1)}, bf16[1,512,512]{2,1,0:T(8,128)(2,1)}, u32[]{:S(2)}) copy-start(bf16[1,512,512]{2,1,0:T(8,128)(2,1)} %param.10) | copy-start | bytes 1572868
  6.5 22.9 %copy-start.2 = (bf16[1,512,512]{2,1,0:T(8,128)(2,1)S(1)}, bf16[1,512,512]{2,1,0:T(8,128)(2,1)}, u32[]{:S(2)}) copy-start(bf16[1,512,512]{2,1,0:T(8,128)(2,1)} %param.11) | copy-start | bytes 1572868
  6.5 104.6 %all-gather.4.cloned.1.call-start = ((), (), s32[]{:S(2)}) async-start(), calls=%async_computation.2 | async-start | bytes 4259840 | tf_op jit(solution)/shard_map/all_gather | solution.py:135
  25.3 4.2 %collective-permute-start = (bf16[4,192,512]{2,1,0:T(8,128)(2,1)S(1)}, bf16[4,192,512]{2,1,0:T(8,128)(2,1)S(1)}, u32[]{:S(2)}, u32[]{:S(2)}) collective-permute-start(bf16[4,192,512]{2,1,0:T(8,128)(2,1)S(1)} %bitcast.14), channel_id=1, source_target_pairs={{0,64},{64,0},{1,65},{65,1},{2,66},{66,2},{3,67},{67,3},{4,68},{68... | collective-permute-start | bytes 2359304 | tf_op jit(solution)/shard_map/ppermute | solution.py:115
  29.5 0.7 copy-start.6
  32.7 4.2 %collective-permute-start.1 = (bf16[4,192,512]{2,1,0:T(8,128)(2,1)S(1)}, bf16[4,192,512]{2,1,0:T(8,128)(2,1)S(1)}, u32[]{:S(2)}, u32[]{:S(2)}) collective-permute-start(bf16[4,192,512]{2,1,0:T(8,128)(2,1)S(1)} %get-tuple-element.8), channel_id=1, source_target_pairs={{0,64},{64,0},{1,65},{65,1},{2,66},{66,2},{3,67},{67,3},{4,68},{68... | collective-permute-start | bytes 2359304 | tf_op jit(solution)/shard_map/ppermute | solution.py:115
  37.1 34.2 %copy-start.3 = (bf16[1,512,512]{2,1,0:T(8,128)(2,1)S(1)}, bf16[1,512,512]{2,1,0:T(8,128)(2,1)}, u32[]{:S(2)}) copy-start(bf16[1,512,512]{2,1,0:T(8,128)(2,1)} %param.12) | copy-start | bytes 1572868
  67.1 4.2 %collective-permute-start.2 = (bf16[4,192,512]{2,1,0:T(8,128)(2,1)S(1)}, bf16[4,192,512]{2,1,0:T(8,128)(2,1)S(1)}, u32[]{:S(2)}, u32[]{:S(2)}) collective-permute-start(bf16[4,192,512]{2,1,0:T(8,128)(2,1)S(1)} %bitcast.16), channel_id=1, source_target_pairs={{0,64},{64,0},{1,65},{65,1},{2,66},{66,2},{3,67},{67,3},{4,68},{68... | collective-permute-start | bytes 2359304 | tf_op jit(solution)/shard_map/ppermute | solution.py:115
  71.3 39.8 %copy-start.4 = (bf16[8,16,2048]{2,1,0:T(8,128)(2,1)S(1)}, bf16[8,16,2048]{2,1,0:T(8,128)(2,1)}, u32[]{:S(2)}) copy-start(bf16[8,16,2048]{2,1,0:T(8,128)(2,1)} %param.18) | copy-start | bytes 1572868
  71.3 39.8 %copy-start.5 = (f32[2048]{0:T(1024)S(1)}, f32[2048]{0:T(1024)}, u32[]{:S(2)}) copy-start(f32[2048]{0:T(1024)} %param.17) | copy-start | bytes 24580
  111.1 2.2 %copy-start = (bf16[2048,1024]{1,0:T(8,128)(2,1)S(1)}, bf16[2048,1024]{1,0:T(8,128)(2,1)}, u32[]{:S(2)}) copy-start(bf16[2048,1024]{1,0:T(8,128)(2,1)} %all-gather.4.cloned.1.call-done.weight) | copy-start | bytes 12582916
Sparse Core Ops, SparseCore 0:
  10.4 100.6 all-gather.3

commit v2 on v1

--- a/solution.py
+++ b/solution.py
@@ -13,7 +13,7 @@
 F32 = jnp.float32
 VMEM = pl.BlockSpec(memory_space=pltpu.VMEM)
 SMEM = pl.BlockSpec(memory_space=pltpu.SMEM)
-PARAMS = pltpu.CompilerParams(vmem_limit_bytes=40 * 1024 * 1024)
+PARAMS = pltpu.CompilerParams(vmem_limit_bytes=24 * 1024 * 1024)
 
 
 def dot(left, right, a, b):
@@ -56,19 +56,17 @@
     part = rows // 3
     for i, grad in enumerate((g0, g1, g2)):
         for x in range(chips):
-            mine = pl.multiple_of(x * 2 * part + core * part, part)
-            theirs = pl.multiple_of(x * 2 * part + (1 - core) * part, part)
+            base = lax.rem(core_ref[1] + x, chips) * 2 * part
+            mine = pl.multiple_of(base + core * part, part)
+            theirs = pl.multiple_of(base + (1 - core) * part, part)
             keep[x, i * part : (i + 1) * part, :] = grad[pl.ds(mine, part), :]
             send[x, i * part : (i + 1) * part, :] = grad[pl.ds(theirs, part), :]
 
 
-def rescale_kernel(parts, weight, new):
+def rescale_kernel(p0, p1, p2, p3, weight, new):
     base = weight[...].astype(F32)
-    moved = base
-    total = parts[0].astype(F32)
-    for x in range(1, parts.shape[0]):
-        total = total + parts[x].astype(F32)
-    moved = base + total
+    total = p0[...].astype(F32) + p1[...].astype(F32)
+    moved = base + (total + (p2[...].astype(F32) + p3[...].astype(F32)))
     factor = jnp.sqrt(jnp.mean(base * base, -1, keepdims=True) + epsilon) / jnp.sqrt(
         jnp.mean(moved * moved, -1, keepdims=True) + epsilon
     )
@@ -89,26 +87,29 @@
     out[...] = dot(hidden, down[...], 1, 1).astype(BF)
 
 
-def output_kernel(moved, gain, gate, weight, out, *, seqs, heads):
+def output_kernel(core_ref, moved, gain, gate, mine, theirs, out, *, seqs, heads):
     total, size = moved.shape
     rows = total // heads
     tokens = rows // seqs
-    everything = moved[...]
     row = lax.broadcasted_iota(jnp.int32, (rows, total), 0)
     column = lax.broadcasted_iota(jnp.int32, (rows, total), 1)
-    acc = None
+    first = (row % seqs * heads) * tokens + row // seqs
+    left = right = None
     for h in range(heads):
-        source = (row % seqs * heads + h) * tokens + row // seqs
-        pick = jnp.where(column == source, 1.0, 0.0).astype(BF)
-        mixed = dot(pick, everything, 1, 0)
+        pick = jnp.where(column == first + h * tokens, 1.0, 0.0).astype(BF)
+        mixed = dot(pick, moved[...], 1, 0)
         square = jnp.mean(mixed * mixed, -1, keepdims=True)
-        g = gate[:, h * size : (h + 1) * size].astype(F32)
-        normed = mixed * lax.rsqrt(square + epsilon) * gain[:, h * size : (h + 1) * size] * (
-            g * jax.nn.sigmoid(g)
-        )
-        part = dot(normed.astype(BF), weight[h * size : (h + 1) * size, :], 1, 0)
-        acc = part if acc is None else acc + part
-    out[...] = acc.astype(BF)
+        span = slice(h * size, (h + 1) * size)
+        g = gate[:, span].astype(F32)
+        normed = mixed * lax.rsqrt(square + epsilon) * gain[:, span] * (g * jax.nn.sigmoid(g))
+        normed = normed.astype(BF)
+        one, two = dot(normed, mine[span, :], 1, 0), dot(normed, theirs[span, :], 1, 0)
+        left = one if left is None else left + one
+        right = two if right is None else right + two
+    half = mine.shape[1]
+    core = core_ref[0]
+    out[:, pl.ds(pl.multiple_of(core * half, half), half)] = left.astype(BF)
+    out[:, pl.ds(pl.multiple_of((1 - core) * half, half), half)] = right.astype(BF)
 
 
 def swap(a):
@@ -128,11 +129,16 @@
     out_weight,
 ):
     chips = lax.axis_size("x")
-    core = lax.axis_index("core").astype(jnp.int32).reshape(1)
+    core = jnp.stack([lax.axis_index(a).astype(jnp.int32) for a in ("core", "x")])
     tokens, width = key_rows.shape[1:]
     part = fast_gate.shape[1]
     units = part * chips * 2
-    full_weight = lax.all_gather(out_weight, "hs", axis=0, tiled=True)
+    count = lax.axis_size("hs")
+    depth, half = out_weight.shape[0], out_weight.shape[1] // 2
+    piece = lax.dynamic_slice_in_dim(out_weight, core[0] * half, half, 1)
+    mine = lax.all_to_all(
+        jnp.broadcast_to(piece, (count, depth, half)), "hs", split_axis=0, concat_axis=0, tiled=True
+    ).reshape(count * depth, half)
     weights = jnp.concatenate([fast_gate[0], fast_up[0], fast_down[0]], axis=0)
     rows = weights.shape[0]
     own = lax.all_gather(weights, "x", axis=0, tiled=False)
@@ -148,16 +154,20 @@
         compiler_params=PARAMS,
         name="grads",
     )(core, key_rows[0], value_rows[0], step_rates, own, other)
-    summed = (keep.astype(F32) + swap(send).astype(F32)).astype(BF)
-    parts = lax.all_to_all(summed, "x", split_axis=0, concat_axis=0, tiled=True)
+    got = swap(send)
+    parts = []
+    for r in range(chips):
+        summed = (keep[r].astype(F32) + got[r].astype(F32)).astype(BF)
+        ring = [(x, (x + r) % chips) for x in range(chips)]
+        parts.append(lax.ppermute(summed, "x", ring) if r else summed)
     new = pl.pallas_call(
         rescale_kernel,
         out_shape=jax.ShapeDtypeStruct((rows, width), BF),
-        in_specs=[VMEM] * 2,
+        in_specs=[VMEM] * 5,
         out_specs=VMEM,
         compiler_params=PARAMS,
         name="rescale",
-    )(parts, weights)
+    )(*parts, weights)
     own = lax.all_gather(new, "x", axis=0, tiled=False)
     other = swap(own)
     head_out = pl.pallas_call(
@@ -169,6 +179,7 @@
         compiler_params=PARAMS,
         name="query",
     )(core, query_rows[0], own, other)
+    theirs = swap(mine)
     pairs = lax.axis_size("hs")
     blocks = head_out.reshape(pairs, tokens // pairs, width)
     moved = lax.all_to_all(blocks, "hs", split_axis=0, concat_axis=0, tiled=True)
@@ -178,15 +189,17 @@
     result = pl.pallas_call(
         functools.partial(output_kernel, seqs=seqs, heads=heads),
         out_shape=jax.ShapeDtypeStruct((few * seqs, columns), BF),
-        in_specs=[VMEM] * 4,
+        in_specs=[SMEM] + [VMEM] * 5,
         out_specs=VMEM,
         compiler_params=PARAMS,
         name="project",
     )(
+        core,
         moved.reshape(tokens, width),
         out_gain.reshape(1, model),
         gate_input.reshape(few * seqs, model),
-        full_weight,
+        mine,
+        theirs,
     )
     return result.reshape(few, seqs, columns)
 

time: 123 us -> 126 us (1.024)
  the two profiles are of different devices: /device:TPU:4 before, /device:TPU:2 now
where the time goes in v2:
time: 126 us
  blocking collectives  57.7 us (46%)
  starting transfers between devices  35.1 us (28%)
  waiting for transfers between devices  19.4 us (15%)
  Pallas kernels  8.46 us (7%)
  local copies, waits for them, and re-layouts  4.54 us (4%)
    all_to_all x1, blocking collectives, body(): lax.all_to_all(blocks, 'hs', split_axis=0, concat_axis=0, tiled=True)  28.8 us
    all_to_all x1, starting transfers between devices, body(): lax.all_to_all(jnp.broadcast_to(piece, (count, depth, half)), 'hs', split...  16.7 us
    all_gather x1, blocking collectives, body(): own = lax.all_gather(new, 'x', axis=0, tiled=False)  14.5 us
    all_gather x1, blocking collectives, body(): own = lax.all_gather(weights, 'x', axis=0, tiled=False)  14.4 us
    ppermute x3, starting transfers between devices, body(): parts.append(lax.ppermute(summed, 'x', ring) if r else summed)  10.4 us
    ppermute x4, starting transfers between devices, swap(): return lax.ppermute(a, 'core', [(0, 1), (1, 0)])  7.9 us
    ppermute x4, waiting for transfers between devices, swap(): return lax.ppermute(a, 'core', [(0, 1), (1, 0)])  6.68 us
    all_to_all x1, waiting for transfers between devices, body(): lax.all_to_all(jnp.broadcast_to(piece, (count, depth, half)), 'hs', split...  6.46 us
  transfers between devices with their start and end apart: 8, of which 6 were waited for; matrix products, arithmetic and copies ran while one was open for 0% of the time, Pallas kernels for 4%

profile of v2, /device:TPU:2, one launch (start us, length us, event | category | flops | bytes accessed | tf_op | source)
XLA Modules:
  0.0 125.6 jit_solution(5679343562102441056)
XLA Ops:
  0.0 0.0 copy-start
  0.0 0.8 copy-done
  0.8 1.6 %broadcast_in_dim.3 = bf16[64,32,512]{2,1,0:T(8,128)(2,1)} broadcast(bf16[32,512]{1,0:T(8,128)(2,1)S(1)} %constant_dynamic-slice_fusion), dimensions={1,2} | broadcast | bytes 2129920 | tf_op jit(solution)/shard_map/broadcast_in_dim | solution.py:140
  2.4 16.7 %all-to-all-start.1 = ((bf16[64,32,512]{2,1,0:T(8,128)(2,1)}), bf16[64,32,512]{2,1,0:T(8,128)(2,1)S(1)}, u32[]{:S(2)}, u32[]{:S(2)}) async-start(bf16[64,32,512]{2,1,0:T(8,128)(2,1)} %broadcast_in_dim.3), calls=%async_computation.1 | async-start | bytes 4194304 | tf_op jit(solution)/shard_map/all_to_all | solution.py:139
  19.2 0.0 copy-done.7
  19.2 14.4 %all-gather = bf16[768,512]{1,0:T(8,128)(2,1)S(1)} all-gather(bf16[192,512]{1,0:T(8,128)(2,1)S(1)} %pad_maximum_fusion.weight), channel_id=2, replica_groups=mesh['x'=4,'core'=2,'hs'=64] {'x'}, dimensions={0}, use_global_device_ids=true | all-gather | bytes 983040 | tf_op jit(solution)/shard_map/all_gather | solution.py:144
  33.6 1.9 %collective-permute-start = (bf16[4,192,512]{2,1,0:T(8,128)(2,1)S(1)}, bf16[4,192,512]{2,1,0:T(8,128)(2,1)}, u32[]{:S(2)}, u32[]{:S(2)}) collective-permute-start(bf16[4,192,512]{2,1,0:T(8,128)(2,1)S(1)} %bitcast.26), channel_id=1, source_target_pairs={{0,64},{64,0},{1,65},{65,1},{2,66},{66,2},{3,67},{67,3},{4,68},{68... | collective-permute-start | bytes 2359304 | tf_op jit(solution)/shard_map/ppermute | solution.py:116
  35.5 0.1 pad_add_fusion.core_ref
  35.6 2.3 %collective-permute-done.other = bf16[4,192,512]{2,1,0:T(8,128)(2,1)} collective-permute-done((bf16[4,192,512]{2,1,0:T(8,128)(2,1)S(1)}, bf16[4,192,512]{2,1,0:T(8,128)(2,1)}, u32[]{:S(2)}, u32[]{:S(2)}) %collective-permute-start) | collective-permute-done | bytes 786464 | tf_op jit(solution)/shard_map/ppermute | solution.py:116
  37.9 1.0 copy-done.1
  39.0 1.0 copy-done.2
  40.0 3.7 %grads.1 = (bf16[4,192,512]{2,1,0:T(8,128)(2,1)S(1)}, bf16[4,192,512]{2,1,0:T(8,128)(2,1)S(1)}) custom-call(s32[2]{0:T(128)S(1)} %pad_add_fusion.core_ref, bf16[512,512]{1,0:T(8,128)(2,1)S(1)} %bitcast.32, bf16[512,512]{1,0:T(8,128)(2,1)S(1)} %bitcast.33, f32[1,512]{1,0:T(1,128)S(1)} %copy-done.6, bf16[4,192,512]{2,1,0:T(8,128)(2,1)S(1)} %bitcast.27, ...), custom_call_target="tpu_custom_call" | custom-call | tf_op jit(solution)/shard_map/grads/pallas_call | solution.py:148
  43.7 2.0 %collective-permute-start.1 = (bf16[4,192,512]{2,1,0:T(8,128)(2,1)S(1)}, bf16[4,192,512]{2,1,0:T(8,128)(2,1)S(1)}, u32[]{:S(2)}, u32[]{:S(2)}) collective-permute-start(bf16[4,192,512]{2,1,0:T(8,128)(2,1)S(1)} %get-tuple-element.8), channel_id=1, source_target_pairs={{0,64},{64,0},{1,65},{65,1},{2,66},{66,2},{3,67},{67,3},{4,68},{68... | collective-permute-start | bytes 2359304 | tf_op jit(solution)/shard_map/ppermute | solution.py:116
  45.7 2.1 %collective-permute-done.1 = bf16[4,192,512]{2,1,0:T(8,128)(2,1)S(1)} collective-permute-done((bf16[4,192,512]{2,1,0:T(8,128)(2,1)S(1)}, bf16[4,192,512]{2,1,0:T(8,128)(2,1)S(1)}, u32[]{:S(2)}, u32[]{:S(2)}) %collective-permute-start.1) | collective-permute-done | bytes 786464 | tf_op jit(solution)/shard_map/ppermute | solution.py:116
  47.9 0.2 fusion.3
  48.1 1.9 %collective-permute-start.4 = (bf16[192,512]{1,0:T(8,128)(2,1)S(1)}, bf16[192,512]{1,0:T(8,128)(2,1)S(1)}, u32[]{:S(2)}, u32[]{:S(2)}) collective-permute-start(bf16[192,512]{1,0:T(8,128)(2,1)S(1)} %get-tuple-element.9), channel_id=1, source_target_pairs={{0,384},{128,0},{256,128},{384,256},{1,385},{129,1},{257,129},{385... | collective-permute-start | bytes 589832 | tf_op jit(solution)/shard_map/ppermute | solution.py:162
  50.0 4.0 %collective-permute-start.3 = (bf16[192,512]{1,0:T(8,128)(2,1)S(1)}, bf16[192,512]{1,0:T(8,128)(2,1)S(1)}, u32[]{:S(2)}, u32[]{:S(2)}) collective-permute-start(bf16[192,512]{1,0:T(8,128)(2,1)S(1)} %get-tuple-element.10), channel_id=1, source_target_pairs={{0,256},{128,384},{256,0},{384,128},{1,257},{129,385},{257,1},{385... | collective-permute-start | bytes 589832 | tf_op jit(solution)/shard_map/ppermute | solution.py:162
  54.0 4.5 %collective-permute-start.2 = (bf16[192,512]{1,0:T(8,128)(2,1)S(1)}, bf16[192,512]{1,0:T(8,128)(2,1)S(1)}, u32[]{:S(2)}, u32[]{:S(2)}) collective-permute-start(bf16[192,512]{1,0:T(8,128)(2,1)S(1)} %get-tuple-element.11), channel_id=1, source_target_pairs={{0,128},{128,256},{256,384},{384,0},{1,129},{129,257},{257,385},{3... | collective-permute-start | bytes 589832 | tf_op jit(solution)/shard_map/ppermute | solution.py:162
  58.5 0.0 collective-permute-done.4.p3
  58.5 2.9 %collective-permute-done.3.p2 = bf16[192,512]{1,0:T(8,128)(2,1)S(1)} collective-permute-done((bf16[192,512]{1,0:T(8,128)(2,1)S(1)}, bf16[192,512]{1,0:T(8,128)(2,1)S(1)}, u32[]{:S(2)}, u32[]{:S(2)}) %collective-permute-start.3) | collective-permute-done | bytes 196640 | tf_op jit(solution)/shard_map/ppermute | solution.py:162
  61.5 3.4 %collective-permute-done.2.p1 = bf16[192,512]{1,0:T(8,128)(2,1)S(1)} collective-permute-done((bf16[192,512]{1,0:T(8,128)(2,1)S(1)}, bf16[192,512]{1,0:T(8,128)(2,1)S(1)}, u32[]{:S(2)}, u32[]{:S(2)}) %collective-permute-start.2) | collective-permute-done | bytes 196640 | tf_op jit(solution)/shard_map/ppermute | solution.py:162
  64.8 0.3 rescale.1
  65.1 6.5 %all-to-all-done.1 = bf16[64,32,512]{2,1,0:T(8,128)(2,1)S(1)} async-done(((bf16[64,32,512]{2,1,0:T(8,128)(2,1)}), bf16[64,32,512]{2,1,0:T(8,128)(2,1)S(1)}, u32[]{:S(2)}, u32[]{:S(2)}) %all-to-all-start.1) | async-done | bytes 2097184 | tf_op jit(solution)/shard_map/all_to_all | solution.py:139
  71.6 2.0 %collective-permute-start.6 = (bf16[2048,512]{1,0:T(8,128)(2,1)S(1)}, bf16[2048,512]{1,0:T(8,128)(2,1)S(1)}, u32[]{:S(2)}, u32[]{:S(2)}) collective-permute-start(bf16[2048,512]{1,0:T(8,128)(2,1)S(1)} %bitcast.24), channel_id=1, source_target_pairs={{0,64},{64,0},{1,65},{65,1},{2,66},{66,2},{3,67},{67,3},{4,68},{68... | collective-permute-start | bytes 6291464 | tf_op jit(solution)/shard_map/ppermute | solution.py:116
  73.6 14.5 %all-gather.1 = bf16[768,512]{1,0:T(8,128)(2,1)S(1)} all-gather(bf16[192,512]{1,0:T(8,128)(2,1)S(1)} %rescale.1), channel_id=3, replica_groups=mesh['x'=4,'core'=2,'hs'=64] {'x'}, dimensions={0}, use_global_device_ids=true | all-gather | bytes 983040 | tf_op jit(solution)/shard_map/all_gather | solution.py:171
  88.1 1.9 %collective-permute-start.5 = (bf16[4,192,512]{2,1,0:T(8,128)(2,1)S(1)}, bf16[4,192,512]{2,1,0:T(8,128)(2,1)S(1)}, u32[]{:S(2)}, u32[]{:S(2)}) collective-permute-start(bf16[4,192,512]{2,1,0:T(8,128)(2,1)S(1)} %bitcast.28), channel_id=1, source_target_pairs={{0,64},{64,0},{1,65},{65,1},{2,66},{66,2},{3,67},{67,3},{4,68},{68... | collective-permute-start | bytes 2359304 | tf_op jit(solution)/shard_map/ppermute | solution.py:116
  90.1 2.3 %collective-permute-done.5.other = bf16[4,192,512]{2,1,0:T(8,128)(2,1)S(1)} collective-permute-done((bf16[4,192,512]{2,1,0:T(8,128)(2,1)S(1)}, bf16[4,192,512]{2,1,0:T(8,128)(2,1)S(1)}, u32[]{:S(2)}, u32[]{:S(2)}) %collective-permute-start.5) | collective-permute-done | bytes 786464 | tf_op jit(solution)/shard_map/ppermute | solution.py:116
  92.3 1.6 %query.1 = bf16[512,512]{1,0:T(8,128)(2,1)S(1)} custom-call(s32[2]{0:T(128)S(1)} %pad_add_fusion.core_ref, bf16[512,512]{1,0:T(8,128)(2,1)S(1)} %bitcast.34, bf16[4,192,512]{2,1,0:T(8,128)(2,1)S(1)} %bitcast.29, bf16[4,192,512]{2,1,0:T(8,128)(2,1)S(1)} %collective-permute-done.5.other), custom_call_target="tpu_custom_call" | custom-call | tf_op jit(solution)/shard_map/query/pallas_call | solution.py:173
  94.0 28.8 %all_to_all.10 = bf16[64,8,512]{2,1,0:T(8,128)(2,1)S(1)} all-to-all(bf16[64,8,512]{2,1,0:T(8,128)(2,1)S(1)} %bitcast.30), channel_id=1, replica_groups=mesh['x'=4,'core'=2,'hs'=64] {'hs'}, dimensions={0} | all-to-all | bytes 1048576 | tf_op jit(solution)/shard_map/all_to_all | solution.py:185
  122.7 0.0 collective-permute-done.6.theirs
  122.7 0.0 copy-done.5
  122.7 2.9 %project.1 = bf16[128,1024]{1,0:T(8,128)(2,1)} custom-call(s32[2]{0:T(128)S(1)} %pad_add_fusion.core_ref, bf16[512,512]{1,0:T(8,128)(2,1)S(1)} %bitcast.31, f32[1,2048]{1,0:T(1,128)S(1)} %bitcast.36, bf16[128,2048]{1,0:T(8,128)(2,1)S(1)} %bitcast.35, bf16[2048,512]{1,0:T(8,128)(2,1)S(1)} %bitcast.25, bf16[2048,512]{1,0:T(8,128)(2,1)S(1)} %collective-permute-done.6.theirs), custom_call_target="tpu_custom_call" | custom-call | tf_op jit(solution)/shard_map/project/pallas_call | solution.py:189
  (16 shorter events, 0.0 us)
Async XLA Ops:
  0.0 0.8 copy-start
  2.4 16.8 %copy-start.7 = (bf16[1,64,512]{2,1,0:T(8,128)(2,1)S(1)}, bf16[1,64,512]{2,1,0:T(8,128)(2,1)}, u32[]{:S(2)}) copy-start(bf16[1,64,512]{2,1,0:T(8,128)(2,1)} %param.16) | copy-start | bytes 196612
  2.4 16.8 %copy-start.8 = (bf16[1,64,512]{2,1,0:T(8,128)(2,1)S(1)}, bf16[1,64,512]{2,1,0:T(8,128)(2,1)}, u32[]{:S(2)}) copy-start(bf16[1,64,512]{2,1,0:T(8,128)(2,1)} %param.15) | copy-start | bytes 196612
  2.4 16.8 %copy-start.9 = (bf16[1,64,512]{2,1,0:T(8,128)(2,1)S(1)}, bf16[1,64,512]{2,1,0:T(8,128)(2,1)}, u32[]{:S(2)}) copy-start(bf16[1,64,512]{2,1,0:T(8,128)(2,1)} %param.14) | copy-start | bytes 196612
  2.4 35.5 %copy-start.6 = (f32[1,512]{1,0:T(1,128)S(1)}, f32[1,512]{1,0:T(1,128)}, u32[]{:S(2)}) copy-start(f32[1,512]{1,0:T(1,128)} %rate.1) | copy-start | bytes 6148
  2.4 69.1 %all-to-all-start.1 = ((bf16[64,32,512]{2,1,0:T(8,128)(2,1)}), bf16[64,32,512]{2,1,0:T(8,128)(2,1)S(1)}, u32[]{:S(2)}, u32[]{:S(2)}) async-start(bf16[64,32,512]{2,1,0:T(8,128)(2,1)} %broadcast_in_dim.3), calls=%async_computation.1 | async-start | bytes 4194304 | tf_op jit(solution)/shard_map/all_to_all | solution.py:139
  33.6 4.3 %collective-permute-start = (bf16[4,192,512]{2,1,0:T(8,128)(2,1)S(1)}, bf16[4,192,512]{2,1,0:T(8,128)(2,1)}, u32[]{:S(2)}, u32[]{:S(2)}) collective-permute-start(bf16[4,192,512]{2,1,0:T(8,128)(2,1)S(1)} %bitcast.26), channel_id=1, source_target_pairs={{0,64},{64,0},{1,65},{65,1},{2,66},{66,2},{3,67},{67,3},{4,68},{68... | collective-permute-start | bytes 2359304 | tf_op jit(solution)/shard_map/ppermute | solution.py:116
  37.9 1.0 copy-start.1
  39.0 1.0 copy-start.2
  43.7 4.2 %collective-permute-start.1 = (bf16[4,192,512]{2,1,0:T(8,128)(2,1)S(1)}, bf16[4,192,512]{2,1,0:T(8,128)(2,1)S(1)}, u32[]{:S(2)}, u32[]{:S(2)}) collective-permute-start(bf16[4,192,512]{2,1,0:T(8,128)(2,1)S(1)} %get-tuple-element.8), channel_id=1, source_target_pairs={{0,64},{64,0},{1,65},{65,1},{2,66},{66,2},{3,67},{67,3},{4,68},{68... | collective-permute-start | bytes 2359304 | tf_op jit(solution)/shard_map/ppermute | solution.py:116
  47.9 44.4 %copy-start.3 = (bf16[1,512,512]{2,1,0:T(8,128)(2,1)S(1)}, bf16[1,512,512]{2,1,0:T(8,128)(2,1)}, u32[]{:S(2)}) copy-start(bf16[1,512,512]{2,1,0:T(8,128)(2,1)} %param.12) | copy-start | bytes 1572868
  48.1 10.4 %collective-permute-start.4 = (bf16[192,512]{1,0:T(8,128)(2,1)S(1)}, bf16[192,512]{1,0:T(8,128)(2,1)S(1)}, u32[]{:S(2)}, u32[]{:S(2)}) collective-permute-start(bf16[192,512]{1,0:T(8,128)(2,1)S(1)} %get-tuple-element.9), channel_id=1, source_target_pairs={{0,384},{128,0},{256,128},{384,256},{1,385},{129,1},{257,129},{385... | collective-permute-start | bytes 589832 | tf_op jit(solution)/shard_map/ppermute | solution.py:162
  50.0 11.5 %collective-permute-start.3 = (bf16[192,512]{1,0:T(8,128)(2,1)S(1)}, bf16[192,512]{1,0:T(8,128)(2,1)S(1)}, u32[]{:S(2)}, u32[]{:S(2)}) collective-permute-start(bf16[192,512]{1,0:T(8,128)(2,1)S(1)} %get-tuple-element.10), channel_id=1, source_target_pairs={{0,256},{128,384},{256,0},{384,128},{1,257},{129,385},{257,1},{385... | collective-permute-start | bytes 589832 | tf_op jit(solution)/shard_map/ppermute | solution.py:162
  54.0 10.8 %collective-permute-start.2 = (bf16[192,512]{1,0:T(8,128)(2,1)S(1)}, bf16[192,512]{1,0:T(8,128)(2,1)S(1)}, u32[]{:S(2)}, u32[]{:S(2)}) collective-permute-start(bf16[192,512]{1,0:T(8,128)(2,1)S(1)} %get-tuple-element.11), channel_id=1, source_target_pairs={{0,128},{128,256},{256,384},{384,0},{1,129},{129,257},{257,385},{3... | collective-permute-start | bytes 589832 | tf_op jit(solution)/shard_map/ppermute | solution.py:162
  71.6 51.2 %copy-start.4 = (bf16[8,16,2048]{2,1,0:T(8,128)(2,1)S(1)}, bf16[8,16,2048]{2,1,0:T(8,128)(2,1)}, u32[]{:S(2)}) copy-start(bf16[8,16,2048]{2,1,0:T(8,128)(2,1)} %param.18) | copy-start | bytes 1572868
  71.6 51.2 %copy-start.5 = (f32[2048]{0:T(1024)S(1)}, f32[2048]{0:T(1024)}, u32[]{:S(2)}) copy-start(f32[2048]{0:T(1024)} %param.17) | copy-start | bytes 24580
  71.6 51.2 %collective-permute-start.6 = (bf16[2048,512]{1,0:T(8,128)(2,1)S(1)}, bf16[2048,512]{1,0:T(8,128)(2,1)S(1)}, u32[]{:S(2)}, u32[]{:S(2)}) collective-permute-start(bf16[2048,512]{1,0:T(8,128)(2,1)S(1)} %bitcast.24), channel_id=1, source_target_pairs={{0,64},{64,0},{1,65},{65,1},{2,66},{66,2},{3,67},{67,3},{4,68},{68... | collective-permute-start | bytes 6291464 | tf_op jit(solution)/shard_map/ppermute | solution.py:116
  88.1 4.2 %collective-permute-start.5 = (bf16[4,192,512]{2,1,0:T(8,128)(2,1)S(1)}, bf16[4,192,512]{2,1,0:T(8,128)(2,1)S(1)}, u32[]{:S(2)}, u32[]{:S(2)}) collective-permute-start(bf16[4,192,512]{2,1,0:T(8,128)(2,1)S(1)} %bitcast.28), channel_id=1, source_target_pairs={{0,64},{64,0},{1,65},{65,1},{2,66},{66,2},{3,67},{67,3},{4,68},{68... | collective-permute-start | bytes 2359304 | tf_op jit(solution)/shard_map/ppermute | solution.py:116

commit v3 on v2

v3 whole, which is shorter than its diff:
```python
import functools

import jax
import jax.numpy as jnp
from jax import lax
from jax.experimental import pallas as pl
from jax.experimental.pallas import tpu as pltpu
from jax.sharding import Mesh
from jax.sharding import PartitionSpec as P

epsilon = 1e-06
BF = jnp.bfloat16
F32 = jnp.float32
VMEM = pl.BlockSpec(memory_space=pltpu.VMEM)
SMEM = pl.BlockSpec(memory_space=pltpu.SMEM)
PARAMS = pltpu.CompilerParams(vmem_limit_bytes=16 * 1024 * 1024)


def dot(left, right, a, b):
    return lax.dot_general(left, right, (((a,), (b,)), ((), ())), preferred_element_type=F32)


def pack_kernel(key, value, rate, down, out):
    tokens, width = key.shape
    column = jnp.transpose(jnp.broadcast_to(rate[...], (128, tokens)))
    out[:tokens, :] = key[...]
    out[tokens : 2 * tokens, :] = (
        jnp.concatenate([column] * (width // 128), axis=1) * value[...].astype(F32)
    ).astype(BF)
    out[2 * tokens :, :] = down[...]


def choose_kernel(place_ref, gate, up, down, other, out):
    core = place_ref[0]
    part, width = gate.shape
    half = width // 2
    own, theirs = down[...], other[other.shape[0] - part :, :]
    first = core == 0
    rows = jnp.concatenate(
        [jnp.where(first, own.astype(F32), theirs.astype(F32)), jnp.where(first, theirs.astype(F32), own.astype(F32))],
        axis=0,
    )
    unit = lax.broadcasted_iota(jnp.int32, (width, half), 0)
    slot = lax.broadcasted_iota(jnp.int32, (width, half), 1)
    source = (slot // part * 2 + core) * part + slot % part
    chosen = dot(rows.astype(BF), jnp.where(unit == source, 1.0, 0.0).astype(BF), 1, 0).astype(BF)
    out[:part, :] = gate[...]
    out[part : 2 * part, :] = up[...]
    out[2 * part : 3 * part, :half] = chosen[:part, :]
    out[2 * part : 3 * part, half:] = chosen[part:, :]
    total = jnp.sum(rows * rows, -1, keepdims=True)
    total = jnp.transpose(jnp.broadcast_to(total, (2 * part, 128)))[:1, :]
    high = total.astype(BF).astype(F32)
    middle = (total - high).astype(BF).astype(F32)
    low = total - high - middle
    tail = out.shape[0] - 3 * part
    row = lax.broadcasted_iota(jnp.int32, (tail, 2 * part), 0)
    terms = jnp.where(row == 0, high, jnp.where(row == 1, middle, jnp.where(row == 2, low, 0.0)))
    out[3 * part :, :] = jnp.concatenate(
        [terms, jnp.zeros((tail, width - 2 * part), F32)], axis=1
    ).astype(BF)


def halves(held):
    chips, _, width = held.shape
    part = width // (2 * chips)
    half = width // 2
    gate = jnp.concatenate([held[x, :part, :] for x in range(chips)], axis=0)
    up = jnp.concatenate([held[x, part : 2 * part, :] for x in range(chips)], axis=0)
    down = jnp.concatenate(
        [
            held[x, 2 * part : 3 * part, c * half : (c + 1) * half]
            for x in range(chips)
            for c in range(2)
        ],
        axis=0,
    )
    return gate, up, down


def grad_kernel(place_ref, mine, theirs, held, o0, o1, o2, o3, g0, g1, g2):
    gate, up, down = halves(held)
    chips, _, width = held.shape
    part = width // (2 * chips)
    half = width // 2
    tokens = width
    total = None
    for rows in (mine, theirs):
        k, scaled = rows[:tokens, :], rows[tokens : 2 * tokens, :]
        pre_gate = dot(k, gate, 1, 1)
        pre_up = dot(k, up, 1, 1)
        back = dot(scaled, down, 1, 0)
        sig = jax.nn.sigmoid(pre_gate)
        act = pre_gate * sig
        hidden = (act * pre_up).astype(BF)
        back_gate = (back * pre_up * sig * (1.0 + pre_gate * (1.0 - sig))).astype(BF)
        back_up = (back * act).astype(BF)
        grads = (dot(back_gate, k, 0, 0), dot(back_up, k, 0, 0), dot(scaled, hidden, 0, 0))
        if total is None:
            g0[...], g1[...], g2[...] = grads
            total = grads
        else:
            for g, grad in zip((g0, g1, g2), grads):
                g[...] += grad
    for r, out in enumerate((o0, o1, o2, o3)):
        x = lax.rem(place_ref[1] + r, chips)
        spot = pl.multiple_of(x * part, part)
        out[:part, :] = g0[pl.ds(spot, part), :].astype(BF)
        out[part : 2 * part, :] = g1[pl.ds(spot, part), :].astype(BF)
        for c in range(2):
            spot = pl.multiple_of((2 * x + c) * part, part)
            out[2 * part :, c * half : (c + 1) * half] = g2[pl.ds(spot, part), :].astype(BF)


def rescale_kernel(p0, p1, p2, p3, weight, new):
    rows = p0.shape[0]
    whole = rows // 3 * 2
    base = weight[:rows, :].astype(F32)
    total = p0[...].astype(F32) + p1[...].astype(F32)
    moved = base + (total + (p2[...].astype(F32) + p3[...].astype(F32)))
    factor = jnp.sqrt(jnp.mean(base * base, -1, keepdims=True) + epsilon) / jnp.sqrt(
        jnp.mean(moved * moved, -1, keepdims=True) + epsilon
    )
    new[:whole, :] = (moved * factor)[:whole, :].astype(BF)
    new[whole:, :] = moved[whole:, :].astype(BF)


def query_kernel(query, held, own, other, out):
    chips, _, width = own.shape
    q = query[...]
    result = squares = None
    for rows in (own, other):
        gate, up, down = halves(rows)
        pre_gate = dot(q, gate, 1, 1)
        pre_up = dot(q, up, 1, 1)
        hidden = (pre_gate * jax.nn.sigmoid(pre_gate) * pre_up).astype(BF)
        part = dot(hidden, down, 1, 1)
        d = down.astype(F32)
        square = jnp.sum(d * d, -1, keepdims=True)
        result = part if result is None else result + part
        squares = square if squares is None else squares + square
    moved = jnp.transpose(jnp.broadcast_to(squares, (width, 128)))[:1, :]
    span = width // chips
    tail = own.shape[1]
    base = jnp.concatenate(
        [
            jnp.sum(held[x, tail:, :span].astype(F32), 0, keepdims=True)
            for x in range(chips)
        ],
        axis=1,
    )
    factor = jnp.sqrt(base * (1.0 / width) + epsilon) / jnp.sqrt(moved * (1.0 / width) + epsilon)
    out[...] = (result * factor).astype(BF)


def output_kernel(core_ref, moved, gain, gate, mine, theirs, out, *, seqs, heads):
    total, size = moved.shape
    rows = total // heads
    tokens = rows // seqs
    row = lax.broadcasted_iota(jnp.int32, (rows, total), 0)
    column = lax.broadcasted_iota(jnp.int32, (rows, total), 1)
    first = (row % seqs * heads) * tokens + row // seqs
    left = right = None
    for h in range(heads):
        pick = jnp.where(column == first + h * tokens, 1.0, 0.0).astype(BF)
        mixed = dot(pick, moved[...], 1, 0)
        square = jnp.mean(mixed * mixed, -1, keepdims=True)
        span = slice(h * size, (h + 1) * size)
        g = gate[:, span].astype(F32)
        normed = mixed * lax.rsqrt(square + epsilon) * gain[:, span] * (g * jax.nn.sigmoid(g))
        normed = normed.astype(BF)
        one, two = dot(normed, mine[span, :], 1, 0), dot(normed, theirs[span, :], 1, 0)
        left = one if left is None else left + one
        right = two if right is None else right + two
    half = mine.shape[1]
    core = core_ref[0]
    out[:, pl.ds(pl.multiple_of(core * half, half), half)] = left.astype(BF)
    out[:, pl.ds(pl.multiple_of((1 - core) * half, half), half)] = right.astype(BF)


pin = lax.optimization_barrier


def swap(a):
    return lax.ppermute(a, "core", [(0, 1), (1, 0)])


def body(
    key_rows,
    value_rows,
    query_rows,
    step_rates,
    fast_gate,
    fast_up,
    fast_down,
    out_gain,
    gate_input,
    out_weight,
):
    chips = lax.axis_size("x")
    place = jnp.stack([lax.axis_index(a).astype(jnp.int32) for a in ("core", "x")])
    tokens, width = key_rows.shape[1:]
    part = fast_gate.shape[1]
    rows = 3 * part
    mine = pl.pallas_call(
        pack_kernel,
        out_shape=jax.ShapeDtypeStruct((2 * tokens + part, width), BF),
        in_specs=[VMEM] * 4,
        out_specs=VMEM,
        compiler_params=PARAMS,
        name="pack",
    )(key_rows[0], value_rows[0], step_rates, fast_down[0])
    mine, out_weight = pin((mine, out_weight))
    theirs = swap(mine)
    count = lax.axis_size("hs")
    depth, half = out_weight.shape[0], out_weight.shape[1] // 2
    piece = lax.dynamic_slice_in_dim(out_weight, place[0] * half, half, 1)
    left = lax.all_to_all(
        jnp.broadcast_to(piece, (count, depth, half)), "hs", split_axis=0, concat_axis=0, tiled=True
    ).reshape(count * depth, half)
    weights = pl.pallas_call(
        choose_kernel,
        out_shape=jax.ShapeDtypeStruct((rows + 16, width), BF),
        in_specs=[SMEM] + [VMEM] * 4,
        out_specs=VMEM,
        compiler_params=PARAMS,
        name="choose",
    )(place, fast_gate[0], fast_up[0], fast_down[0], theirs)
    held = lax.all_gather(weights, "x", axis=0, tiled=False)
    sums = pl.pallas_call(
        grad_kernel,
        out_shape=(jax.ShapeDtypeStruct((rows, width), BF),) * chips,
        in_specs=[SMEM] + [VMEM] * 3,
        out_specs=(VMEM,) * chips,
        scratch_shapes=[
            pltpu.VMEM((width // 2, width), F32),
            pltpu.VMEM((width // 2, width), F32),
            pltpu.VMEM((width, width // 2), F32),
        ],
        compiler_params=PARAMS,
        name="grads",
    )(place, mine, theirs, held)
    parts = [
        lax.ppermute(a, "x", [(x, (x + r) % chips) for x in range(chips)]) if r else a
        for r, a in enumerate(sums)
    ]
    new = pl.pallas_call(
        rescale_kernel,
        out_shape=jax.ShapeDtypeStruct((rows, width), BF),
        in_specs=[VMEM] * 5,
        out_specs=VMEM,
        compiler_params=PARAMS,
        name="rescale",
    )(*parts, weights)
    own = lax.all_gather(new, "x", axis=0, tiled=False)
    own, left = pin((own, left))
    other = swap(own)
    right = swap(left)
    head_out = pl.pallas_call(
        query_kernel,
        out_shape=jax.ShapeDtypeStruct((tokens, width), BF),
        in_specs=[VMEM] * 4,
        out_specs=VMEM,
        compiler_params=PARAMS,
        name="query",
    )(query_rows[0], held, own, other)
    blocks = head_out.reshape(count, tokens // count, width)
    moved = lax.all_to_all(blocks, "hs", split_axis=0, concat_axis=0, tiled=True)
    few, seqs, model = gate_input.shape
    heads = model // width
    columns = out_weight.shape[1]
    result = pl.pallas_call(
        functools.partial(output_kernel, seqs=seqs, heads=heads),
        out_shape=jax.ShapeDtypeStruct((few * seqs, columns), BF),
        in_specs=[SMEM] + [VMEM] * 5,
        out_specs=VMEM,
        compiler_params=PARAMS,
        name="project",
    )(
        place,
        moved.reshape(tokens, width),
        out_gain.reshape(1, model),
        gate_input.reshape(few * seqs, model),
        left,
        right,
    )
    return result.reshape(few, seqs, columns)


def solution(mesh):
    ctx, pairs = mesh.devices.shape
    split = Mesh(mesh.devices.reshape(ctx // 2, 2, pairs), ("x", "core", "hs"))
    c = ("x", "core")
    return jax.shard_map(
        body,
        mesh=split,
        in_specs=(
            P("hs", c, None),
            P("hs", c, None),
            P("hs", c, None),
            P("hs", c),
            P("hs", c, None),
            P("hs", c, None),
            P("hs", c, None),
            P(),
            P(c + ("hs",), None, None),
            P("hs", None),
        ),
        out_specs=P(c + ("hs",), None, None),
        check_vma=False,
    )
```

time: 126 us -> 122 us (0.968)
  the two profiles are of different devices: /device:TPU:2 before, /device:TPU:8 now
where the time goes in v3:
time: 122 us
  blocking collectives  60.9 us (50%)
  starting transfers between devices  33.1 us (27%)
  waiting for transfers between devices  11.4 us (9%)
  Pallas kernels  9.6 us (8%)
  local copies, waits for them, and re-layouts  6.46 us (5%)
    all_to_all x1, blocking collectives, body(): lax.all_to_all(blocks, 'hs', split_axis=0, concat_axis=0, tiled=True)  32 us
    all_to_all x1, starting transfers between devices, body(): lax.all_to_all(jnp.broadcast_to(piece, (count, depth, half)), 'hs', split...  16.7 us
    all_gather x1, blocking collectives, body(): own = lax.all_gather(new, 'x', axis=0, tiled=False)  14.8 us
    all_gather x1, blocking collectives, body(): held = lax.all_gather(weights, 'x', axis=0, tiled=False)  14.1 us
    ppermute x3, starting transfers between devices, body(): lax.ppermute(a, 'x', [(x, (x + r) % chips) for x in range(chips)])  10.2 us
    ppermute x3, starting transfers between devices, swap(): return lax.ppermute(a, 'core', [(0, 1), (1, 0)])  6.24 us
    ppermute x3, waiting for transfers between devices, swap(): return lax.ppermute(a, 'core', [(0, 1), (1, 0)])  5.81 us
    ppermute x3, waiting for transfers between devices, body(): lax.ppermute(a, 'x', [(x, (x + r) % chips) for x in range(chips)])  5.63 us
  transfers between devices with their start and end apart: 7, of which 5 were waited for; matrix products, arithmetic and copies ran while one was open for 0% of the time, Pallas kernels for 5%

profile of v3, /device:TPU:8, one launch (start us, length us, event | category | flops | bytes accessed | tf_op | source)
XLA Modules:
  0.0 121.8 jit_solution(9496355808298231251)
XLA Ops:
  0.0 0.0 copy-start
  0.0 1.1 copy-done.4
  1.1 1.0 copy-done.5
  2.1 0.8 copy-done.8
  3.0 0.7 copy-done.13
  3.6 0.2 pack.1.mine
  3.8 0.0 copy-start.1
  3.9 1.6 %broadcast_in_dim.3 = bf16[64,32,512]{2,1,0:T(8,128)(2,1)} broadcast(bf16[32,512]{1,0:T(8,128)(2,1)S(1)} %constant_dynamic-slice_fusion), dimensions={1,2} | broadcast | bytes 2129920 | tf_op jit(solution)/shard_map/broadcast_in_dim | solution.py:219
  5.5 16.7 %all-to-all-start = ((bf16[64,32,512]{2,1,0:T(8,128)(2,1)}), bf16[64,32,512]{2,1,0:T(8,128)(2,1)S(1)}, u32[]{:S(2)}, u32[]{:S(2)}) async-start(bf16[64,32,512]{2,1,0:T(8,128)(2,1)} %broadcast_in_dim.3), calls=%async_computation | async-start | bytes 4194304 | tf_op jit(solution)/shard_map/all_to_all | solution.py:218
  22.2 1.9 %collective-permute-start = (bf16[1088,512]{1,0:T(8,128)(2,1)S(1)}, bf16[1088,512]{1,0:T(8,128)(2,1)}, u32[]{:S(2)}, u32[]{:S(2)}) collective-permute-start(bf16[1088,512]{1,0:T(8,128)(2,1)S(1)} %pack.1.mine), channel_id=1, source_target_pairs={{0,64},{64,0},{1,65},{65,1},{2,66},{66,2},{3,67},{67,3},{4,68},{68... | collective-permute-start | bytes 3342344 | tf_op jit(solution)/shard_map/ppermute | solution.py:185
  24.2 0.1 pad_add_fusion.place_ref.core_ref
  24.3 2.8 %collective-permute-done.other.theirs = bf16[1088,512]{1,0:T(8,128)(2,1)} collective-permute-done((bf16[1088,512]{1,0:T(8,128)(2,1)S(1)}, bf16[1088,512]{1,0:T(8,128)(2,1)}, u32[]{:S(2)}, u32[]{:S(2)}) %collective-permute-start) | collective-permute-done | bytes 1114144 | tf_op jit(solution)/shard_map/ppermute | solution.py:185
  27.0 1.5 %choose.1.weight = bf16[208,512]{1,0:T(8,128)(2,1)S(1)} custom-call(s32[2]{0:T(128)S(1)} %pad_add_fusion.place_ref.core_ref, bf16[64,512]{1,0:T(8,128)(2,1)S(1)} %bitcast.30, bf16[64,512]{1,0:T(8,128)(2,1)S(1)} %bitcast.31, bf16[64,512]{1,0:T(8,128)(2,1)S(1)} %bitcast.29, bf16[1088,512]{1,0:T(8,128)(2,1)} %collective-permute-done.other.theirs), custom_call_target="tpu_custom_call" | custom-call | tf_op jit(solution)/shard_map/choose/pallas_call | solution.py:221
  28.5 14.1 %all-gather = bf16[832,512]{1,0:T(8,128)(2,1)S(1)} all-gather(bf16[208,512]{1,0:T(8,128)(2,1)S(1)} %choose.1.weight), channel_id=2, replica_groups=mesh['x'=4,'core'=2,'hs'=64] {'x'}, dimensions={0}, use_global_device_ids=true | all-gather | bytes 1064960 | tf_op jit(solution)/shard_map/all_gather | solution.py:229
  42.6 3.8 %grads.1 = (bf16[192,512]{1,0:T(8,128)(2,1)S(1)}, bf16[192,512]{1,0:T(8,128)(2,1)S(1)}, bf16[192,512]{1,0:T(8,128)(2,1)S(1)}, bf16[192,512]{1,0:T(8,128)(2,1)S(1)}) custom-call(s32[2]{0:T(128)S(1)} %pad_add_fusion.place_ref.core_ref, bf16[1088,512]{1,0:T(8,128)(2,1)S(1)} %copy-done.2, bf16[1088,512]{1,0:T(8,128)(2,1)} %collective-permute-done.other.theirs, ...), custom_call_target="tpu_custom_call" | custom-call | tf_op jit(solution)/shard_map/grads/pallas_call | solution.py:230
  46.5 3.7 %collective-permute-start.1 = (bf16[192,512]{1,0:T(8,128)(2,1)S(1)}, bf16[192,512]{1,0:T(8,128)(2,1)S(1)}, u32[]{:S(2)}, u32[]{:S(2)}) collective-permute-start(bf16[192,512]{1,0:T(8,128)(2,1)S(1)} %get-tuple-element.15), channel_id=1, source_target_pairs={{0,128},{128,256},{256,384},{384,0},{1,129},{129,257},{257,385},{3... | collective-permute-start | bytes 589832 | tf_op jit(solution)/shard_map/ppermute | solution.py:244
  50.1 4.6 %collective-permute-start.2 = (bf16[192,512]{1,0:T(8,128)(2,1)S(1)}, bf16[192,512]{1,0:T(8,128)(2,1)S(1)}, u32[]{:S(2)}, u32[]{:S(2)}) collective-permute-start(bf16[192,512]{1,0:T(8,128)(2,1)S(1)} %get-tuple-element.16), channel_id=1, source_target_pairs={{0,256},{128,384},{256,0},{384,128},{1,257},{129,385},{257,1},{385... | collective-permute-start | bytes 589832 | tf_op jit(solution)/shard_map/ppermute | solution.py:244
  54.7 1.9 %collective-permute-start.3 = (bf16[192,512]{1,0:T(8,128)(2,1)S(1)}, bf16[192,512]{1,0:T(8,128)(2,1)S(1)}, u32[]{:S(2)}, u32[]{:S(2)}) collective-permute-start(bf16[192,512]{1,0:T(8,128)(2,1)S(1)} %get-tuple-element.17), channel_id=1, source_target_pairs={{0,384},{128,0},{256,128},{384,256},{1,385},{129,1},{257,129},{385... | collective-permute-start | bytes 589832 | tf_op jit(solution)/shard_map/ppermute | solution.py:244
  56.7 0.7 collective-permute-done.1.p1
  57.3 2.4 %collective-permute-done.2.p2 = bf16[192,512]{1,0:T(8,128)(2,1)S(1)} collective-permute-done((bf16[192,512]{1,0:T(8,128)(2,1)S(1)}, bf16[192,512]{1,0:T(8,128)(2,1)S(1)}, u32[]{:S(2)}, u32[]{:S(2)}) %collective-permute-start.2) | collective-permute-done | bytes 196640 | tf_op jit(solution)/shard_map/ppermute | solution.py:244
  59.8 2.5 %collective-permute-done.3.p3 = bf16[192,512]{1,0:T(8,128)(2,1)S(1)} collective-permute-done((bf16[192,512]{1,0:T(8,128)(2,1)S(1)}, bf16[192,512]{1,0:T(8,128)(2,1)S(1)}, u32[]{:S(2)}, u32[]{:S(2)}) %collective-permute-start.3) | collective-permute-done | bytes 196640 | tf_op jit(solution)/shard_map/ppermute | solution.py:244
  62.3 0.2 rescale.1
  62.5 14.8 %all-gather.1 = bf16[768,512]{1,0:T(8,128)(2,1)} all-gather(bf16[192,512]{1,0:T(8,128)(2,1)S(1)} %rescale.1), channel_id=3, replica_groups=mesh['x'=4,'core'=2,'hs'=64] {'x'}, dimensions={0}, use_global_device_ids=true | all-gather | bytes 983040 | tf_op jit(solution)/shard_map/all_gather | solution.py:255
  77.4 0.0 all-to-all-done
  77.4 1.9 %collective-permute-start.5 = (bf16[2048,512]{1,0:T(8,128)(2,1)S(1)}, bf16[2048,512]{1,0:T(8,128)(2,1)S(1)}, u32[]{:S(2)}, u32[]{:S(2)}) collective-permute-start(bf16[2048,512]{1,0:T(8,128)(2,1)S(1)} %bitcast.16), channel_id=1, source_target_pairs={{0,64},{64,0},{1,65},{65,1},{2,66},{66,2},{3,67},{67,3},{4,68},{68... | collective-permute-start | bytes 6291464 | tf_op jit(solution)/shard_map/ppermute | solution.py:185
  79.3 2.4 %collective-permute-start.4 = (bf16[4,192,512]{2,1,0:T(8,128)(2,1)}, bf16[4,192,512]{2,1,0:T(8,128)(2,1)S(1)}, u32[]{:S(2)}, u32[]{:S(2)}) collective-permute-start(bf16[4,192,512]{2,1,0:T(8,128)(2,1)} %bitcast.20), channel_id=1, source_target_pairs={{0,64},{64,0},{1,65},{65,1},{2,66},{66,2},{3,67},{67,3},{4,68},{68... | collective-permute-start | bytes 2359304 | tf_op jit(solution)/shard_map/ppermute | solution.py:185
  81.7 3.0 %collective-permute-done.4.other = bf16[4,192,512]{2,1,0:T(8,128)(2,1)S(1)} collective-permute-done((bf16[4,192,512]{2,1,0:T(8,128)(2,1)}, bf16[4,192,512]{2,1,0:T(8,128)(2,1)S(1)}, u32[]{:S(2)}, u32[]{:S(2)}) %collective-permute-start.4) | collective-permute-done | bytes 786464 | tf_op jit(solution)/shard_map/ppermute | solution.py:185
  84.7 1.1 copy-done.3
  85.9 1.0 query.1
  86.9 32.0 %all_to_all.10 = bf16[64,8,512]{2,1,0:T(8,128)(2,1)S(1)} all-to-all(bf16[64,8,512]{2,1,0:T(8,128)(2,1)S(1)} %bitcast.22), channel_id=1, replica_groups=mesh['x'=4,'core'=2,'hs'=64] {'hs'}, dimensions={0} | all-to-all | bytes 1048576 | tf_op jit(solution)/shard_map/all_to_all | solution.py:268
  118.9 0.0 collective-permute-done.5.theirs
  118.9 2.9 %project.1 = bf16[128,1024]{1,0:T(8,128)(2,1)} custom-call(s32[2]{0:T(128)S(1)} %pad_add_fusion.place_ref.core_ref, bf16[512,512]{1,0:T(8,128)(2,1)S(1)} %bitcast.23, f32[1,2048]{1,0:T(1,128)S(1)} %bitcast.32, bf16[128,2048]{1,0:T(8,128)(2,1)S(1)} %bitcast.27, bf16[2048,512]{1,0:T(8,128)(2,1)S(1)} %bitcast.17, ...), custom_call_target="tpu_custom_call" | custom-call | tf_op jit(solution)/shard_map/project/pallas_call | solution.py:272
  (22 shorter events, 0.1 us)
Async XLA Ops:
  0.0 3.8 %copy-start = (bf16[32,1024]{1,0:T(8,128)(2,1)S(1)}, bf16[32,1024]{1,0:T(8,128)(2,1)}, u32[]{:S(2)}) copy-start(bf16[32,1024]{1,0:T(8,128)(2,1)} %param.19) | copy-start | bytes 196612
  0.0 1.1 copy-start.4
  1.1 1.0 copy-start.5
  2.1 0.8 copy-start.8
  3.0 0.7 copy-start.13
  3.8 18.4 %copy-start.1 = (bf16[1088,512]{1,0:T(8,128)(2,1)}, bf16[1088,512]{1,0:T(8,128)(2,1)S(1)}, u32[]{:S(2)}) copy-start(bf16[1088,512]{1,0:T(8,128)(2,1)S(1)} %pack.1.mine) | copy-start | bytes 3342340
  5.5 21.5 %copy-start.9 = (bf16[1,64,512]{2,1,0:T(8,128)(2,1)S(1)}, bf16[1,64,512]{2,1,0:T(8,128)(2,1)}, u32[]{:S(2)}) copy-start(bf16[1,64,512]{2,1,0:T(8,128)(2,1)} %param.16) | copy-start | bytes 196612
  5.5 21.5 %copy-start.10 = (bf16[1,64,512]{2,1,0:T(8,128)(2,1)S(1)}, bf16[1,64,512]{2,1,0:T(8,128)(2,1)}, u32[]{:S(2)}) copy-start(bf16[1,64,512]{2,1,0:T(8,128)(2,1)} %param.14) | copy-start | bytes 196612
  5.5 21.5 %copy-start.11 = (bf16[1,64,512]{2,1,0:T(8,128)(2,1)S(1)}, bf16[1,64,512]{2,1,0:T(8,128)(2,1)}, u32[]{:S(2)}) copy-start(bf16[1,64,512]{2,1,0:T(8,128)(2,1)} %param.15) | copy-start | bytes 196612
  5.5 71.8 %all-to-all-start = ((bf16[64,32,512]{2,1,0:T(8,128)(2,1)}), bf16[64,32,512]{2,1,0:T(8,128)(2,1)S(1)}, u32[]{:S(2)}, u32[]{:S(2)}) async-start(bf16[64,32,512]{2,1,0:T(8,128)(2,1)} %broadcast_in_dim.3), calls=%async_computation | async-start | bytes 4194304 | tf_op jit(solution)/shard_map/all_to_all | solution.py:218
  22.2 4.8 %collective-permute-start = (bf16[1088,512]{1,0:T(8,128)(2,1)S(1)}, bf16[1088,512]{1,0:T(8,128)(2,1)}, u32[]{:S(2)}, u32[]{:S(2)}) collective-permute-start(bf16[1088,512]{1,0:T(8,128)(2,1)S(1)} %pack.1.mine), channel_id=1, source_target_pairs={{0,64},{64,0},{1,65},{65,1},{2,66},{66,2},{3,67},{67,3},{4,68},{68... | collective-permute-start | bytes 3342344 | tf_op jit(solution)/shard_map/ppermute | solution.py:185
  24.2 18.4 %copy-start.2 = (bf16[1088,512]{1,0:T(8,128)(2,1)S(1)}, bf16[1088,512]{1,0:T(8,128)(2,1)}, u32[]{:S(2)}) copy-start(bf16[1088,512]{1,0:T(8,128)(2,1)} %copy-done.1) | copy-start | bytes 3342340
  42.6 42.1 %copy-start.6 = (bf16[1,512,512]{2,1,0:T(8,128)(2,1)S(1)}, bf16[1,512,512]{2,1,0:T(8,128)(2,1)}, u32[]{:S(2)}) copy-start(bf16[1,512,512]{2,1,0:T(8,128)(2,1)} %param.12) | copy-start | bytes 1572868
  46.5 10.9 %collective-permute-start.1 = (bf16[192,512]{1,0:T(8,128)(2,1)S(1)}, bf16[192,512]{1,0:T(8,128)(2,1)S(1)}, u32[]{:S(2)}, u32[]{:S(2)}) collective-permute-start(bf16[192,512]{1,0:T(8,128)(2,1)S(1)} %get-tuple-element.15), channel_id=1, source_target_pairs={{0,128},{128,256},{256,384},{384,0},{1,129},{129,257},{257,385},{3... | collective-permute-start | bytes 589832 | tf_op jit(solution)/shard_map/ppermute | solution.py:244
  50.1 9.6 %collective-permute-start.2 = (bf16[192,512]{1,0:T(8,128)(2,1)S(1)}, bf16[192,512]{1,0:T(8,128)(2,1)S(1)}, u32[]{:S(2)}, u32[]{:S(2)}) collective-permute-start(bf16[192,512]{1,0:T(8,128)(2,1)S(1)} %get-tuple-element.16), channel_id=1, source_target_pairs={{0,256},{128,384},{256,0},{384,128},{1,257},{129,385},{257,1},{385... | collective-permute-start | bytes 589832 | tf_op jit(solution)/shard_map/ppermute | solution.py:244
  54.7 7.6 %collective-permute-start.3 = (bf16[192,512]{1,0:T(8,128)(2,1)S(1)}, bf16[192,512]{1,0:T(8,128)(2,1)S(1)}, u32[]{:S(2)}, u32[]{:S(2)}) collective-permute-start(bf16[192,512]{1,0:T(8,128)(2,1)S(1)} %get-tuple-element.17), channel_id=1, source_target_pairs={{0,384},{128,0},{256,128},{384,256},{1,385},{129,1},{257,129},{385... | collective-permute-start | bytes 589832 | tf_op jit(solution)/shard_map/ppermute | solution.py:244
  77.4 41.5 %collective-permute-start.5 = (bf16[2048,512]{1,0:T(8,128)(2,1)S(1)}, bf16[2048,512]{1,0:T(8,128)(2,1)S(1)}, u32[]{:S(2)}, u32[]{:S(2)}) collective-permute-start(bf16[2048,512]{1,0:T(8,128)(2,1)S(1)} %bitcast.16), channel_id=1, source_target_pairs={{0,64},{64,0},{1,65},{65,1},{2,66},{66,2},{3,67},{67,3},{4,68},{68... | collective-permute-start | bytes 6291464 | tf_op jit(solution)/shard_map/ppermute | solution.py:185
  79.3 5.5 %collective-permute-start.4 = (bf16[4,192,512]{2,1,0:T(8,128)(2,1)}, bf16[4,192,512]{2,1,0:T(8,128)(2,1)S(1)}, u32[]{:S(2)}, u32[]{:S(2)}) collective-permute-start(bf16[4,192,512]{2,1,0:T(8,128)(2,1)} %bitcast.20), channel_id=1, source_target_pairs={{0,64},{64,0},{1,65},{65,1},{2,66},{66,2},{3,67},{67,3},{4,68},{68... | collective-permute-start | bytes 2359304 | tf_op jit(solution)/shard_map/ppermute | solution.py:185
  84.7 1.1 copy-start.3
  85.9 33.0 %copy-start.7 = (bf16[8,16,2048]{2,1,0:T(8,128)(2,1)S(1)}, bf16[8,16,2048]{2,1,0:T(8,128)(2,1)}, u32[]{:S(2)}) copy-start(bf16[8,16,2048]{2,1,0:T(8,128)(2,1)} %param.18) | copy-start | bytes 1572868
  85.9 33.0 %copy-start.12 = (f32[2048]{0:T(1024)S(1)}, f32[2048]{0:T(1024)}, u32[]{:S(2)}) copy-start(f32[2048]{0:T(1024)} %param.17) | copy-start | bytes 24580

commit v4 on v3

--- a/solution.py
+++ b/solution.py
@@ -12,29 +12,43 @@
 BF = jnp.bfloat16
 F32 = jnp.float32
 VMEM = pl.BlockSpec(memory_space=pltpu.VMEM)
+HBM = pl.BlockSpec(memory_space=pltpu.HBM)
 SMEM = pl.BlockSpec(memory_space=pltpu.SMEM)
-PARAMS = pltpu.CompilerParams(vmem_limit_bytes=16 * 1024 * 1024)
+PARAMS = pltpu.CompilerParams(vmem_limit_bytes=20 * 1024 * 1024)
 
 
 def dot(left, right, a, b):
     return lax.dot_general(left, right, (((a,), (b,)), ((), ())), preferred_element_type=F32)
 
 
-def pack_kernel(key, value, rate, down, out):
+def pack_kernel(key, value, rate, down, out, value_buf, rate_buf, sems):
     tokens, width = key.shape
-    column = jnp.transpose(jnp.broadcast_to(rate[...], (128, tokens)))
-    out[:tokens, :] = key[...]
+    part = down.shape[0]
+    copies = [
+        pltpu.make_async_copy(rate, rate_buf, sems.at[0]),
+        pltpu.make_async_copy(value, value_buf, sems.at[1]),
+        pltpu.make_async_copy(key, out.at[pl.ds(0, tokens), :], sems.at[2]),
+        pltpu.make_async_copy(down, out.at[pl.ds(2 * tokens, part), :], sems.at[3]),
+    ]
+    for copy in copies:
+        copy.start()
+    copies[0].wait()
+    column = jnp.transpose(jnp.broadcast_to(rate_buf[...], (128, tokens)))
+    copies[1].wait()
     out[tokens : 2 * tokens, :] = (
-        jnp.concatenate([column] * (width // 128), axis=1) * value[...].astype(F32)
+        jnp.concatenate([column] * (width // 128), axis=1) * value_buf[...].astype(F32)
     ).astype(BF)
-    out[2 * tokens :, :] = down[...]
+    copies[2].wait()
+    copies[3].wait()
 
 
 def choose_kernel(place_ref, gate, up, down, other, out):
     core = place_ref[0]
     part, width = gate.shape
     half = width // 2
-    own, theirs = down[...], other[other.shape[0] - part :, :]
+    out[:part, :] = gate[...]
+    out[part : 2 * part, :] = up[...]
+    own, theirs = down[...], other[...]
     first = core == 0
     rows = jnp.concatenate(
         [jnp.where(first, own.astype(F32), theirs.astype(F32)), jnp.where(first, theirs.astype(F32), own.astype(F32))],
@@ -44,8 +58,6 @@
     slot = lax.broadcasted_iota(jnp.int32, (width, half), 1)
     source = (slot // part * 2 + core) * part + slot % part
     chosen = dot(rows.astype(BF), jnp.where(unit == source, 1.0, 0.0).astype(BF), 1, 0).astype(BF)
-    out[:part, :] = gate[...]
-    out[part : 2 * part, :] = up[...]
     out[2 * part : 3 * part, :half] = chosen[:part, :]
     out[2 * part : 3 * part, half:] = chosen[part:, :]
     total = jnp.sum(rows * rows, -1, keepdims=True)
@@ -78,14 +90,18 @@
     return gate, up, down
 
 
-def grad_kernel(place_ref, mine, theirs, held, o0, o1, o2, o3, g0, g1, g2):
+def grad_kernel(place_ref, mine, theirs, held, o0, o1, o2, o3, g0, g1, g2, fetched, sem):
     gate, up, down = halves(held)
     chips, _, width = held.shape
     part = width // (2 * chips)
     half = width // 2
     tokens = width
     total = None
-    for rows in (mine, theirs):
+    copy = pltpu.make_async_copy(theirs.at[pl.ds(0, 2 * tokens), :], fetched, sem)
+    copy.start()
+    for rows in (mine, fetched):
+        if rows is fetched:
+            copy.wait()
         k, scaled = rows[:tokens, :], rows[tokens : 2 * tokens, :]
         pre_gate = dot(k, gate, 1, 1)
         pre_up = dot(k, up, 1, 1)
@@ -205,19 +221,25 @@
     mine = pl.pallas_call(
         pack_kernel,
         out_shape=jax.ShapeDtypeStruct((2 * tokens + part, width), BF),
-        in_specs=[VMEM] * 4,
-        out_specs=VMEM,
-        compiler_params=PARAMS,
+        in_specs=[HBM] * 4,
+        out_specs=VMEM,
+        scratch_shapes=[
+            pltpu.VMEM((tokens, width), BF),
+            pltpu.VMEM((1, tokens), F32),
+            pltpu.SemaphoreType.DMA((4,)),
+        ],
+        compiler_params=pltpu.CompilerParams(vmem_limit_bytes=60 * 1024 * 1024),
         name="pack",
     )(key_rows[0], value_rows[0], step_rates, fast_down[0])
-    mine, out_weight = pin((mine, out_weight))
     theirs = swap(mine)
     count = lax.axis_size("hs")
     depth, half = out_weight.shape[0], out_weight.shape[1] // 2
     piece = lax.dynamic_slice_in_dim(out_weight, place[0] * half, half, 1)
-    left = lax.all_to_all(
-        jnp.broadcast_to(piece, (count, depth, half)), "hs", split_axis=0, concat_axis=0, tiled=True
-    ).reshape(count * depth, half)
+    pieces = jnp.broadcast_to(piece, (count, depth, half))
+    pieces, theirs = pin((pieces, theirs))
+    left = lax.all_to_all(pieces, "hs", split_axis=0, concat_axis=0, tiled=True).reshape(
+        count * depth, half
+    )
     weights = pl.pallas_call(
         choose_kernel,
         out_shape=jax.ShapeDtypeStruct((rows + 16, width), BF),
@@ -225,17 +247,19 @@
         out_specs=VMEM,
         compiler_params=PARAMS,
         name="choose",
-    )(place, fast_gate[0], fast_up[0], fast_down[0], theirs)
+    )(place, fast_gate[0], fast_up[0], fast_down[0], theirs[2 * tokens :])
     held = lax.all_gather(weights, "x", axis=0, tiled=False)
     sums = pl.pallas_call(
         grad_kernel,
         out_shape=(jax.ShapeDtypeStruct((rows, width), BF),) * chips,
-        in_specs=[SMEM] + [VMEM] * 3,
+        in_specs=[SMEM, VMEM, HBM, VMEM],
         out_specs=(VMEM,) * chips,
         scratch_shapes=[
             pltpu.VMEM((width // 2, width), F32),
             pltpu.VMEM((width // 2, width), F32),
             pltpu.VMEM((width, width // 2), F32),
+            pltpu.VMEM((2 * tokens, width), BF),
+            pltpu.SemaphoreType.DMA,
         ],
         compiler_params=PARAMS,
         name="grads",
@@ -253,9 +277,7 @@
         name="rescale",
     )(*parts, weights)
     own = lax.all_gather(new, "x", axis=0, tiled=False)
-    own, left = pin((own, left))
     other = swap(own)
-    right = swap(left)
     head_out = pl.pallas_call(
         query_kernel,
         out_shape=jax.ShapeDtypeStruct((tokens, width), BF),
@@ -264,6 +286,8 @@
         compiler_params=PARAMS,
         name="query",
     )(query_rows[0], held, own, other)
+    head_out, left = pin((head_out, left))
+    right = swap(left)
     blocks = head_out.reshape(count, tokens // count, width)
     moved = lax.all_to_all(blocks, "hs", split_axis=0, concat_axis=0, tiled=True)
     few, seqs, model = gate_input.shape

time: 122 us -> 118 us (0.967)
  local copies, waits for them, and re-layouts: 6.46 us -> 2.64 us
    unnamed x28 -> x20, local copies, waits for them, and re-layouts: 4.8 us -> 0.04 us
    pallas_call x1, Pallas kernels: 0.17 us -> 2.28 us  [body(): pl.pallas_call(pack_kernel, out_shape=jax.ShapeDtypeStruct((2 * tokens +...]
  transfers between devices with their start and end apart: 7 -> 7, of which waited for: 5 -> 5; matrix products, arithmetic and copies ran while one was open for 0% -> 1% of each run, Pallas kernels for 5% -> 5%
where the time goes in v4:
time: 118 us
  blocking collectives  60.1 us (51%)
  starting transfers between devices  33.1 us (28%)
  waiting for transfers between devices  10.8 us (9%)
  Pallas kernels  10.6 us (9%)
  local copies, waits for them, and re-layouts  2.64 us (2%)
    all_to_all x1, blocking collectives, body(): lax.all_to_all(blocks, 'hs', split_axis=0, concat_axis=0, tiled=True)  32.4 us
    all_to_all x1, starting transfers between devices, body(): lax.all_to_all(pieces, 'hs', split_axis=0, concat_axis=0, tiled=True)  16.7 us
    all_gather x1, blocking collectives, body(): own = lax.all_gather(new, 'x', axis=0, tiled=False)  14 us
    all_gather x1, blocking collectives, body(): held = lax.all_gather(weights, 'x', axis=0, tiled=False)  13.8 us
    ppermute x3, starting transfers between devices, body(): lax.ppermute(a, 'x', [(x, (x + r) % chips) for x in range(chips)])  10.5 us
    ppermute x3, starting transfers between devices, swap(): return lax.ppermute(a, 'core', [(0, 1), (1, 0)])  5.88 us
    ppermute x3, waiting for transfers between devices, body(): lax.ppermute(a, 'x', [(x, (x + r) % chips) for x in range(chips)])  5.63 us
    ppermute x3, waiting for transfers between devices, swap(): return lax.ppermute(a, 'core', [(0, 1), (1, 0)])  5.15 us
  transfers between devices with their start and end apart: 7, of which 5 were waited for; matrix products, arithmetic and copies ran while one was open for 1% of the time, Pallas kernels for 5%

profile of v4, /device:TPU:8, one launch (start us, length us, event | category | flops | bytes accessed | tf_op | source)
XLA Modules:
  0.0 117.5 jit_solution(2726112519772409357)
XLA Ops:
  0.0 0.0 copy-start
  0.0 2.3 %pack.1.mine = bf16[1088,512]{1,0:T(8,128)(2,1)} custom-call(bf16[512,512]{1,0:T(8,128)(2,1)} %bitcast.31, bf16[512,512]{1,0:T(8,128)(2,1)} %bitcast.32, f32[1,512]{1,0:T(1,128)} %rate.1, bf16[64,512]{1,0:T(8,128)(2,1)} %bitcast.26), custom_call_target="tpu_custom_call" | custom-call | tf_op jit(solution)/shard_map/pack/pallas_call | solution.py:221
  2.3 1.9 %collective-permute-start = (bf16[1088,512]{1,0:T(8,128)(2,1)}, bf16[1088,512]{1,0:T(8,128)(2,1)S(1)}, u32[]{:S(2)}, u32[]{:S(2)}) collective-permute-start(bf16[1088,512]{1,0:T(8,128)(2,1)} %pack.1.mine), channel_id=1, source_target_pairs={{0,64},{64,0},{1,65},{65,1},{2,66},{66,2},{3,67},{67,3},{4,68},{68... | collective-permute-start | bytes 3342344 | tf_op jit(solution)/shard_map/ppermute | solution.py:201
  4.2 0.0 copy-done
  4.3 2.9 %collective-permute-done.theirs = bf16[1088,512]{1,0:T(8,128)(2,1)S(1)} collective-permute-done((bf16[1088,512]{1,0:T(8,128)(2,1)}, bf16[1088,512]{1,0:T(8,128)(2,1)S(1)}, u32[]{:S(2)}, u32[]{:S(2)}) %collective-permute-start) | collective-permute-done | bytes 1114144 | tf_op jit(solution)/shard_map/ppermute | solution.py:201
  7.2 1.7 %broadcast_in_dim.3 = bf16[64,32,512]{2,1,0:T(8,128)(2,1)} broadcast(bf16[32,512]{1,0:T(8,128)(2,1)S(1)} %constant_dynamic-slice_fusion), dimensions={1,2} | broadcast | bytes 2129920 | tf_op jit(solution)/shard_map/broadcast_in_dim | solution.py:238
  8.8 0.0 copy-done.2
  8.8 16.7 %all-to-all-start = ((bf16[64,32,512]{2,1,0:T(8,128)(2,1)}), bf16[64,32,512]{2,1,0:T(8,128)(2,1)S(1)}, u32[]{:S(2)}, u32[]{:S(2)}) async-start(bf16[64,32,512]{2,1,0:T(8,128)(2,1)} %broadcast_in_dim.3), calls=%async_computation | async-start | bytes 4194304 | tf_op jit(solution)/shard_map/all_to_all | solution.py:240
  25.6 0.0 copy-start.3
  25.6 0.1 pad_add_fusion.place_ref.core_ref
  25.7 0.9 slice.3.other
  26.6 0.0 copy-done.6
  26.6 0.0 copy-done.7
  26.6 0.8 choose.1.weight
  27.4 13.8 %all-gather = bf16[832,512]{1,0:T(8,128)(2,1)S(1)} all-gather(bf16[208,512]{1,0:T(8,128)(2,1)S(1)} %choose.1.weight), channel_id=2, replica_groups=mesh['x'=4,'core'=2,'hs'=64] {'x'}, dimensions={0}, use_global_device_ids=true | all-gather | bytes 1064960 | tf_op jit(solution)/shard_map/all_gather | solution.py:251
  41.2 3.5 %grads.1 = (bf16[192,512]{1,0:T(8,128)(2,1)S(1)}, bf16[192,512]{1,0:T(8,128)(2,1)S(1)}, bf16[192,512]{1,0:T(8,128)(2,1)S(1)}, bf16[192,512]{1,0:T(8,128)(2,1)S(1)}) custom-call(s32[2]{0:T(128)S(1)} %pad_add_fusion.place_ref.core_ref, bf16[1088,512]{1,0:T(8,128)(2,1)S(1)} %copy-done.1, bf16[1088,512]{1,0:T(8,128)(2,1)S(1)} %copy-done.3, ...), custom_call_target="tpu_custom_call" | custom-call | tf_op jit(solution)/shard_map/grads/pallas_call | solution.py:252
  44.7 4.0 %collective-permute-start.1 = (bf16[192,512]{1,0:T(8,128)(2,1)S(1)}, bf16[192,512]{1,0:T(8,128)(2,1)S(1)}, u32[]{:S(2)}, u32[]{:S(2)}) collective-permute-start(bf16[192,512]{1,0:T(8,128)(2,1)S(1)} %get-tuple-element.15), channel_id=1, source_target_pairs={{0,128},{128,256},{256,384},{384,0},{1,129},{129,257},{257,385},{3... | collective-permute-start | bytes 589832 | tf_op jit(solution)/shard_map/ppermute | solution.py:268
  48.6 4.6 %collective-permute-start.2 = (bf16[192,512]{1,0:T(8,128)(2,1)S(1)}, bf16[192,512]{1,0:T(8,128)(2,1)S(1)}, u32[]{:S(2)}, u32[]{:S(2)}) collective-permute-start(bf16[192,512]{1,0:T(8,128)(2,1)S(1)} %get-tuple-element.16), channel_id=1, source_target_pairs={{0,256},{128,384},{256,0},{384,128},{1,257},{129,385},{257,1},{385... | collective-permute-start | bytes 589832 | tf_op jit(solution)/shard_map/ppermute | solution.py:268
  53.2 1.9 %collective-permute-start.3 = (bf16[192,512]{1,0:T(8,128)(2,1)S(1)}, bf16[192,512]{1,0:T(8,128)(2,1)S(1)}, u32[]{:S(2)}, u32[]{:S(2)}) collective-permute-start(bf16[192,512]{1,0:T(8,128)(2,1)S(1)} %get-tuple-element.17), channel_id=1, source_target_pairs={{0,384},{128,0},{256,128},{384,256},{1,385},{129,1},{257,129},{385... | collective-permute-start | bytes 589832 | tf_op jit(solution)/shard_map/ppermute | solution.py:268
  55.2 0.2 collective-permute-done.1.p1
  55.4 2.3 %collective-permute-done.2.p2 = bf16[192,512]{1,0:T(8,128)(2,1)S(1)} collective-permute-done((bf16[192,512]{1,0:T(8,128)(2,1)S(1)}, bf16[192,512]{1,0:T(8,128)(2,1)S(1)}, u32[]{:S(2)}, u32[]{:S(2)}) %collective-permute-start.2) | collective-permute-done | bytes 196640 | tf_op jit(solution)/shard_map/ppermute | solution.py:268
  57.7 3.1 %collective-permute-done.3.p3 = bf16[192,512]{1,0:T(8,128)(2,1)S(1)} collective-permute-done((bf16[192,512]{1,0:T(8,128)(2,1)S(1)}, bf16[192,512]{1,0:T(8,128)(2,1)S(1)}, u32[]{:S(2)}, u32[]{:S(2)}) %collective-permute-start.3) | collective-permute-done | bytes 196640 | tf_op jit(solution)/shard_map/ppermute | solution.py:268
  60.8 0.2 rescale.1
  61.0 14.0 %all-gather.1 = bf16[768,512]{1,0:T(8,128)(2,1)S(1)} all-gather(bf16[192,512]{1,0:T(8,128)(2,1)S(1)} %rescale.1), channel_id=3, replica_groups=mesh['x'=4,'core'=2,'hs'=64] {'x'}, dimensions={0}, use_global_device_ids=true | all-gather | bytes 983040 | tf_op jit(solution)/shard_map/all_gather | solution.py:279
  75.0 1.9 %collective-permute-start.4 = (bf16[4,192,512]{2,1,0:T(8,128)(2,1)S(1)}, bf16[4,192,512]{2,1,0:T(8,128)(2,1)S(1)}, u32[]{:S(2)}, u32[]{:S(2)}) collective-permute-start(bf16[4,192,512]{2,1,0:T(8,128)(2,1)S(1)} %bitcast.20), channel_id=1, source_target_pairs={{0,64},{64,0},{1,65},{65,1},{2,66},{66,2},{3,67},{67,3},{4,68},{68... | collective-permute-start | bytes 2359304 | tf_op jit(solution)/shard_map/ppermute | solution.py:201
  76.9 2.3 %collective-permute-done.4.other = bf16[4,192,512]{2,1,0:T(8,128)(2,1)S(1)} collective-permute-done((bf16[4,192,512]{2,1,0:T(8,128)(2,1)S(1)}, bf16[4,192,512]{2,1,0:T(8,128)(2,1)S(1)}, u32[]{:S(2)}, u32[]{:S(2)}) %collective-permute-start.4) | collective-permute-done | bytes 786464 | tf_op jit(solution)/shard_map/ppermute | solution.py:201
  79.2 1.0 query.1
  80.2 0.0 all-to-all-done
  80.2 2.0 %collective-permute-start.5 = (bf16[2048,512]{1,0:T(8,128)(2,1)S(1)}, bf16[2048,512]{1,0:T(8,128)(2,1)S(1)}, u32[]{:S(2)}, u32[]{:S(2)}) collective-permute-start(bf16[2048,512]{1,0:T(8,128)(2,1)S(1)} %bitcast.16), channel_id=1, source_target_pairs={{0,64},{64,0},{1,65},{65,1},{2,66},{66,2},{3,67},{67,3},{4,68},{68... | collective-permute-start | bytes 6291464 | tf_op jit(solution)/shard_map/ppermute | solution.py:201
  82.3 32.4 %all_to_all.10 = bf16[64,8,512]{2,1,0:T(8,128)(2,1)S(1)} all-to-all(bf16[64,8,512]{2,1,0:T(8,128)(2,1)S(1)} %bitcast.22), channel_id=1, replica_groups=mesh['x'=4,'core'=2,'hs'=64] {'hs'}, dimensions={0} | all-to-all | bytes 1048576 | tf_op jit(solution)/shard_map/all_to_all | solution.py:292
  114.6 0.0 collective-permute-done.5.theirs
  114.6 2.9 %project.1 = bf16[128,1024]{1,0:T(8,128)(2,1)} custom-call(s32[2]{0:T(128)S(1)} %pad_add_fusion.place_ref.core_ref, bf16[512,512]{1,0:T(8,128)(2,1)S(1)} %bitcast.23, f32[1,2048]{1,0:T(1,128)S(1)} %bitcast.30, bf16[128,2048]{1,0:T(8,128)(2,1)S(1)} %bitcast.25, bf16[2048,512]{1,0:T(8,128)(2,1)S(1)} %bitcast.17, ...), custom_call_target="tpu_custom_call" | custom-call | tf_op jit(solution)/shard_map/project/pallas_call | solution.py:296
  (15 shorter events, 0.0 us)
Async XLA Ops:
  0.0 4.2 %copy-start = (bf16[32,1024]{1,0:T(8,128)(2,1)S(1)}, bf16[32,1024]{1,0:T(8,128)(2,1)}, u32[]{:S(2)}) copy-start(bf16[32,1024]{1,0:T(8,128)(2,1)} %param.19) | copy-start | bytes 196612
  2.3 4.9 %collective-permute-start = (bf16[1088,512]{1,0:T(8,128)(2,1)}, bf16[1088,512]{1,0:T(8,128)(2,1)S(1)}, u32[]{:S(2)}, u32[]{:S(2)}) collective-permute-start(bf16[1088,512]{1,0:T(8,128)(2,1)} %pack.1.mine), channel_id=1, source_target_pairs={{0,64},{64,0},{1,65},{65,1},{2,66},{66,2},{3,67},{67,3},{4,68},{68... | collective-permute-start | bytes 3342344 | tf_op jit(solution)/shard_map/ppermute | solution.py:201
  7.2 1.7 %copy-start.2 = (bf16[1088,512]{1,0:T(8,128)(2,1)}, bf16[1088,512]{1,0:T(8,128)(2,1)S(1)}, u32[]{:S(2)}) copy-start(bf16[1088,512]{1,0:T(8,128)(2,1)S(1)} %collective-permute-done.theirs) | copy-start | bytes 3342340
  8.8 17.8 %copy-start.6 = (bf16[1,64,512]{2,1,0:T(8,128)(2,1)S(1)}, bf16[1,64,512]{2,1,0:T(8,128)(2,1)}, u32[]{:S(2)}) copy-start(bf16[1,64,512]{2,1,0:T(8,128)(2,1)} %param.16) | copy-start | bytes 196612
  8.8 17.8 %copy-start.7 = (bf16[1,64,512]{2,1,0:T(8,128)(2,1)S(1)}, bf16[1,64,512]{2,1,0:T(8,128)(2,1)}, u32[]{:S(2)}) copy-start(bf16[1,64,512]{2,1,0:T(8,128)(2,1)} %param.14) | copy-start | bytes 196612
  8.8 17.8 %copy-start.8 = (bf16[1,64,512]{2,1,0:T(8,128)(2,1)S(1)}, bf16[1,64,512]{2,1,0:T(8,128)(2,1)}, u32[]{:S(2)}) copy-start(bf16[1,64,512]{2,1,0:T(8,128)(2,1)} %param.15) | copy-start | bytes 196612
  8.8 32.3 %copy-start.1 = (bf16[1088,512]{1,0:T(8,128)(2,1)S(1)}, bf16[1088,512]{1,0:T(8,128)(2,1)}, u32[]{:S(2)}) copy-start(bf16[1088,512]{1,0:T(8,128)(2,1)} %pack.1.mine) | copy-start | bytes 3342340
  8.8 71.4 %all-to-all-start = ((bf16[64,32,512]{2,1,0:T(8,128)(2,1)}), bf16[64,32,512]{2,1,0:T(8,128)(2,1)S(1)}, u32[]{:S(2)}, u32[]{:S(2)}) async-start(bf16[64,32,512]{2,1,0:T(8,128)(2,1)} %broadcast_in_dim.3), calls=%async_computation | async-start | bytes 4194304 | tf_op jit(solution)/shard_map/all_to_all | solution.py:240
  25.6 15.6 %copy-start.3 = (bf16[1088,512]{1,0:T(8,128)(2,1)S(1)}, bf16[1088,512]{1,0:T(8,128)(2,1)}, u32[]{:S(2)}) copy-start(bf16[1088,512]{1,0:T(8,128)(2,1)} %copy-done.2) | copy-start | bytes 3342340
  41.2 38.0 %copy-start.4 = (bf16[1,512,512]{2,1,0:T(8,128)(2,1)S(1)}, bf16[1,512,512]{2,1,0:T(8,128)(2,1)}, u32[]{:S(2)}) copy-start(bf16[1,512,512]{2,1,0:T(8,128)(2,1)} %param.12) | copy-start | bytes 1572868
  44.7 10.7 %collective-permute-start.1 = (bf16[192,512]{1,0:T(8,128)(2,1)S(1)}, bf16[192,512]{1,0:T(8,128)(2,1)S(1)}, u32[]{:S(2)}, u32[]{:S(2)}) collective-permute-start(bf16[192,512]{1,0:T(8,128)(2,1)S(1)} %get-tuple-element.15), channel_id=1, source_target_pairs={{0,128},{128,256},{256,384},{384,0},{1,129},{129,257},{257,385},{3... | collective-permute-start | bytes 589832 | tf_op jit(solution)/shard_map/ppermute | solution.py:268
  48.6 9.1 %collective-permute-start.2 = (bf16[192,512]{1,0:T(8,128)(2,1)S(1)}, bf16[192,512]{1,0:T(8,128)(2,1)S(1)}, u32[]{:S(2)}, u32[]{:S(2)}) collective-permute-start(bf16[192,512]{1,0:T(8,128)(2,1)S(1)} %get-tuple-element.16), channel_id=1, source_target_pairs={{0,256},{128,384},{256,0},{384,128},{1,257},{129,385},{257,1},{385... | collective-permute-start | bytes 589832 | tf_op jit(solution)/shard_map/ppermute | solution.py:268
  53.2 7.6 %collective-permute-start.3 = (bf16[192,512]{1,0:T(8,128)(2,1)S(1)}, bf16[192,512]{1,0:T(8,128)(2,1)S(1)}, u32[]{:S(2)}, u32[]{:S(2)}) collective-permute-start(bf16[192,512]{1,0:T(8,128)(2,1)S(1)} %get-tuple-element.17), channel_id=1, source_target_pairs={{0,384},{128,0},{256,128},{384,256},{1,385},{129,1},{257,129},{385... | collective-permute-start | bytes 589832 | tf_op jit(solution)/shard_map/ppermute | solution.py:268
  75.0 4.2 %collective-permute-start.4 = (bf16[4,192,512]{2,1,0:T(8,128)(2,1)S(1)}, bf16[4,192,512]{2,1,0:T(8,128)(2,1)S(1)}, u32[]{:S(2)}, u32[]{:S(2)}) collective-permute-start(bf16[4,192,512]{2,1,0:T(8,128)(2,1)S(1)} %bitcast.20), channel_id=1, source_target_pairs={{0,64},{64,0},{1,65},{65,1},{2,66},{66,2},{3,67},{67,3},{4,68},{68... | collective-permute-start | bytes 2359304 | tf_op jit(solution)/shard_map/ppermute | solution.py:201
  79.2 35.5 %copy-start.5 = (bf16[8,16,2048]{2,1,0:T(8,128)(2,1)S(1)}, bf16[8,16,2048]{2,1,0:T(8,128)(2,1)}, u32[]{:S(2)}) copy-start(bf16[8,16,2048]{2,1,0:T(8,128)(2,1)} %param.18) | copy-start | bytes 1572868
  79.2 35.5 %copy-start.9 = (f32[2048]{0:T(1024)S(1)}, f32[2048]{0:T(1024)}, u32[]{:S(2)}) copy-start(f32[2048]{0:T(1024)} %param.17) | copy-start | bytes 24580
  80.2 34.4 %collective-permute-start.5 = (bf16[2048,512]{1,0:T(8,128)(2,1)S(1)}, bf16[2048,512]{1,0:T(8,128)(2,1)S(1)}, u32[]{:S(2)}, u32[]{:S(2)}) collective-permute-start(bf16[2048,512]{1,0:T(8,128)(2,1)S(1)} %bitcast.16), channel_id=1, source_target_pairs={{0,64},{64,0},{1,65},{65,1},{2,66},{66,2},{3,67},{67,3},{4,68},{68... | collective-permute-start | bytes 6291464 | tf_op jit(solution)/shard_map/ppermute | solution.py:201

commit v5 on v4

--- a/solution.py
+++ b/solution.py
@@ -21,14 +21,12 @@
     return lax.dot_general(left, right, (((a,), (b,)), ((), ())), preferred_element_type=F32)
 
 
-def pack_kernel(key, value, rate, down, out, value_buf, rate_buf, sems):
+def pack_kernel(key, value, rate, out, value_buf, rate_buf, sems):
     tokens, width = key.shape
-    part = down.shape[0]
     copies = [
         pltpu.make_async_copy(rate, rate_buf, sems.at[0]),
         pltpu.make_async_copy(value, value_buf, sems.at[1]),
         pltpu.make_async_copy(key, out.at[pl.ds(0, tokens), :], sems.at[2]),
-        pltpu.make_async_copy(down, out.at[pl.ds(2 * tokens, part), :], sems.at[3]),
     ]
     for copy in copies:
         copy.start()
@@ -39,7 +37,6 @@
         jnp.concatenate([column] * (width // 128), axis=1) * value_buf[...].astype(F32)
     ).astype(BF)
     copies[2].wait()
-    copies[3].wait()
 
 
 def choose_kernel(place_ref, gate, up, down, other, out):
@@ -96,13 +93,13 @@
     part = width // (2 * chips)
     half = width // 2
     tokens = width
-    total = None
-    copy = pltpu.make_async_copy(theirs.at[pl.ds(0, 2 * tokens), :], fetched, sem)
+    found = []
+    copy = pltpu.make_async_copy(theirs, fetched, sem)
     copy.start()
     for rows in (mine, fetched):
         if rows is fetched:
             copy.wait()
-        k, scaled = rows[:tokens, :], rows[tokens : 2 * tokens, :]
+        k, scaled = rows[:tokens, :], rows[tokens:, :]
         pre_gate = dot(k, gate, 1, 1)
         pre_up = dot(k, up, 1, 1)
         back = dot(scaled, down, 1, 0)
@@ -111,21 +108,17 @@
         hidden = (act * pre_up).astype(BF)
         back_gate = (back * pre_up * sig * (1.0 + pre_gate * (1.0 - sig))).astype(BF)
         back_up = (back * act).astype(BF)
-        grads = (dot(back_gate, k, 0, 0), dot(back_up, k, 0, 0), dot(scaled, hidden, 0, 0))
-        if total is None:
-            g0[...], g1[...], g2[...] = grads
-            total = grads
-        else:
-            for g, grad in zip((g0, g1, g2), grads):
-                g[...] += grad
+        found.append((dot(back_gate, k, 0, 0), dot(back_up, k, 0, 0), dot(scaled, hidden, 0, 0)))
+    for g, one, two in zip((g0, g1, g2), *found):
+        g[...] = (one + two).astype(BF)
     for r, out in enumerate((o0, o1, o2, o3)):
         x = lax.rem(place_ref[1] + r, chips)
         spot = pl.multiple_of(x * part, part)
-        out[:part, :] = g0[pl.ds(spot, part), :].astype(BF)
-        out[part : 2 * part, :] = g1[pl.ds(spot, part), :].astype(BF)
+        out[:part, :] = g0[pl.ds(spot, part), :]
+        out[part : 2 * part, :] = g1[pl.ds(spot, part), :]
         for c in range(2):
             spot = pl.multiple_of((2 * x + c) * part, part)
-            out[2 * part :, c * half : (c + 1) * half] = g2[pl.ds(spot, part), :].astype(BF)
+            out[2 * part :, c * half : (c + 1) * half] = g2[pl.ds(spot, part), :]
 
 
 def rescale_kernel(p0, p1, p2, p3, weight, new):
@@ -220,23 +213,23 @@
     rows = 3 * part
     mine = pl.pallas_call(
         pack_kernel,
-        out_shape=jax.ShapeDtypeStruct((2 * tokens + part, width), BF),
-        in_specs=[HBM] * 4,
+        out_shape=jax.ShapeDtypeStruct((2 * tokens, width), BF),
+        in_specs=[HBM] * 3,
         out_specs=VMEM,
         scratch_shapes=[
             pltpu.VMEM((tokens, width), BF),
             pltpu.VMEM((1, tokens), F32),
-            pltpu.SemaphoreType.DMA((4,)),
+            pltpu.SemaphoreType.DMA((3,)),
         ],
         compiler_params=pltpu.CompilerParams(vmem_limit_bytes=60 * 1024 * 1024),
         name="pack",
-    )(key_rows[0], value_rows[0], step_rates, fast_down[0])
+    )(key_rows[0], value_rows[0], step_rates)
+    mine, other_down = pin((mine, swap(fast_down[0])))
     theirs = swap(mine)
     count = lax.axis_size("hs")
     depth, half = out_weight.shape[0], out_weight.shape[1] // 2
     piece = lax.dynamic_slice_in_dim(out_weight, place[0] * half, half, 1)
     pieces = jnp.broadcast_to(piece, (count, depth, half))
-    pieces, theirs = pin((pieces, theirs))
     left = lax.all_to_all(pieces, "hs", split_axis=0, concat_axis=0, tiled=True).reshape(
         count * depth, half
     )
@@ -247,7 +240,7 @@
         out_specs=VMEM,
         compiler_params=PARAMS,
         name="choose",
-    )(place, fast_gate[0], fast_up[0], fast_down[0], theirs[2 * tokens :])
+    )(place, fast_gate[0], fast_up[0], fast_down[0], other_down)
     held = lax.all_gather(weights, "x", axis=0, tiled=False)
     sums = pl.pallas_call(
         grad_kernel,
@@ -255,9 +248,9 @@
         in_specs=[SMEM, VMEM, HBM, VMEM],
         out_specs=(VMEM,) * chips,
         scratch_shapes=[
-            pltpu.VMEM((width // 2, width), F32),
-            pltpu.VMEM((width // 2, width), F32),
-            pltpu.VMEM((width, width // 2), F32),
+            pltpu.VMEM((width // 2, width), BF),
+            pltpu.VMEM((width // 2, width), BF),
+            pltpu.VMEM((width, width // 2), BF),
             pltpu.VMEM((2 * tokens, width), BF),
             pltpu.SemaphoreType.DMA,
         ],

time: 118 us -> 119 us (level)
  waiting for transfers between devices: 10.8 us -> 7.89 us
  starting transfers between devices: 33.1 us -> 35.5 us
    ppermute x3 -> x4, waiting for transfers between devices: 5.15 us -> 2.26 us  [swap(): return lax.ppermute(a, 'core', [(0, 1), (1, 0)])]
    ppermute x3 -> x4, starting transfers between devices: 5.88 us -> 8.54 us  [swap(): return lax.ppermute(a, 'core', [(0, 1), (1, 0)])]
  transfers between devices with their start and end apart: 7 -> 8, of which waited for: 5 -> 4; matrix products, arithmetic and copies ran while one was open for 1% -> 0% of each run, Pallas kernels for 5% -> 7%
where the time goes in v5:
time: 119 us; the launch traced here: 118 us
  blocking collectives  60.6 us (51%)
  starting transfers between devices  35.5 us (30%)
  Pallas kernels  11.6 us (10%)
  waiting for transfers between devices  7.89 us (7%)
  local copies, waits for them, and re-layouts  2.47 us (2%)
    all_to_all x1, blocking collectives, body(): lax.all_to_all(blocks, 'hs', split_axis=0, concat_axis=0, tiled=True)  32.4 us
    all_to_all x1, starting transfers between devices, body(): lax.all_to_all(pieces, 'hs', split_axis=0, concat_axis=0, tiled=True)  16.7 us
    all_gather x1, blocking collectives, body(): own = lax.all_gather(new, 'x', axis=0, tiled=False)  14.2 us
    all_gather x1, blocking collectives, body(): held = lax.all_gather(weights, 'x', axis=0, tiled=False)  14 us
    ppermute x3, starting transfers between devices, body(): lax.ppermute(a, 'x', [(x, (x + r) % chips) for x in range(chips)])  10.2 us
    ppermute x4, starting transfers between devices, swap(): return lax.ppermute(a, 'core', [(0, 1), (1, 0)])  8.54 us
    ppermute x3, waiting for transfers between devices, body(): lax.ppermute(a, 'x', [(x, (x + r) % chips) for x in range(chips)])  5.63 us
    pallas_call x1, Pallas kernels, body(): pl.pallas_call(grad_kernel, out_shape=(jax.ShapeDtypeStruct((rows, width)...  4.48 us
  transfers between devices with their start and end apart: 8, of which 4 were waited for; matrix products, arithmetic and copies ran while one was open for 0% of the time, Pallas kernels for 7%

profile of v5, /device:TPU:8, one launch (start us, length us, event | category | flops | bytes accessed | tf_op | source)
XLA Modules:
  0.0 118.3 jit_solution(16895960896982815616)
XLA Ops:
  0.0 0.0 copy-start
  0.0 0.8 copy-done
  0.8 1.6 %broadcast_in_dim.3 = bf16[64,32,512]{2,1,0:T(8,128)(2,1)} broadcast(bf16[32,512]{1,0:T(8,128)(2,1)S(1)} %constant_dynamic-slice_fusion), dimensions={1,2} | broadcast | bytes 2129920 | tf_op jit(solution)/shard_map/broadcast_in_dim | solution.py:232
  2.4 16.7 %all-to-all-start = ((bf16[64,32,512]{2,1,0:T(8,128)(2,1)}), bf16[64,32,512]{2,1,0:T(8,128)(2,1)S(1)}, u32[]{:S(2)}, u32[]{:S(2)}) async-start(bf16[64,32,512]{2,1,0:T(8,128)(2,1)} %broadcast_in_dim.3), calls=%async_computation | async-start | bytes 4194304 | tf_op jit(solution)/shard_map/all_to_all | solution.py:233
  19.2 0.0 copy-start.4
  19.2 0.0 copy-start.5
  19.2 0.0 copy-done.6
  19.2 2.1 %collective-permute-start = (bf16[64,512]{1,0:T(8,128)(2,1)S(1)}, bf16[64,512]{1,0:T(8,128)(2,1)S(1)}, u32[]{:S(2)}, u32[]{:S(2)}) collective-permute-start(bf16[64,512]{1,0:T(8,128)(2,1)S(1)} %bitcast.28), channel_id=1, source_target_pairs={{0,64},{64,0},{1,65},{65,1},{2,66},{66,2},{3,67},{67,3},{4,68},{68... | collective-permute-start | bytes 196616 | tf_op jit(solution)/shard_map/ppermute | solution.py:194
  21.3 2.2 %pack.1.mine = bf16[1024,512]{1,0:T(8,128)(2,1)} custom-call(bf16[512,512]{1,0:T(8,128)(2,1)} %bitcast.31, bf16[512,512]{1,0:T(8,128)(2,1)} %bitcast.32, f32[1,512]{1,0:T(1,128)} %rate.1), custom_call_target="tpu_custom_call" | custom-call | tf_op jit(solution)/shard_map/pack/pallas_call | solution.py:214
  23.5 0.0 collective-permute-done.other
  23.5 2.5 %collective-permute-start.1 = (bf16[1024,512]{1,0:T(8,128)(2,1)}, bf16[1024,512]{1,0:T(8,128)(2,1)}, u32[]{:S(2)}, u32[]{:S(2)}) collective-permute-start(bf16[1024,512]{1,0:T(8,128)(2,1)} %pack.1.mine), channel_id=1, source_target_pairs={{0,64},{64,0},{1,65},{65,1},{2,66},{66,2},{3,67},{67,3},{4,68},{68... | collective-permute-start | bytes 3145736 | tf_op jit(solution)/shard_map/ppermute | solution.py:194
  26.0 0.1 pad_add_fusion.place_ref.core_ref
  26.1 0.8 choose.1.weight
  26.9 14.0 %all-gather = bf16[832,512]{1,0:T(8,128)(2,1)S(1)} all-gather(bf16[208,512]{1,0:T(8,128)(2,1)S(1)} %choose.1.weight), channel_id=2, replica_groups=mesh['x'=4,'core'=2,'hs'=64] {'x'}, dimensions={0}, use_global_device_ids=true | all-gather | bytes 1064960 | tf_op jit(solution)/shard_map/all_gather | solution.py:244
  40.9 0.0 collective-permute-done.1.theirs
  40.9 4.5 %grads.1 = (bf16[192,512]{1,0:T(8,128)(2,1)S(1)}, bf16[192,512]{1,0:T(8,128)(2,1)S(1)}, bf16[192,512]{1,0:T(8,128)(2,1)S(1)}, bf16[192,512]{1,0:T(8,128)(2,1)S(1)}) custom-call(s32[2]{0:T(128)S(1)} %pad_add_fusion.place_ref.core_ref, bf16[1024,512]{1,0:T(8,128)(2,1)S(1)} %copy-done.1, bf16[1024,512]{1,0:T(8,128)(2,1)} %collective-permute-done.1.theirs, ...), custom_call_target="tpu_custom_call" | custom-call | tf_op jit(solution)/shard_map/grads/pallas_call | solution.py:245
  45.4 3.7 %collective-permute-start.2 = (bf16[192,512]{1,0:T(8,128)(2,1)S(1)}, bf16[192,512]{1,0:T(8,128)(2,1)S(1)}, u32[]{:S(2)}, u32[]{:S(2)}) collective-permute-start(bf16[192,512]{1,0:T(8,128)(2,1)S(1)} %get-tuple-element.16), channel_id=1, source_target_pairs={{0,128},{128,256},{256,384},{384,0},{1,129},{129,257},{257,385},{3... | collective-permute-start | bytes 589832 | tf_op jit(solution)/shard_map/ppermute | solution.py:261
  49.1 4.6 %collective-permute-start.3 = (bf16[192,512]{1,0:T(8,128)(2,1)S(1)}, bf16[192,512]{1,0:T(8,128)(2,1)S(1)}, u32[]{:S(2)}, u32[]{:S(2)}) collective-permute-start(bf16[192,512]{1,0:T(8,128)(2,1)S(1)} %get-tuple-element.17), channel_id=1, source_target_pairs={{0,256},{128,384},{256,0},{384,128},{1,257},{129,385},{257,1},{385... | collective-permute-start | bytes 589832 | tf_op jit(solution)/shard_map/ppermute | solution.py:261
  53.7 1.9 %collective-permute-start.4 = (bf16[192,512]{1,0:T(8,128)(2,1)S(1)}, bf16[192,512]{1,0:T(8,128)(2,1)S(1)}, u32[]{:S(2)}, u32[]{:S(2)}) collective-permute-start(bf16[192,512]{1,0:T(8,128)(2,1)S(1)} %get-tuple-element.18), channel_id=1, source_target_pairs={{0,384},{128,0},{256,128},{384,256},{1,385},{129,1},{257,129},{385... | collective-permute-start | bytes 589832 | tf_op jit(solution)/shard_map/ppermute | solution.py:261
  55.6 0.6 collective-permute-done.2.p1
  56.3 2.3 %collective-permute-done.3.p2 = bf16[192,512]{1,0:T(8,128)(2,1)S(1)} collective-permute-done((bf16[192,512]{1,0:T(8,128)(2,1)S(1)}, bf16[192,512]{1,0:T(8,128)(2,1)S(1)}, u32[]{:S(2)}, u32[]{:S(2)}) %collective-permute-start.3) | collective-permute-done | bytes 196640 | tf_op jit(solution)/shard_map/ppermute | solution.py:261
  58.6 2.7 %collective-permute-done.4.p3 = bf16[192,512]{1,0:T(8,128)(2,1)S(1)} collective-permute-done((bf16[192,512]{1,0:T(8,128)(2,1)S(1)}, bf16[192,512]{1,0:T(8,128)(2,1)S(1)}, u32[]{:S(2)}, u32[]{:S(2)}) %collective-permute-start.4) | collective-permute-done | bytes 196640 | tf_op jit(solution)/shard_map/ppermute | solution.py:261
  61.3 0.2 rescale.1
  61.5 14.2 %all-gather.1 = bf16[768,512]{1,0:T(8,128)(2,1)S(1)} all-gather(bf16[192,512]{1,0:T(8,128)(2,1)S(1)} %rescale.1), channel_id=3, replica_groups=mesh['x'=4,'core'=2,'hs'=64] {'x'}, dimensions={0}, use_global_device_ids=true | all-gather | bytes 983040 | tf_op jit(solution)/shard_map/all_gather | solution.py:272
  75.8 1.9 %collective-permute-start.5 = (bf16[4,192,512]{2,1,0:T(8,128)(2,1)S(1)}, bf16[4,192,512]{2,1,0:T(8,128)(2,1)S(1)}, u32[]{:S(2)}, u32[]{:S(2)}) collective-permute-start(bf16[4,192,512]{2,1,0:T(8,128)(2,1)S(1)} %bitcast.20), channel_id=1, source_target_pairs={{0,64},{64,0},{1,65},{65,1},{2,66},{66,2},{3,67},{67,3},{4,68},{68... | collective-permute-start | bytes 2359304 | tf_op jit(solution)/shard_map/ppermute | solution.py:194
  77.7 2.3 %collective-permute-done.5.other = bf16[4,192,512]{2,1,0:T(8,128)(2,1)S(1)} collective-permute-done((bf16[4,192,512]{2,1,0:T(8,128)(2,1)S(1)}, bf16[4,192,512]{2,1,0:T(8,128)(2,1)S(1)}, u32[]{:S(2)}, u32[]{:S(2)}) %collective-permute-start.5) | collective-permute-done | bytes 786464 | tf_op jit(solution)/shard_map/ppermute | solution.py:194
  79.9 1.0 query.1
  80.9 0.0 all-to-all-done
  81.0 2.0 %collective-permute-start.6 = (bf16[2048,512]{1,0:T(8,128)(2,1)S(1)}, bf16[2048,512]{1,0:T(8,128)(2,1)S(1)}, u32[]{:S(2)}, u32[]{:S(2)}) collective-permute-start(bf16[2048,512]{1,0:T(8,128)(2,1)S(1)} %bitcast.16), channel_id=1, source_target_pairs={{0,64},{64,0},{1,65},{65,1},{2,66},{66,2},{3,67},{67,3},{4,68},{68... | collective-permute-start | bytes 6291464 | tf_op jit(solution)/shard_map/ppermute | solution.py:194
  83.0 32.4 %all_to_all.10 = bf16[64,8,512]{2,1,0:T(8,128)(2,1)S(1)} all-to-all(bf16[64,8,512]{2,1,0:T(8,128)(2,1)S(1)} %bitcast.22), channel_id=1, replica_groups=mesh['x'=4,'core'=2,'hs'=64] {'hs'}, dimensions={0} | all-to-all | bytes 1048576 | tf_op jit(solution)/shard_map/all_to_all | solution.py:285
  115.4 0.0 collective-permute-done.6.theirs
  115.4 2.9 %project.1 = bf16[128,1024]{1,0:T(8,128)(2,1)} custom-call(s32[2]{0:T(128)S(1)} %pad_add_fusion.place_ref.core_ref, bf16[512,512]{1,0:T(8,128)(2,1)S(1)} %bitcast.23, f32[1,2048]{1,0:T(1,128)S(1)} %bitcast.30, bf16[128,2048]{1,0:T(8,128)(2,1)S(1)} %bitcast.25, bf16[2048,512]{1,0:T(8,128)(2,1)S(1)} %bitcast.17, ...), custom_call_target="tpu_custom_call" | custom-call | tf_op jit(solution)/shard_map/project/pallas_call | solution.py:289
  (12 shorter events, 0.0 us)
Async XLA Ops:
  0.0 0.8 copy-start
  2.4 16.7 %copy-start.6 = (bf16[1,64,512]{2,1,0:T(8,128)(2,1)S(1)}, bf16[1,64,512]{2,1,0:T(8,128)(2,1)}, u32[]{:S(2)}) copy-start(bf16[1,64,512]{2,1,0:T(8,128)(2,1)} %param.16) | copy-start | bytes 196612
  2.4 78.5 %all-to-all-start = ((bf16[64,32,512]{2,1,0:T(8,128)(2,1)}), bf16[64,32,512]{2,1,0:T(8,128)(2,1)S(1)}, u32[]{:S(2)}, u32[]{:S(2)}) async-start(bf16[64,32,512]{2,1,0:T(8,128)(2,1)} %broadcast_in_dim.3), calls=%async_computation | async-start | bytes 4194304 | tf_op jit(solution)/shard_map/all_to_all | solution.py:233
  19.2 7.0 %copy-start.4 = (bf16[1,64,512]{2,1,0:T(8,128)(2,1)S(1)}, bf16[1,64,512]{2,1,0:T(8,128)(2,1)}, u32[]{:S(2)}) copy-start(bf16[1,64,512]{2,1,0:T(8,128)(2,1)} %param.14) | copy-start | bytes 196612
  19.2 6.9 %copy-start.5 = (bf16[1,64,512]{2,1,0:T(8,128)(2,1)S(1)}, bf16[1,64,512]{2,1,0:T(8,128)(2,1)}, u32[]{:S(2)}) copy-start(bf16[1,64,512]{2,1,0:T(8,128)(2,1)} %param.15) | copy-start | bytes 196612
  19.2 4.3 %collective-permute-start = (bf16[64,512]{1,0:T(8,128)(2,1)S(1)}, bf16[64,512]{1,0:T(8,128)(2,1)S(1)}, u32[]{:S(2)}, u32[]{:S(2)}) collective-permute-start(bf16[64,512]{1,0:T(8,128)(2,1)S(1)} %bitcast.28), channel_id=1, source_target_pairs={{0,64},{64,0},{1,65},{65,1},{2,66},{66,2},{3,67},{67,3},{4,68},{68... | collective-permute-start | bytes 196616 | tf_op jit(solution)/shard_map/ppermute | solution.py:194
  23.5 17.4 %copy-start.1 = (bf16[1024,512]{1,0:T(8,128)(2,1)S(1)}, bf16[1024,512]{1,0:T(8,128)(2,1)}, u32[]{:S(2)}) copy-start(bf16[1024,512]{1,0:T(8,128)(2,1)} %pack.1.mine) | copy-start | bytes 3145732
  23.5 17.4 %collective-permute-start.1 = (bf16[1024,512]{1,0:T(8,128)(2,1)}, bf16[1024,512]{1,0:T(8,128)(2,1)}, u32[]{:S(2)}, u32[]{:S(2)}) collective-permute-start(bf16[1024,512]{1,0:T(8,128)(2,1)} %pack.1.mine), channel_id=1, source_target_pairs={{0,64},{64,0},{1,65},{65,1},{2,66},{66,2},{3,67},{67,3},{4,68},{68... | collective-permute-start | bytes 3145736 | tf_op jit(solution)/shard_map/ppermute | solution.py:194
  40.9 39.0 %copy-start.2 = (bf16[1,512,512]{2,1,0:T(8,128)(2,1)S(1)}, bf16[1,512,512]{2,1,0:T(8,128)(2,1)}, u32[]{:S(2)}) copy-start(bf16[1,512,512]{2,1,0:T(8,128)(2,1)} %param.12) | copy-start | bytes 1572868
  45.4 10.9 %collective-permute-start.2 = (bf16[192,512]{1,0:T(8,128)(2,1)S(1)}, bf16[192,512]{1,0:T(8,128)(2,1)S(1)}, u32[]{:S(2)}, u32[]{:S(2)}) collective-permute-start(bf16[192,512]{1,0:T(8,128)(2,1)S(1)} %get-tuple-element.16), channel_id=1, source_target_pairs={{0,128},{128,256},{256,384},{384,0},{1,129},{129,257},{257,385},{3... | collective-permute-start | bytes 589832 | tf_op jit(solution)/shard_map/ppermute | solution.py:261
  49.1 9.5 %collective-permute-start.3 = (bf16[192,512]{1,0:T(8,128)(2,1)S(1)}, bf16[192,512]{1,0:T(8,128)(2,1)S(1)}, u32[]{:S(2)}, u32[]{:S(2)}) collective-permute-start(bf16[192,512]{1,0:T(8,128)(2,1)S(1)} %get-tuple-element.17), channel_id=1, source_target_pairs={{0,256},{128,384},{256,0},{384,128},{1,257},{129,385},{257,1},{385... | collective-permute-start | bytes 589832 | tf_op jit(solution)/shard_map/ppermute | solution.py:261
  53.7 7.6 %collective-permute-start.4 = (bf16[192,512]{1,0:T(8,128)(2,1)S(1)}, bf16[192,512]{1,0:T(8,128)(2,1)S(1)}, u32[]{:S(2)}, u32[]{:S(2)}) collective-permute-start(bf16[192,512]{1,0:T(8,128)(2,1)S(1)} %get-tuple-element.18), channel_id=1, source_target_pairs={{0,384},{128,0},{256,128},{384,256},{1,385},{129,1},{257,129},{385... | collective-permute-start | bytes 589832 | tf_op jit(solution)/shard_map/ppermute | solution.py:261
  75.8 4.2 %collective-permute-start.5 = (bf16[4,192,512]{2,1,0:T(8,128)(2,1)S(1)}, bf16[4,192,512]{2,1,0:T(8,128)(2,1)S(1)}, u32[]{:S(2)}, u32[]{:S(2)}) collective-permute-start(bf16[4,192,512]{2,1,0:T(8,128)(2,1)S(1)} %bitcast.20), channel_id=1, source_target_pairs={{0,64},{64,0},{1,65},{65,1},{2,66},{66,2},{3,67},{67,3},{4,68},{68... | collective-permute-start | bytes 2359304 | tf_op jit(solution)/shard_map/ppermute | solution.py:194
  79.9 35.5 %copy-start.3 = (bf16[8,16,2048]{2,1,0:T(8,128)(2,1)S(1)}, bf16[8,16,2048]{2,1,0:T(8,128)(2,1)}, u32[]{:S(2)}) copy-start(bf16[8,16,2048]{2,1,0:T(8,128)(2,1)} %param.18) | copy-start | bytes 1572868
  79.9 35.5 %copy-start.7 = (f32[2048]{0:T(1024)S(1)}, f32[2048]{0:T(1024)}, u32[]{:S(2)}) copy-start(f32[2048]{0:T(1024)} %param.17) | copy-start | bytes 24580
  81.0 34.4 %collective-permute-start.6 = (bf16[2048,512]{1,0:T(8,128)(2,1)S(1)}, bf16[2048,512]{1,0:T(8,128)(2,1)S(1)}, u32[]{:S(2)}, u32[]{:S(2)}) collective-permute-start(bf16[2048,512]{1,0:T(8,128)(2,1)S(1)} %bitcast.16), channel_id=1, source_target_pairs={{0,64},{64,0},{1,65},{65,1},{2,66},{66,2},{3,67},{67,3},{4,68},{68... | collective-permute-start | bytes 6291464 | tf_op jit(solution)/shard_map/ppermute | solution.py:194

commit v6 on v5

--- a/solution.py
+++ b/solution.py
@@ -87,30 +87,44 @@
     return gate, up, down
 
 
-def grad_kernel(place_ref, mine, theirs, held, o0, o1, o2, o3, g0, g1, g2, fetched, sem):
-    gate, up, down = halves(held)
+def grad_kernel(
+    place_ref, mine, theirs, held, o0, o1, o2, o3, g0, g1, g2, keys, values, bg, bu, hid, sems
+):
     chips, _, width = held.shape
     part = width // (2 * chips)
     half = width // 2
     tokens = width
-    found = []
-    copy = pltpu.make_async_copy(theirs, fetched, sem)
-    copy.start()
-    for rows in (mine, fetched):
-        if rows is fetched:
-            copy.wait()
-        k, scaled = rows[:tokens, :], rows[tokens:, :]
+    copies = [
+        pltpu.make_async_copy(
+            source.at[pl.ds(j * tokens, tokens), :],
+            target.at[pl.ds(i * tokens, tokens), :],
+            sems.at[i, j],
+        )
+        for i, source in enumerate((mine, theirs))
+        for j, target in enumerate((keys, values))
+    ]
+    for copy in copies:
+        copy.start()
+    gate, up, down = halves(held)
+    for i in range(2):
+        if i:
+            for copy in copies:
+                copy.wait()
+            k, scaled = keys[tokens:, :], values[tokens:, :]
+        else:
+            k, scaled = mine[:tokens, :], mine[tokens:, :]
         pre_gate = dot(k, gate, 1, 1)
         pre_up = dot(k, up, 1, 1)
         back = dot(scaled, down, 1, 0)
         sig = jax.nn.sigmoid(pre_gate)
         act = pre_gate * sig
-        hidden = (act * pre_up).astype(BF)
-        back_gate = (back * pre_up * sig * (1.0 + pre_gate * (1.0 - sig))).astype(BF)
-        back_up = (back * act).astype(BF)
-        found.append((dot(back_gate, k, 0, 0), dot(back_up, k, 0, 0), dot(scaled, hidden, 0, 0)))
-    for g, one, two in zip((g0, g1, g2), *found):
-        g[...] = (one + two).astype(BF)
+        span = slice(i * tokens, (i + 1) * tokens)
+        hid[span, :] = (act * pre_up).astype(BF)
+        bg[span, :] = (back * pre_up * sig * (1.0 + pre_gate * (1.0 - sig))).astype(BF)
+        bu[span, :] = (back * act).astype(BF)
+    g0[...] = dot(bg[...], keys[...], 0, 0).astype(BF)
+    g1[...] = dot(bu[...], keys[...], 0, 0).astype(BF)
+    g2[...] = dot(values[...], hid[...], 0, 0).astype(BF)
     for r, out in enumerate((o0, o1, o2, o3)):
         x = lax.rem(place_ref[1] + r, chips)
         spot = pl.multiple_of(x * part, part)
@@ -252,7 +266,11 @@
             pltpu.VMEM((width // 2, width), BF),
             pltpu.VMEM((width, width // 2), BF),
             pltpu.VMEM((2 * tokens, width), BF),
-            pltpu.SemaphoreType.DMA,
+            pltpu.VMEM((2 * tokens, width), BF),
+            pltpu.VMEM((2 * tokens, width // 2), BF),
+            pltpu.VMEM((2 * tokens, width // 2), BF),
+            pltpu.VMEM((2 * tokens, width // 2), BF),
+            pltpu.SemaphoreType.DMA((2, 2)),
         ],
         compiler_params=PARAMS,
         name="grads",

time: 119 us -> 119 us (level)
  no operation moved by 1% of the time
where the time goes in v6:
time: 119 us; the launch traced here: 118 us
  blocking collectives  60.6 us (51%)
  starting transfers between devices  35.5 us (30%)
  Pallas kernels  11.5 us (10%)
  waiting for transfers between devices  7.9 us (7%)
  local copies, waits for them, and re-layouts  2.47 us (2%)
    all_to_all x1, blocking collectives, body(): lax.all_to_all(blocks, 'hs', split_axis=0, concat_axis=0, tiled=True)  32.4 us
    all_to_all x1, starting transfers between devices, body(): lax.all_to_all(pieces, 'hs', split_axis=0, concat_axis=0, tiled=True)  16.7 us
    all_gather x1, blocking collectives, body(): own = lax.all_gather(new, 'x', axis=0, tiled=False)  14.2 us
    all_gather x1, blocking collectives, body(): held = lax.all_gather(weights, 'x', axis=0, tiled=False)  14 us
    ppermute x3, starting transfers between devices, body(): lax.ppermute(a, 'x', [(x, (x + r) % chips) for x in range(chips)])  10.2 us
    ppermute x4, starting transfers between devices, swap(): return lax.ppermute(a, 'core', [(0, 1), (1, 0)])  8.55 us
    ppermute x3, waiting for transfers between devices, body(): lax.ppermute(a, 'x', [(x, (x + r) % chips) for x in range(chips)])  5.63 us
    pallas_call x1, Pallas kernels, body(): pl.pallas_call(grad_kernel, out_shape=(jax.ShapeDtypeStruct((rows, width)...  4.4 us
  transfers between devices with their start and end apart: 8, of which 4 were waited for; matrix products, arithmetic and copies ran while one was open for 0% of the time, Pallas kernels for 7%

profile of v6, /device:TPU:8, one launch (start us, length us, event | category | flops | bytes accessed | tf_op | source)
XLA Modules:
  0.0 118.2 jit_solution(11150175516808288316)
XLA Ops:
  0.0 0.0 copy-start
  0.0 0.8 copy-done
  0.8 1.6 %broadcast_in_dim.3 = bf16[64,32,512]{2,1,0:T(8,128)(2,1)} broadcast(bf16[32,512]{1,0:T(8,128)(2,1)S(1)} %constant_dynamic-slice_fusion), dimensions={1,2} | broadcast | bytes 2129920 | tf_op jit(solution)/shard_map/broadcast_in_dim | solution.py:246
  2.4 16.7 %all-to-all-start = ((bf16[64,32,512]{2,1,0:T(8,128)(2,1)}), bf16[64,32,512]{2,1,0:T(8,128)(2,1)S(1)}, u32[]{:S(2)}, u32[]{:S(2)}) async-start(bf16[64,32,512]{2,1,0:T(8,128)(2,1)} %broadcast_in_dim.3), calls=%async_computation | async-start | bytes 4194304 | tf_op jit(solution)/shard_map/all_to_all | solution.py:247
  19.2 0.0 copy-start.4
  19.2 0.0 copy-start.5
  19.2 0.0 copy-done.6
  19.2 2.1 %collective-permute-start = (bf16[64,512]{1,0:T(8,128)(2,1)S(1)}, bf16[64,512]{1,0:T(8,128)(2,1)S(1)}, u32[]{:S(2)}, u32[]{:S(2)}) collective-permute-start(bf16[64,512]{1,0:T(8,128)(2,1)S(1)} %bitcast.28), channel_id=1, source_target_pairs={{0,64},{64,0},{1,65},{65,1},{2,66},{66,2},{3,67},{67,3},{4,68},{68... | collective-permute-start | bytes 196616 | tf_op jit(solution)/shard_map/ppermute | solution.py:208
  21.3 2.2 %pack.1.mine = bf16[1024,512]{1,0:T(8,128)(2,1)} custom-call(bf16[512,512]{1,0:T(8,128)(2,1)} %bitcast.31, bf16[512,512]{1,0:T(8,128)(2,1)} %bitcast.32, f32[1,512]{1,0:T(1,128)} %rate.1), custom_call_target="tpu_custom_call" | custom-call | tf_op jit(solution)/shard_map/pack/pallas_call | solution.py:228
  23.5 0.0 collective-permute-done.other
  23.5 2.5 %collective-permute-start.1 = (bf16[1024,512]{1,0:T(8,128)(2,1)}, bf16[1024,512]{1,0:T(8,128)(2,1)}, u32[]{:S(2)}, u32[]{:S(2)}) collective-permute-start(bf16[1024,512]{1,0:T(8,128)(2,1)} %pack.1.mine), channel_id=1, source_target_pairs={{0,64},{64,0},{1,65},{65,1},{2,66},{66,2},{3,67},{67,3},{4,68},{68... | collective-permute-start | bytes 3145736 | tf_op jit(solution)/shard_map/ppermute | solution.py:208
  26.0 0.1 pad_add_fusion.place_ref.core_ref
  26.1 0.8 choose.1.weight
  26.9 14.0 %all-gather = bf16[832,512]{1,0:T(8,128)(2,1)S(1)} all-gather(bf16[208,512]{1,0:T(8,128)(2,1)S(1)} %choose.1.weight), channel_id=2, replica_groups=mesh['x'=4,'core'=2,'hs'=64] {'x'}, dimensions={0}, use_global_device_ids=true | all-gather | bytes 1064960 | tf_op jit(solution)/shard_map/all_gather | solution.py:258
  40.9 0.0 collective-permute-done.1.theirs
  40.9 4.4 %grads.1 = (bf16[192,512]{1,0:T(8,128)(2,1)S(1)}, bf16[192,512]{1,0:T(8,128)(2,1)S(1)}, bf16[192,512]{1,0:T(8,128)(2,1)S(1)}, bf16[192,512]{1,0:T(8,128)(2,1)S(1)}) custom-call(s32[2]{0:T(128)S(1)} %pad_add_fusion.place_ref.core_ref, bf16[1024,512]{1,0:T(8,128)(2,1)S(1)} %copy-done.1, bf16[1024,512]{1,0:T(8,128)(2,1)} %collective-permute-done.1.theirs, ...), custom_call_target="tpu_custom_call" | custom-call | tf_op jit(solution)/shard_map/grads/pallas_call | solution.py:259
  45.3 3.7 %collective-permute-start.2 = (bf16[192,512]{1,0:T(8,128)(2,1)S(1)}, bf16[192,512]{1,0:T(8,128)(2,1)S(1)}, u32[]{:S(2)}, u32[]{:S(2)}) collective-permute-start(bf16[192,512]{1,0:T(8,128)(2,1)S(1)} %get-tuple-element.16), channel_id=1, source_target_pairs={{0,128},{128,256},{256,384},{384,0},{1,129},{129,257},{257,385},{3... | collective-permute-start | bytes 589832 | tf_op jit(solution)/shard_map/ppermute | solution.py:279
  49.0 4.6 %collective-permute-start.3 = (bf16[192,512]{1,0:T(8,128)(2,1)S(1)}, bf16[192,512]{1,0:T(8,128)(2,1)S(1)}, u32[]{:S(2)}, u32[]{:S(2)}) collective-permute-start(bf16[192,512]{1,0:T(8,128)(2,1)S(1)} %get-tuple-element.17), channel_id=1, source_target_pairs={{0,256},{128,384},{256,0},{384,128},{1,257},{129,385},{257,1},{385... | collective-permute-start | bytes 589832 | tf_op jit(solution)/shard_map/ppermute | solution.py:279
  53.6 1.9 %collective-permute-start.4 = (bf16[192,512]{1,0:T(8,128)(2,1)S(1)}, bf16[192,512]{1,0:T(8,128)(2,1)S(1)}, u32[]{:S(2)}, u32[]{:S(2)}) collective-permute-start(bf16[192,512]{1,0:T(8,128)(2,1)S(1)} %get-tuple-element.18), channel_id=1, source_target_pairs={{0,384},{128,0},{256,128},{384,256},{1,385},{129,1},{257,129},{385... | collective-permute-start | bytes 589832 | tf_op jit(solution)/shard_map/ppermute | solution.py:279
  55.6 0.6 collective-permute-done.2.p1
  56.2 2.3 %collective-permute-done.3.p2 = bf16[192,512]{1,0:T(8,128)(2,1)S(1)} collective-permute-done((bf16[192,512]{1,0:T(8,128)(2,1)S(1)}, bf16[192,512]{1,0:T(8,128)(2,1)S(1)}, u32[]{:S(2)}, u32[]{:S(2)}) %collective-permute-start.3) | collective-permute-done | bytes 196640 | tf_op jit(solution)/shard_map/ppermute | solution.py:279
  58.5 2.7 %collective-permute-done.4.p3 = bf16[192,512]{1,0:T(8,128)(2,1)S(1)} collective-permute-done((bf16[192,512]{1,0:T(8,128)(2,1)S(1)}, bf16[192,512]{1,0:T(8,128)(2,1)S(1)}, u32[]{:S(2)}, u32[]{:S(2)}) %collective-permute-start.4) | collective-permute-done | bytes 196640 | tf_op jit(solution)/shard_map/ppermute | solution.py:279
  61.2 0.2 rescale.1
  61.4 14.2 %all-gather.1 = bf16[768,512]{1,0:T(8,128)(2,1)S(1)} all-gather(bf16[192,512]{1,0:T(8,128)(2,1)S(1)} %rescale.1), channel_id=3, replica_groups=mesh['x'=4,'core'=2,'hs'=64] {'x'}, dimensions={0}, use_global_device_ids=true | all-gather | bytes 983040 | tf_op jit(solution)/shard_map/all_gather | solution.py:290
  75.7 1.9 %collective-permute-start.5 = (bf16[4,192,512]{2,1,0:T(8,128)(2,1)S(1)}, bf16[4,192,512]{2,1,0:T(8,128)(2,1)S(1)}, u32[]{:S(2)}, u32[]{:S(2)}) collective-permute-start(bf16[4,192,512]{2,1,0:T(8,128)(2,1)S(1)} %bitcast.20), channel_id=1, source_target_pairs={{0,64},{64,0},{1,65},{65,1},{2,66},{66,2},{3,67},{67,3},{4,68},{68... | collective-permute-start | bytes 2359304 | tf_op jit(solution)/shard_map/ppermute | solution.py:208
  77.6 2.3 %collective-permute-done.5.other = bf16[4,192,512]{2,1,0:T(8,128)(2,1)S(1)} collective-permute-done((bf16[4,192,512]{2,1,0:T(8,128)(2,1)S(1)}, bf16[4,192,512]{2,1,0:T(8,128)(2,1)S(1)}, u32[]{:S(2)}, u32[]{:S(2)}) %collective-permute-start.5) | collective-permute-done | bytes 786464 | tf_op jit(solution)/shard_map/ppermute | solution.py:208
  79.8 1.0 query.1
  80.9 0.0 all-to-all-done
  80.9 2.0 %collective-permute-start.6 = (bf16[2048,512]{1,0:T(8,128)(2,1)S(1)}, bf16[2048,512]{1,0:T(8,128)(2,1)S(1)}, u32[]{:S(2)}, u32[]{:S(2)}) collective-permute-start(bf16[2048,512]{1,0:T(8,128)(2,1)S(1)} %bitcast.16), channel_id=1, source_target_pairs={{0,64},{64,0},{1,65},{65,1},{2,66},{66,2},{3,67},{67,3},{4,68},{68... | collective-permute-start | bytes 6291464 | tf_op jit(solution)/shard_map/ppermute | solution.py:208
  82.9 32.4 %all_to_all.10 = bf16[64,8,512]{2,1,0:T(8,128)(2,1)S(1)} all-to-all(bf16[64,8,512]{2,1,0:T(8,128)(2,1)S(1)} %bitcast.22), channel_id=1, replica_groups=mesh['x'=4,'core'=2,'hs'=64] {'hs'}, dimensions={0} | all-to-all | bytes 1048576 | tf_op jit(solution)/shard_map/all_to_all | solution.py:303
  115.3 0.0 collective-permute-done.6.theirs
  115.3 2.9 %project.1 = bf16[128,1024]{1,0:T(8,128)(2,1)} custom-call(s32[2]{0:T(128)S(1)} %pad_add_fusion.place_ref.core_ref, bf16[512,512]{1,0:T(8,128)(2,1)S(1)} %bitcast.23, f32[1,2048]{1,0:T(1,128)S(1)} %bitcast.30, bf16[128,2048]{1,0:T(8,128)(2,1)S(1)} %bitcast.25, bf16[2048,512]{1,0:T(8,128)(2,1)S(1)} %bitcast.17, ...), custom_call_target="tpu_custom_call" | custom-call | tf_op jit(solution)/shard_map/project/pallas_call | solution.py:307
  (12 shorter events, 0.0 us)
Async XLA Ops:
  0.0 0.8 copy-start
  2.4 16.7 %copy-start.6 = (bf16[1,64,512]{2,1,0:T(8,128)(2,1)S(1)}, bf16[1,64,512]{2,1,0:T(8,128)(2,1)}, u32[]{:S(2)}) copy-start(bf16[1,64,512]{2,1,0:T(8,128)(2,1)} %param.16) | copy-start | bytes 196612
  2.4 78.4 %all-to-all-start = ((bf16[64,32,512]{2,1,0:T(8,128)(2,1)}), bf16[64,32,512]{2,1,0:T(8,128)(2,1)S(1)}, u32[]{:S(2)}, u32[]{:S(2)}) async-start(bf16[64,32,512]{2,1,0:T(8,128)(2,1)} %broadcast_in_dim.3), calls=%async_computation | async-start | bytes 4194304 | tf_op jit(solution)/shard_map/all_to_all | solution.py:247
  19.2 7.0 %copy-start.4 = (bf16[1,64,512]{2,1,0:T(8,128)(2,1)S(1)}, bf16[1,64,512]{2,1,0:T(8,128)(2,1)}, u32[]{:S(2)}) copy-start(bf16[1,64,512]{2,1,0:T(8,128)(2,1)} %param.14) | copy-start | bytes 196612
  19.2 6.9 %copy-start.5 = (bf16[1,64,512]{2,1,0:T(8,128)(2,1)S(1)}, bf16[1,64,512]{2,1,0:T(8,128)(2,1)}, u32[]{:S(2)}) copy-start(bf16[1,64,512]{2,1,0:T(8,128)(2,1)} %param.15) | copy-start | bytes 196612
  19.2 4.3 %collective-permute-start = (bf16[64,512]{1,0:T(8,128)(2,1)S(1)}, bf16[64,512]{1,0:T(8,128)(2,1)S(1)}, u32[]{:S(2)}, u32[]{:S(2)}) collective-permute-start(bf16[64,512]{1,0:T(8,128)(2,1)S(1)} %bitcast.28), channel_id=1, source_target_pairs={{0,64},{64,0},{1,65},{65,1},{2,66},{66,2},{3,67},{67,3},{4,68},{68... | collective-permute-start | bytes 196616 | tf_op jit(solution)/shard_map/ppermute | solution.py:208
  23.5 17.4 %copy-start.1 = (bf16[1024,512]{1,0:T(8,128)(2,1)S(1)}, bf16[1024,512]{1,0:T(8,128)(2,1)}, u32[]{:S(2)}) copy-start(bf16[1024,512]{1,0:T(8,128)(2,1)} %pack.1.mine) | copy-start | bytes 3145732
  23.5 17.4 %collective-permute-start.1 = (bf16[1024,512]{1,0:T(8,128)(2,1)}, bf16[1024,512]{1,0:T(8,128)(2,1)}, u32[]{:S(2)}, u32[]{:S(2)}) collective-permute-start(bf16[1024,512]{1,0:T(8,128)(2,1)} %pack.1.mine), channel_id=1, source_target_pairs={{0,64},{64,0},{1,65},{65,1},{2,66},{66,2},{3,67},{67,3},{4,68},{68... | collective-permute-start | bytes 3145736 | tf_op jit(solution)/shard_map/ppermute | solution.py:208
  40.9 39.0 %copy-start.2 = (bf16[1,512,512]{2,1,0:T(8,128)(2,1)S(1)}, bf16[1,512,512]{2,1,0:T(8,128)(2,1)}, u32[]{:S(2)}) copy-start(bf16[1,512,512]{2,1,0:T(8,128)(2,1)} %param.12) | copy-start | bytes 1572868
  45.3 10.9 %collective-permute-start.2 = (bf16[192,512]{1,0:T(8,128)(2,1)S(1)}, bf16[192,512]{1,0:T(8,128)(2,1)S(1)}, u32[]{:S(2)}, u32[]{:S(2)}) collective-permute-start(bf16[192,512]{1,0:T(8,128)(2,1)S(1)} %get-tuple-element.16), channel_id=1, source_target_pairs={{0,128},{128,256},{256,384},{384,0},{1,129},{129,257},{257,385},{3... | collective-permute-start | bytes 589832 | tf_op jit(solution)/shard_map/ppermute | solution.py:279
  49.0 9.5 %collective-permute-start.3 = (bf16[192,512]{1,0:T(8,128)(2,1)S(1)}, bf16[192,512]{1,0:T(8,128)(2,1)S(1)}, u32[]{:S(2)}, u32[]{:S(2)}) collective-permute-start(bf16[192,512]{1,0:T(8,128)(2,1)S(1)} %get-tuple-element.17), channel_id=1, source_target_pairs={{0,256},{128,384},{256,0},{384,128},{1,257},{129,385},{257,1},{385... | collective-permute-start | bytes 589832 | tf_op jit(solution)/shard_map/ppermute | solution.py:279
  53.6 7.6 %collective-permute-start.4 = (bf16[192,512]{1,0:T(8,128)(2,1)S(1)}, bf16[192,512]{1,0:T(8,128)(2,1)S(1)}, u32[]{:S(2)}, u32[]{:S(2)}) collective-permute-start(bf16[192,512]{1,0:T(8,128)(2,1)S(1)} %get-tuple-element.18), channel_id=1, source_target_pairs={{0,384},{128,0},{256,128},{384,256},{1,385},{129,1},{257,129},{385... | collective-permute-start | bytes 589832 | tf_op jit(solution)/shard_map/ppermute | solution.py:279
  75.7 4.2 %collective-permute-start.5 = (bf16[4,192,512]{2,1,0:T(8,128)(2,1)S(1)}, bf16[4,192,512]{2,1,0:T(8,128)(2,1)S(1)}, u32[]{:S(2)}, u32[]{:S(2)}) collective-permute-start(bf16[4,192,512]{2,1,0:T(8,128)(2,1)S(1)} %bitcast.20), channel_id=1, source_target_pairs={{0,64},{64,0},{1,65},{65,1},{2,66},{66,2},{3,67},{67,3},{4,68},{68... | collective-permute-start | bytes 2359304 | tf_op jit(solution)/shard_map/ppermute | solution.py:208
  79.8 35.5 %copy-start.3 = (bf16[8,16,2048]{2,1,0:T(8,128)(2,1)S(1)}, bf16[8,16,2048]{2,1,0:T(8,128)(2,1)}, u32[]{:S(2)}) copy-start(bf16[8,16,2048]{2,1,0:T(8,128)(2,1)} %param.18) | copy-start | bytes 1572868
  79.8 35.5 %copy-start.7 = (f32[2048]{0:T(1024)S(1)}, f32[2048]{0:T(1024)}, u32[]{:S(2)}) copy-start(f32[2048]{0:T(1024)} %param.17) | copy-start | bytes 24580
  80.9 34.4 %collective-permute-start.6 = (bf16[2048,512]{1,0:T(8,128)(2,1)S(1)}, bf16[2048,512]{1,0:T(8,128)(2,1)S(1)}, u32[]{:S(2)}, u32[]{:S(2)}) collective-permute-start(bf16[2048,512]{1,0:T(8,128)(2,1)S(1)} %bitcast.16), channel_id=1, source_target_pairs={{0,64},{64,0},{1,65},{65,1},{2,66},{66,2},{3,67},{67,3},{4,68},{68... | collective-permute-start | bytes 6291464 | tf_op jit(solution)/shard_map/ppermute | solution.py:208

commit v7 on v6

--- a/solution.py
+++ b/solution.py
@@ -21,14 +21,31 @@
     return lax.dot_general(left, right, (((a,), (b,)), ((), ())), preferred_element_type=F32)
 
 
-def pack_kernel(key, value, rate, out, value_buf, rate_buf, sems):
+def pack_kernel(
+    place_ref, key, value, rate, down, weight, out, pieces, value_buf, rate_buf, repeated, sems, more
+):
     tokens, width = key.shape
+    part = down.shape[0]
     copies = [
         pltpu.make_async_copy(rate, rate_buf, sems.at[0]),
         pltpu.make_async_copy(value, value_buf, sems.at[1]),
         pltpu.make_async_copy(key, out.at[pl.ds(0, tokens), :], sems.at[2]),
+        pltpu.make_async_copy(down, out.at[pl.ds(2 * tokens, part), :], sems.at[3]),
     ]
+    few, _, half = repeated.shape
+    start = pl.multiple_of(place_ref[0] * half, half)
+    fetch = pltpu.make_async_copy(weight.at[:, pl.ds(start, half)], repeated.at[0], sems.at[4])
+    fetch.start()
     for copy in copies:
+        copy.start()
+    fetch.wait()
+    for i in range(1, few):
+        repeated[i] = repeated[0]
+    outs = [
+        pltpu.make_async_copy(repeated, pieces.at[pl.ds(i * few, few)], more.at[i])
+        for i in range(pieces.shape[0] // few)
+    ]
+    for copy in outs:
         copy.start()
     copies[0].wait()
     column = jnp.transpose(jnp.broadcast_to(rate_buf[...], (128, tokens)))
@@ -37,6 +54,13 @@
         jnp.concatenate([column] * (width // 128), axis=1) * value_buf[...].astype(F32)
     ).astype(BF)
     copies[2].wait()
+    copies[3].wait()
+    for copy in outs:
+        copy.wait()
+
+
+def tail_kernel(rows, out):
+    out[...] = rows[rows.shape[0] - out.shape[0] :, :]
 
 
 def choose_kernel(place_ref, gate, up, down, other, out):
@@ -112,7 +136,7 @@
                 copy.wait()
             k, scaled = keys[tokens:, :], values[tokens:, :]
         else:
-            k, scaled = mine[:tokens, :], mine[tokens:, :]
+            k, scaled = mine[:tokens, :], mine[tokens : 2 * tokens, :]
         pre_gate = dot(k, gate, 1, 1)
         pre_up = dot(k, up, 1, 1)
         back = dot(scaled, down, 1, 0)
@@ -225,25 +249,37 @@
     tokens, width = key_rows.shape[1:]
     part = fast_gate.shape[1]
     rows = 3 * part
-    mine = pl.pallas_call(
+    count = lax.axis_size("hs")
+    depth, half = out_weight.shape[0], out_weight.shape[1] // 2
+    few = 8
+    mine, pieces = pl.pallas_call(
         pack_kernel,
-        out_shape=jax.ShapeDtypeStruct((2 * tokens, width), BF),
-        in_specs=[HBM] * 3,
-        out_specs=VMEM,
+        out_shape=(
+            jax.ShapeDtypeStruct((2 * tokens + part, width), BF),
+            jax.ShapeDtypeStruct((count, depth, half), BF),
+        ),
+        in_specs=[SMEM] + [HBM] * 5,
+        out_specs=(VMEM, HBM),
         scratch_shapes=[
             pltpu.VMEM((tokens, width), BF),
             pltpu.VMEM((1, tokens), F32),
-            pltpu.SemaphoreType.DMA((3,)),
+            pltpu.VMEM((few, depth, half), BF),
+            pltpu.SemaphoreType.DMA((5,)),
+            pltpu.SemaphoreType.DMA((count // few,)),
         ],
         compiler_params=pltpu.CompilerParams(vmem_limit_bytes=60 * 1024 * 1024),
         name="pack",
-    )(key_rows[0], value_rows[0], step_rates)
-    mine, other_down = pin((mine, swap(fast_down[0])))
+    )(place, key_rows[0], value_rows[0], step_rates, fast_down[0], out_weight)
     theirs = swap(mine)
-    count = lax.axis_size("hs")
-    depth, half = out_weight.shape[0], out_weight.shape[1] // 2
-    piece = lax.dynamic_slice_in_dim(out_weight, place[0] * half, half, 1)
-    pieces = jnp.broadcast_to(piece, (count, depth, half))
+    tail = pl.pallas_call(
+        tail_kernel,
+        out_shape=jax.ShapeDtypeStruct((part, width), BF),
+        in_specs=[VMEM],
+        out_specs=VMEM,
+        compiler_params=PARAMS,
+        name="tail",
+    )(theirs)
+    pieces, theirs, tail = pin((pieces, theirs, tail))
     left = lax.all_to_all(pieces, "hs", split_axis=0, concat_axis=0, tiled=True).reshape(
         count * depth, half
     )
@@ -254,7 +290,7 @@
         out_specs=VMEM,
         compiler_params=PARAMS,
         name="choose",
-    )(place, fast_gate[0], fast_up[0], fast_down[0], other_down)
+    )(place, fast_gate[0], fast_up[0], fast_down[0], tail)
     held = lax.all_gather(weights, "x", axis=0, tiled=False)
     sums = pl.pallas_call(
         grad_kernel,

time: 119 us -> 117 us (0.983)
  waiting for transfers between devices: 7.9 us -> 10.8 us
  starting transfers between devices: 35.5 us -> 33 us
  local copies, waits for them, and re-layouts: 2.47 us -> 0.04 us
    ppermute x4 -> x3, waiting for transfers between devices: 2.26 us -> 5.18 us  [swap(): return lax.ppermute(a, 'core', [(0, 1), (1, 0)])]
    ppermute x4 -> x3, starting transfers between devices: 8.55 us -> 5.88 us  [swap(): return lax.ppermute(a, 'core', [(0, 1), (1, 0)])]
    pallas_call x1 -> x2, Pallas kernels: 2.2 us -> 3.89 us  [the longest x1 3.89 us: body(): pl.pallas_call(pack_kernel, out_shape=(jax.ShapeDtypeStruct((2 * tokens +...]
    broadcast_in_dim x1 -> x0, local copies, waits for them, and re-layouts: 1.6 us -> none  [body(): pieces = jnp.broadcast_to(piece, (count, depth, half))]
  transfers between devices with their start and end apart: 8 -> 7, of which waited for: 4 -> 5; matrix products, arithmetic and copies ran while one was open for 0% -> 0% of each run, Pallas kernels for 7% -> 5%
where the time goes in v7:
time: 117 us
  blocking collectives  60 us (51%)
  starting transfers between devices  33 us (28%)
  Pallas kernels  12.2 us (10%)
  waiting for transfers between devices  10.8 us (9%)
    all_to_all x1, blocking collectives, body(): lax.all_to_all(blocks, 'hs', split_axis=0, concat_axis=0, tiled=True)  32.1 us
    all_to_all x1, starting transfers between devices, body(): lax.all_to_all(pieces, 'hs', split_axis=0, concat_axis=0, tiled=True)  16.7 us
    all_gather x1, blocking collectives, body(): own = lax.all_gather(new, 'x', axis=0, tiled=False)  14.2 us
    all_gather x1, blocking collectives, body(): held = lax.all_gather(weights, 'x', axis=0, tiled=False)  13.8 us
    ppermute x3, starting transfers between devices, body(): lax.ppermute(a, 'x', [(x, (x + r) % chips) for x in range(chips)])  10.4 us
    ppermute x3, starting transfers between devices, swap(): return lax.ppermute(a, 'core', [(0, 1), (1, 0)])  5.88 us
    ppermute x3, waiting for transfers between devices, body(): lax.ppermute(a, 'x', [(x, (x + r) % chips) for x in range(chips)])  5.63 us
    ppermute x3, waiting for transfers between devices, swap(): return lax.ppermute(a, 'core', [(0, 1), (1, 0)])  5.18 us
  transfers between devices with their start and end apart: 7, of which 5 were waited for; matrix products, arithmetic and copies ran while one was open for 0% of the time, Pallas kernels for 5%

profile of v7, /device:TPU:8, one launch (start us, length us, event | category | flops | bytes accessed | tf_op | source)
XLA Modules:
  0.0 117.0 jit_solution(16861574969798086204)
XLA Ops:
  0.0 0.7 pad_add_fusion.place_ref.core_ref
  0.7 3.9 %pack.1 = (bf16[1088,512]{1,0:T(8,128)(2,1)}, bf16[64,32,512]{2,1,0:T(8,128)(2,1)}) custom-call(s32[2]{0:T(128)} %pad_add_fusion.place_ref.core_ref, bf16[512,512]{1,0:T(8,128)(2,1)} %bitcast.31, bf16[512,512]{1,0:T(8,128)(2,1)} %bitcast.32, f32[1,512]{1,0:T(1,128)} %rate.1, bf16[64,512]{1,0:T(8,128)(2,1)} %bitcast.26, bf16[32,1024]{1,0:T(8,128)(2,1)} %weight.1), custom_call_target="tpu_custom_call" | custom-call | tf_op jit(solution)/shard_map/pack/pallas_call | solution.py:255
  4.5 1.9 %collective-permute-start = (bf16[1088,512]{1,0:T(8,128)(2,1)}, bf16[1088,512]{1,0:T(8,128)(2,1)S(1)}, u32[]{:S(2)}, u32[]{:S(2)}) collective-permute-start(bf16[1088,512]{1,0:T(8,128)(2,1)} %get-tuple-element.17.mine), channel_id=1, source_target_pairs={{0,64},{64,0},{1,65},{65,1},{2,66},{66,2},{3,67},{67,3},{4,68},{68... | collective-permute-start | bytes 3342344 | tf_op jit(solution)/shard_map/ppermute | solution.py:232
  6.5 2.9 %collective-permute-done.rows.theirs = bf16[1088,512]{1,0:T(8,128)(2,1)S(1)} collective-permute-done((bf16[1088,512]{1,0:T(8,128)(2,1)}, bf16[1088,512]{1,0:T(8,128)(2,1)S(1)}, u32[]{:S(2)}, u32[]{:S(2)}) %collective-permute-start) | collective-permute-done | bytes 1114144 | tf_op jit(solution)/shard_map/ppermute | solution.py:232
  9.4 0.0 copy-start.4
  9.4 0.0 copy-start.5
  9.4 0.0 copy-start.7
  9.5 16.7 %all-to-all-start = ((bf16[64,32,512]{2,1,0:T(8,128)(2,1)}), bf16[64,32,512]{2,1,0:T(8,128)(2,1)S(1)}, u32[]{:S(2)}, u32[]{:S(2)}) async-start(bf16[64,32,512]{2,1,0:T(8,128)(2,1)} %get-tuple-element.24), calls=%async_computation | async-start | bytes 4194304 | tf_op jit(solution)/shard_map/all_to_all | solution.py:283
  26.2 0.0 copy-start
  26.2 0.0 copy-done.3
  26.2 0.0 copy-done.4
  26.2 0.0 copy-done.5
  26.2 0.8 choose.1.weight
  27.0 13.8 %all-gather = bf16[832,512]{1,0:T(8,128)(2,1)S(1)} all-gather(bf16[208,512]{1,0:T(8,128)(2,1)S(1)} %choose.1.weight), channel_id=2, replica_groups=mesh['x'=4,'core'=2,'hs'=64] {'x'}, dimensions={0}, use_global_device_ids=true | all-gather | bytes 1064960 | tf_op jit(solution)/shard_map/all_gather | solution.py:294
  40.8 3.4 %grads.1 = (bf16[192,512]{1,0:T(8,128)(2,1)S(1)}, bf16[192,512]{1,0:T(8,128)(2,1)S(1)}, bf16[192,512]{1,0:T(8,128)(2,1)S(1)}, bf16[192,512]{1,0:T(8,128)(2,1)S(1)}) custom-call(s32[2]{0:T(128)S(1)} %copy-done.7, bf16[1088,512]{1,0:T(8,128)(2,1)S(1)} %copy-done, bf16[1088,512]{1,0:T(8,128)(2,1)S(1)} %collective-permute-done.rows.theirs, ...), custom_call_target="tpu_custom_call" | custom-call | tf_op jit(solution)/shard_map/grads/pallas_call | solution.py:295
  44.2 3.9 %collective-permute-start.1 = (bf16[192,512]{1,0:T(8,128)(2,1)S(1)}, bf16[192,512]{1,0:T(8,128)(2,1)S(1)}, u32[]{:S(2)}, u32[]{:S(2)}) collective-permute-start(bf16[192,512]{1,0:T(8,128)(2,1)S(1)} %get-tuple-element.21), channel_id=1, source_target_pairs={{0,128},{128,256},{256,384},{384,0},{1,129},{129,257},{257,385},{3... | collective-permute-start | bytes 589832 | tf_op jit(solution)/shard_map/ppermute | solution.py:315
  48.1 4.6 %collective-permute-start.2 = (bf16[192,512]{1,0:T(8,128)(2,1)S(1)}, bf16[192,512]{1,0:T(8,128)(2,1)S(1)}, u32[]{:S(2)}, u32[]{:S(2)}) collective-permute-start(bf16[192,512]{1,0:T(8,128)(2,1)S(1)} %get-tuple-element.22), channel_id=1, source_target_pairs={{0,256},{128,384},{256,0},{384,128},{1,257},{129,385},{257,1},{385... | collective-permute-start | bytes 589832 | tf_op jit(solution)/shard_map/ppermute | solution.py:315
  52.7 1.9 %collective-permute-start.3 = (bf16[192,512]{1,0:T(8,128)(2,1)S(1)}, bf16[192,512]{1,0:T(8,128)(2,1)S(1)}, u32[]{:S(2)}, u32[]{:S(2)}) collective-permute-start(bf16[192,512]{1,0:T(8,128)(2,1)S(1)} %get-tuple-element.23), channel_id=1, source_target_pairs={{0,384},{128,0},{256,128},{384,256},{1,385},{129,1},{257,129},{385... | collective-permute-start | bytes 589832 | tf_op jit(solution)/shard_map/ppermute | solution.py:315
  54.7 0.3 collective-permute-done.1.p1
  55.0 2.2 %collective-permute-done.2.p2 = bf16[192,512]{1,0:T(8,128)(2,1)S(1)} collective-permute-done((bf16[192,512]{1,0:T(8,128)(2,1)S(1)}, bf16[192,512]{1,0:T(8,128)(2,1)S(1)}, u32[]{:S(2)}, u32[]{:S(2)}) %collective-permute-start.2) | collective-permute-done | bytes 196640 | tf_op jit(solution)/shard_map/ppermute | solution.py:315
  57.2 3.1 %collective-permute-done.3.p3 = bf16[192,512]{1,0:T(8,128)(2,1)S(1)} collective-permute-done((bf16[192,512]{1,0:T(8,128)(2,1)S(1)}, bf16[192,512]{1,0:T(8,128)(2,1)S(1)}, u32[]{:S(2)}, u32[]{:S(2)}) %collective-permute-start.3) | collective-permute-done | bytes 196640 | tf_op jit(solution)/shard_map/ppermute | solution.py:315
  60.3 0.2 rescale.1
  60.5 14.2 %all-gather.1 = bf16[768,512]{1,0:T(8,128)(2,1)S(1)} all-gather(bf16[192,512]{1,0:T(8,128)(2,1)S(1)} %rescale.1), channel_id=3, replica_groups=mesh['x'=4,'core'=2,'hs'=64] {'x'}, dimensions={0}, use_global_device_ids=true | all-gather | bytes 983040 | tf_op jit(solution)/shard_map/all_gather | solution.py:326
  74.7 1.9 %collective-permute-start.4 = (bf16[4,192,512]{2,1,0:T(8,128)(2,1)S(1)}, bf16[4,192,512]{2,1,0:T(8,128)(2,1)S(1)}, u32[]{:S(2)}, u32[]{:S(2)}) collective-permute-start(bf16[4,192,512]{2,1,0:T(8,128)(2,1)S(1)} %bitcast.20), channel_id=1, source_target_pairs={{0,64},{64,0},{1,65},{65,1},{2,66},{66,2},{3,67},{67,3},{4,68},{68... | collective-permute-start | bytes 2359304 | tf_op jit(solution)/shard_map/ppermute | solution.py:232
  76.6 2.3 %collective-permute-done.4.other = bf16[4,192,512]{2,1,0:T(8,128)(2,1)S(1)} collective-permute-done((bf16[4,192,512]{2,1,0:T(8,128)(2,1)S(1)}, bf16[4,192,512]{2,1,0:T(8,128)(2,1)S(1)}, u32[]{:S(2)}, u32[]{:S(2)}) %collective-permute-start.4) | collective-permute-done | bytes 786464 | tf_op jit(solution)/shard_map/ppermute | solution.py:232
  78.9 1.0 query.1
  79.9 0.0 all-to-all-done
  79.9 2.0 %collective-permute-start.5 = (bf16[2048,512]{1,0:T(8,128)(2,1)S(1)}, bf16[2048,512]{1,0:T(8,128)(2,1)S(1)}, u32[]{:S(2)}, u32[]{:S(2)}) collective-permute-start(bf16[2048,512]{1,0:T(8,128)(2,1)S(1)} %bitcast.16), channel_id=1, source_target_pairs={{0,64},{64,0},{1,65},{65,1},{2,66},{66,2},{3,67},{67,3},{4,68},{68... | collective-permute-start | bytes 6291464 | tf_op jit(solution)/shard_map/ppermute | solution.py:232
  82.0 32.1 %all_to_all.10 = bf16[64,8,512]{2,1,0:T(8,128)(2,1)S(1)} all-to-all(bf16[64,8,512]{2,1,0:T(8,128)(2,1)S(1)} %bitcast.22), channel_id=1, replica_groups=mesh['x'=4,'core'=2,'hs'=64] {'hs'}, dimensions={0} | all-to-all | bytes 1048576 | tf_op jit(solution)/shard_map/all_to_all | solution.py:339
  114.0 0.0 collective-permute-done.5.theirs
  114.0 0.0 copy-done.2
  114.1 2.9 %project.1 = bf16[128,1024]{1,0:T(8,128)(2,1)} custom-call(s32[2]{0:T(128)S(1)} %copy-done.7, bf16[512,512]{1,0:T(8,128)(2,1)S(1)} %bitcast.23, f32[1,2048]{1,0:T(1,128)S(1)} %bitcast.30, bf16[128,2048]{1,0:T(8,128)(2,1)S(1)} %bitcast.25, bf16[2048,512]{1,0:T(8,128)(2,1)S(1)} %bitcast.17, bf16[2048,512]{1,0:T(8,128)(2,1)S(1)} %collective-permute-done.5.theirs), custom_call_target="tpu_custom_call" | custom-call | tf_op jit(solution)/shard_map/project/pallas_call | solution.py:343
  (9 shorter events, 0.0 us)
Async XLA Ops:
  4.5 4.9 %collective-permute-start = (bf16[1088,512]{1,0:T(8,128)(2,1)}, bf16[1088,512]{1,0:T(8,128)(2,1)S(1)}, u32[]{:S(2)}, u32[]{:S(2)}) collective-permute-start(bf16[1088,512]{1,0:T(8,128)(2,1)} %get-tuple-element.17.mine), channel_id=1, source_target_pairs={{0,64},{64,0},{1,65},{65,1},{2,66},{66,2},{3,67},{67,3},{4,68},{68... | collective-permute-start | bytes 3342344 | tf_op jit(solution)/shard_map/ppermute | solution.py:232
  9.4 16.8 %copy-start.3 = (bf16[1,64,512]{2,1,0:T(8,128)(2,1)S(1)}, bf16[1,64,512]{2,1,0:T(8,128)(2,1)}, u32[]{:S(2)}) copy-start(bf16[1,64,512]{2,1,0:T(8,128)(2,1)} %param.16) | copy-start | bytes 196612
  9.4 16.8 %copy-start.4 = (bf16[1,64,512]{2,1,0:T(8,128)(2,1)S(1)}, bf16[1,64,512]{2,1,0:T(8,128)(2,1)}, u32[]{:S(2)}) copy-start(bf16[1,64,512]{2,1,0:T(8,128)(2,1)} %param.14) | copy-start | bytes 196612
  9.4 16.8 %copy-start.5 = (bf16[1,64,512]{2,1,0:T(8,128)(2,1)S(1)}, bf16[1,64,512]{2,1,0:T(8,128)(2,1)}, u32[]{:S(2)}) copy-start(bf16[1,64,512]{2,1,0:T(8,128)(2,1)} %param.15) | copy-start | bytes 196612
  9.4 16.8 %copy-start.7 = (s32[2]{0:T(128)S(1)}, s32[2]{0:T(128)}, u32[]{:S(2)}) copy-start(s32[2]{0:T(128)} %pad_add_fusion.place_ref.core_ref) | copy-start | bytes 28
  9.5 70.5 %all-to-all-start = ((bf16[64,32,512]{2,1,0:T(8,128)(2,1)}), bf16[64,32,512]{2,1,0:T(8,128)(2,1)S(1)}, u32[]{:S(2)}, u32[]{:S(2)}) async-start(bf16[64,32,512]{2,1,0:T(8,128)(2,1)} %get-tuple-element.24), calls=%async_computation | async-start | bytes 4194304 | tf_op jit(solution)/shard_map/all_to_all | solution.py:283
  26.2 14.6 %copy-start = (bf16[1088,512]{1,0:T(8,128)(2,1)S(1)}, bf16[1088,512]{1,0:T(8,128)(2,1)}, u32[]{:S(2)}) copy-start(bf16[1088,512]{1,0:T(8,128)(2,1)} %get-tuple-element.17.mine) | copy-start | bytes 3342340
  40.8 38.1 %copy-start.1 = (bf16[1,512,512]{2,1,0:T(8,128)(2,1)S(1)}, bf16[1,512,512]{2,1,0:T(8,128)(2,1)}, u32[]{:S(2)}) copy-start(bf16[1,512,512]{2,1,0:T(8,128)(2,1)} %param.12) | copy-start | bytes 1572868
  44.2 10.7 %collective-permute-start.1 = (bf16[192,512]{1,0:T(8,128)(2,1)S(1)}, bf16[192,512]{1,0:T(8,128)(2,1)S(1)}, u32[]{:S(2)}, u32[]{:S(2)}) collective-permute-start(bf16[192,512]{1,0:T(8,128)(2,1)S(1)} %get-tuple-element.21), channel_id=1, source_target_pairs={{0,128},{128,256},{256,384},{384,0},{1,129},{129,257},{257,385},{3... | collective-permute-start | bytes 589832 | tf_op jit(solution)/shard_map/ppermute | solution.py:315
  48.1 9.1 %collective-permute-start.2 = (bf16[192,512]{1,0:T(8,128)(2,1)S(1)}, bf16[192,512]{1,0:T(8,128)(2,1)S(1)}, u32[]{:S(2)}, u32[]{:S(2)}) collective-permute-start(bf16[192,512]{1,0:T(8,128)(2,1)S(1)} %get-tuple-element.22), channel_id=1, source_target_pairs={{0,256},{128,384},{256,0},{384,128},{1,257},{129,385},{257,1},{385... | collective-permute-start | bytes 589832 | tf_op jit(solution)/shard_map/ppermute | solution.py:315
  52.7 7.6 %collective-permute-start.3 = (bf16[192,512]{1,0:T(8,128)(2,1)S(1)}, bf16[192,512]{1,0:T(8,128)(2,1)S(1)}, u32[]{:S(2)}, u32[]{:S(2)}) collective-permute-start(bf16[192,512]{1,0:T(8,128)(2,1)S(1)} %get-tuple-element.23), channel_id=1, source_target_pairs={{0,384},{128,0},{256,128},{384,256},{1,385},{129,1},{257,129},{385... | collective-permute-start | bytes 589832 | tf_op jit(solution)/shard_map/ppermute | solution.py:315
  74.7 4.2 %collective-permute-start.4 = (bf16[4,192,512]{2,1,0:T(8,128)(2,1)S(1)}, bf16[4,192,512]{2,1,0:T(8,128)(2,1)S(1)}, u32[]{:S(2)}, u32[]{:S(2)}) collective-permute-start(bf16[4,192,512]{2,1,0:T(8,128)(2,1)S(1)} %bitcast.20), channel_id=1, source_target_pairs={{0,64},{64,0},{1,65},{65,1},{2,66},{66,2},{3,67},{67,3},{4,68},{68... | collective-permute-start | bytes 2359304 | tf_op jit(solution)/shard_map/ppermute | solution.py:232
  78.9 35.2 %copy-start.2 = (bf16[8,16,2048]{2,1,0:T(8,128)(2,1)S(1)}, bf16[8,16,2048]{2,1,0:T(8,128)(2,1)}, u32[]{:S(2)}) copy-start(bf16[8,16,2048]{2,1,0:T(8,128)(2,1)} %param.18) | copy-start | bytes 1572868
  78.9 35.2 %copy-start.6 = (f32[2048]{0:T(1024)S(1)}, f32[2048]{0:T(1024)}, u32[]{:S(2)}) copy-start(f32[2048]{0:T(1024)} %param.17) | copy-start | bytes 24580
  79.9 34.1 %collective-permute-start.5 = (bf16[2048,512]{1,0:T(8,128)(2,1)S(1)}, bf16[2048,512]{1,0:T(8,128)(2,1)S(1)}, u32[]{:S(2)}, u32[]{:S(2)}) collective-permute-start(bf16[2048,512]{1,0:T(8,128)(2,1)S(1)} %bitcast.16), channel_id=1, source_target_pairs={{0,64},{64,0},{1,65},{65,1},{2,66},{66,2},{3,67},{67,3},{4,68},{68... | collective-permute-start | bytes 6291464 | tf_op jit(solution)/shard_map/ppermute | solution.py:232
